TPU v7x, 32 devices: a whole 2x2x4 slice. The times are simulated.
32 devices in a mesh: stack: 2 (over y), gx: 4 (over z), gy: 2 (over x), gz: 2 (over core).
Axes of the slice: x: 2, y: 2, z: 4, core: 2. Of those that a mesh axis runs over, the one named last changes fastest.
Arguments:
- initial_solid_warmth: float32 [16, 256, 512], P(('stack', 'gz'), 'gy', 'gx'), parts along dimension 0, may hold values from 0 to 1
- dissipated_power: float32 [16, 256, 512], P(('stack', 'gz'), 'gy', 'gx'), parts along dimension 0, may hold values from 0.1 to 2
- thermal_storage: float32 [16, 256, 512], P(('stack', 'gz'), 'gy', 'gx'), parts along dimension 0, may hold values from 0.1 to 1
- thermal_conductance_pair: float32 [2, 16, 256, 512], P(None, ('stack', 'gz'), 'gy', 'gx'), parts along dimension 1, may hold values from 0.3 to 3
- fluid_warmth: float32 [8, 128, 128], P(('stack', 'gy', 'gz'), 'gx'), parts along dimension 0, may hold values from 0 to 1
- exchange_coefficient: float32 [8, 128, 128], P(('stack', 'gy', 'gz'), 'gx'), parts along dimension 0, may hold values from 0.5 to 4
- channel_block_holder: int32 [4, 128, 1], replicated, may hold values from 0 to 3; in each aligned block of 32 rows (0 to 31, 32 to 63, ..., all dimensions but the last counted through in order) at most 16 rows name the same one
- channel_stratum_slot: int32 [4, 128], replicated, may hold values from 0 to 3
- channel_transverse_slot: int32 [4, 128], replicated, may hold values from 0 to 127
Outputs:
- temperature_out: float32 [16, 256, 512], P(('stack', 'gz'), 'gy', 'gx'), parts along dimension 0
- coolant_out: float32 [8, 128, 128], P(('stack', 'gy', 'gz'), 'gx'), parts along dimension 0
There are 2 independent parts, one for each index of `stack`. A program takes and returns all parts, laid end to end along the dimension named above; an argument that names none is the same for every part. Nothing has to cross between parts.
Inputs may be any that keep to these rules, and one draw needn't show every extreme that they name: `channel_block_holder`: within the 32 segments of one device (aligned blocks of 32 entries along the second dimension) no tile is named more than 16 times; some tile is named exactly 16 times.
All inputs are finite; a program needn't handle non-finite values.
Results may differ from a plain program's by a relative error of at most 0.00012.
Values sent between devices are 32-bit elements; how exact they have to be, the bound alone decides.
No kernel may reach another device: no remote copies, remote signals or barrier semaphores. Data moves between devices by JAX's collectives and lax.ppermute only.
A program may use at most 64 MiB of HBM per device.

v0:
```python
import functools

import jax
import jax.numpy as jnp
from jax import lax
from jax.experimental import pallas as pl
from jax.experimental.pallas import tpu as pltpu
from jax.sharding import PartitionSpec as P

STEPS = 2
ITERS = 4
HALO = STEPS * ITERS
GROUP = 2 * HALO
LANES = 128
RAW = 5
FIELDS = 7
coolant_gain = 0.5

VMEM = pl.BlockSpec(memory_space=pltpu.VMEM)
PARAMS = pltpu.CompilerParams(vmem_limit_bytes=40 * 1024 * 1024)


def cost(microseconds):
    return pl.CostEstimate(flops=0, bytes_accessed=int(microseconds * 3e6), transcendentals=0)


def lane_of(rows):
    return lax.broadcasted_iota(jnp.int32, (rows, LANES), 1)


def take(value, index):
    return jnp.take_along_axis(value, index, axis=1, mode="promise_in_bounds")


def edge_columns(rows, turned):
    j = lane_of(rows) % GROUP
    first = j < HALO
    return jnp.where(first, LANES - HALO + j, j - HALO) if not turned else jnp.where(first, j, LANES - GROUP + j)


def split(value):
    high = value.astype(jnp.bfloat16)
    low = (value - high.astype(jnp.float32)).astype(jnp.bfloat16)
    return high, low


def exact_dot(onehot, value):
    high, low = split(value)
    both = jnp.concatenate([high, low], axis=0)
    return jnp.dot(jnp.concatenate([onehot, onehot], axis=1), both, preferred_element_type=jnp.float32)


def coupling(coef, warmth):
    flow = coef * warmth
    second = coolant_gain * coef * coef
    return jnp.concatenate([coef, flow, second, flow - second * warmth], axis=1)


def flip(z, layers, i):
    return jnp.where(z == 0, i, layers - 1 - i)


def pack_kernel(shape, u_ref, p_ref, c_ref, k_ref, f_ref, x_ref, *refs):
    own_ref, left_ref, right_ref, seg_ref = refs[3:7]
    sems = refs[-1]
    layers, rows = shape
    seg = f_ref.shape[0]
    z = lax.axis_index("gz")
    plane = layers * rows
    copies = []

    def fetch(src, dst):
        copies.append(pltpu.make_async_copy(src, dst, sems.at[len(copies)]))
        copies[-1].start()

    fetch(k_ref, own_ref.at[pl.ds(0, 2 * plane), :])
    for field, ref in enumerate((u_ref, p_ref, c_ref), 2):
        fetch(ref, own_ref.at[pl.ds(field * plane, plane), :])
    for j, ref in enumerate((x_ref, f_ref)):
        fetch(ref, own_ref.at[pl.ds(RAW * plane + j * seg, seg), :])
    for table, place in zip(refs[:3], refs[7:10]):
        fetch(table, place)
    chunk = rows // 4
    lane = lane_of(chunk)
    first = lane % GROUP < HALO
    columns = edge_columns(chunk, False), edge_columns(chunk, True)
    edges = RAW * plane + 2 * seg

    def gather(field, at, g):
        value = None
        for i in range(layers):
            start = pl.multiple_of((field * layers + flip(z, layers, i)) * rows + at, chunk)
            taken = take(own_ref[pl.ds(start, chunk), :], columns[g % 2])
            value = taken if value is None else jnp.where(lane // GROUP == (g // 2) * layers + i, taken, value)
        return value

    def place(g, part):
        return pl.ds(edges + ((g % 2) * RAW + part) * chunk, chunk)

    copies[0].wait()
    roots = pl.ds(0, 2 * plane)
    own_ref[roots, :] = jnp.sqrt(own_ref[roots, :])
    for field in range(4):
        if field >= 2:
            copies[field - 1].wait()
        for part in range(4):
            value = gather(field, part * chunk, field)
            if field >= 2:
                value = jnp.where(lane < LANES // 2, own_ref[place(field, part), :], value)
            own_ref[place(field, part), :] = value
    copies[3].wait()
    for g in range(4):
        value = gather(4, g * chunk, g)
        if g >= 2:
            value = jnp.where(lane < LANES // 2, own_ref[place(g, 4), :], value)
        own_ref[place(g, 4), :] = value
    for part in range(RAW):
        even, odd = own_ref[place(0, part), :], own_ref[place(1, part), :]
        left_ref[part * chunk : (part + 1) * chunk, :] = jnp.where(first, odd, even)
        right_ref[part * chunk : (part + 1) * chunk, :] = jnp.where(first, even, odd)
    for copy in copies[4:]:
        copy.wait()
    segments = own_ref[RAW * plane : RAW * plane + 2 * seg, :]
    seg_ref[...] = segments
    left_ref[RAW * chunk :, :] = segments
    right_ref[RAW * chunk :, :] = segments


class Strips:
    def __init__(self, refs, starts, cells_ref, start, rows, layers):
        self.refs, self.starts = refs, starts
        self.cells_ref, self.start = cells_ref, start
        self.rows, self.layers = rows, layers

    def both(self, field, start, n, x, gx, partner):
        chunk = self.rows // 4
        if field < 4:
            g, at = field, start
        else:
            g, at = start // chunk, 4 * chunk + start % chunk
        a, b = (ref[at + begin : at + begin + n, :] for ref, begin in zip(self.refs, self.starts))
        at = self.start + (g % 2) * RAW * chunk + at
        inside = self.cells_ref[at : at + n, :]
        from_left, from_right = jnp.where(x > 0, b, 0.0), jnp.where(x < gx - 1, a, 0.0)
        lane = lane_of(n)
        first = (lane % GROUP < HALO) if g % 2 == 0 else (lane % GROUP >= HALO)
        half = self.layers * GROUP
        src = lane % half
        if partner:
            src = (self.layers - 1 - src // GROUP) * GROUP + src % GROUP
        if g % 2 == 1:
            src = jnp.where(src % GROUP < HALO, src + HALO, src - HALO)
        src = src + half * (g // 2)
        return take(jnp.where(first, from_left, inside), src), take(jnp.where(first, inside, from_right), src)


def place_segments(x, gx, seg, coef_ref, warmth_ref, sources):
    for k, ref, at in sources:
        place = pl.ds(pl.multiple_of(lax.rem(x + k, gx) * seg, seg), seg)
        coef_ref[place, :] = ref[at : at + seg, :]
        warmth_ref[place, :] = ref[at + seg : at + 2 * seg, :]


def tables(z, group, layers, holder_ref, stratum_ref, transverse_ref):
    holder = holder_ref[pl.ds(group, 1), :]
    layer = stratum_ref[pl.ds(group, 1), :]
    layer = jnp.where(z == 0, layer, layers - 1 - layer)
    row = transverse_ref[pl.ds(group, 1), :]
    n = holder.shape[1]
    which = lax.broadcasted_iota(jnp.int32, (8, n), 0)
    stacked = jnp.where(which == 0, holder, jnp.where(which == 1, layer, row))
    eye = lax.broadcasted_iota(jnp.int32, (n, n), 0) == lax.broadcasted_iota(jnp.int32, (n, n), 1)
    columns = lax.dot_general(
        eye.astype(jnp.float32).astype(jnp.bfloat16),
        stacked.astype(jnp.float32).astype(jnp.bfloat16),
        (((1,), (1,)), ((), ())),
        preferred_element_type=jnp.float32,
    )
    return (holder, layer, row), columns


def as_onehot(mask):
    return jnp.where(mask, 1.0, 0.0).astype(jnp.bfloat16)


def combine(raw, added):
    s, t, u, power, storage = raw
    wall, flow, second, later = (added[:, i * LANES : (i + 1) * LANES] for i in range(4))
    return s, t, s * u, storage + wall, power + storage * u + flow, power + later, storage + second


def lengths_of(gx, chunk, seg):
    return [RAW * chunk + 2 * seg] * 2 + [2 * seg] * (gx - 3)


def edge_at(top, rows):
    return 0 if top is True else rows - HALO if top is False else pl.multiple_of(jnp.where(top, 0, rows - HALO), HALO)


def inner_at(top, rows):
    return HALO if top is True else rows - 2 * HALO if top is False else pl.multiple_of(jnp.where(top, HALO, rows - 2 * HALO), HALO)


def sides_of(gy, y):
    return [(y == 1, True)] if gy == 2 else [(True, y > 0), (False, y < gy - 1)]


def maps_kernel(gx, gy, shape, holder_ref, stratum_ref, transverse_ref, *refs):
    layers, rows = shape
    plane = layers * rows
    picks_ref, beside_ref, mine_ref = refs[6:]
    x, y, z = (lax.axis_index(a) for a in ("gx", "gy", "gz"))
    n = holder_ref.shape[1]
    for partner in range(2):
        cells_ref, rows_ref, masks_ref = refs[3 * partner : 3 * partner + 3]
        group = y * 2 + ((1 - z) if partner else z)
        (holder, layer, row), columns = tables(z, group, layers, holder_ref, stratum_ref, transverse_ref)
        cell = jnp.where(holder == x, layer * rows + row, -1)
        cells_ref[...] = as_onehot(lax.broadcasted_iota(jnp.int32, (plane, n), 0) == cell)
        rows_ref[...] = as_onehot(lax.broadcasted_iota(jnp.int32, (rows, n), 0) == row)
        holder, layer, row = (columns[:, j : j + 1].astype(jnp.int32) for j in range(3))
        lane = lane_of(n)
        first = lane % GROUP < HALO
        here = lane // GROUP == layer + partner * layers
        for side, begin in enumerate((x - 1, x)):
            mine = jnp.logical_and(here, holder == jnp.where(first, begin, begin + 1))
            masks_ref[side * n : (side + 1) * n, :] = jnp.where(mine, 1.0, 0.0)
        if partner:
            continue
        mine = holder == x
        mine_ref[...] = jnp.where(jnp.logical_and(mine, lane >= 0), 1.0, 0.0)
        spoilt = None
        for side, (above, live) in enumerate(sides_of(gy, y)):
            start = edge_at(above, rows)
            part = jnp.logical_and(row // HALO == start // HALO, live)
            spoilt = part if spoilt is None else jnp.logical_or(spoilt, part)
            cell = jnp.where(jnp.logical_and(mine, part), layer * HALO + row - start, -1)
            beside_ref[side * n : (side + 1) * n, :] = as_onehot(lane == cell)
        cell = jnp.where(jnp.logical_and(mine, jnp.logical_not(spoilt)), layer * rows + row, -1)
        picks_ref[...] = as_onehot(lax.broadcasted_iota(jnp.int32, (n, plane), 1) == cell)


def join_kernel(mine_ref, *refs):
    out_ref, at = refs[-1], 0
    for ref in refs[:-1]:
        n = ref.shape[0]
        out_ref[at : at + n, :] = ref[...]
        at += n


def partner_rows(layers):
    whole, at = [], 1
    for i in range(layers - 1, -1, -1):
        whole.append((i, HALO - layers + i, at))
        at += HALO - layers + i
    stride = -(-at // 8) * 8
    later, at = [], 0
    for f in range(2):
        for i in range(layers - 1, -1, -1):
            if ITERS - 1 - layers + i > 0:
                later.append((f, i, ITERS - 1 - layers + i, at))
                at += ITERS - 1 - layers + i
    return whole, stride, later, -(-at // 8) * 8


def fill_kernel(partner, gx, gy, shape, seg, *refs):
    layers, rows = shape
    cells_ref, where_ref, rows_ref, masks_ref = refs[:4]
    plane, chunk = layers * rows, rows // 4
    lengths = lengths_of(gx, chunk, seg)
    if partner:
        sources = [(refs[4], sum(lengths[:k])) for k in range(gx - 1)]
        refs = refs[5:]
    else:
        sources = [(ref, 0) for ref in refs[4 : 4 + gx - 1]]
        refs = refs[4 + gx - 1 :]
    sides = 1 if gy == 2 else 2
    out_ref = refs[0]
    if partner:
        coef_ref, warmth_ref = refs[1:3]
    else:
        strip_refs, partner_refs, segments_ref = refs[1 : 1 + sides], refs[1 + sides : 1 + 2 * sides], refs[1 + 2 * sides]
        n = segments_ref.shape[0] // 2
        coef_ref, warmth_ref = segments_ref.at[pl.ds(0, n), :], segments_ref.at[pl.ds(n, n), :]
    x, y, z = (lax.axis_index(a) for a in ("gx", "gy", "gz"))
    base = layers if partner else 0
    distances = [1, gx - 1] + list(range(2, gx - 1))
    held = [(k, ref, at + (RAW * chunk if j < 2 else 0)) for j, (k, (ref, at)) in enumerate(zip(distances, sources))]
    place_segments(x, gx, seg, coef_ref, warmth_ref, [(0, cells_ref, RAW * plane)] + held)
    coef, warmth = coef_ref[...], warmth_ref[...]
    n = coef.shape[0]
    added = exact_dot(where_ref[...], coupling(coef, warmth))
    near = edge_columns(n, False)
    beside = []
    for side in range(2):
        masked = take(coef, near) * masks_ref[side * n : (side + 1) * n, :]
        beside.append(exact_dot(rows_ref[...], coupling(masked, take(warmth, near))))
    planes = layers + 2
    for i in range(layers):
        src = flip(z, layers, i)
        raw = [cells_ref[pl.ds(pl.multiple_of((f * layers + src) * rows, rows), rows), :] for f in range(RAW)]
        for f, value in enumerate(combine(raw, added[i * rows : (i + 1) * rows])):
            out_ref[f * planes + i] = value
    strips = Strips(
        [ref for ref, _ in sources[:2]], [at for _, at in sources[:2]], cells_ref, RAW * plane + 2 * seg, rows, layers
    )
    half = lane_of(chunk) // (LANES // 2) == (1 if partner else 0)
    for part in range(4):
        here = slice(part * chunk, (part + 1) * chunk)
        raw = [strips.both(f, part * chunk, chunk, x, gx, partner) for f in range(RAW)]
        for side in range(2):
            cells = [jnp.where(half, value[side], 0.0) for value in raw]
            for f, value in enumerate(combine(cells, beside[side][here])):
                out_ref[f * planes + layers + side, here, :] = value
    if partner:
        return
    low = lane_of(HALO) < LANES // 2
    upper = lax.broadcasted_iota(jnp.int32, (HALO, LANES), 0) < HALO // 2
    first = lane_of(HALO) % GROUP < HALO
    sent = FIELDS - 1
    for strip_ref, partner_ref, (top, _) in zip(strip_refs, partner_refs, sides_of(gy, y)):
        edge = pl.ds(edge_at(top, rows), HALO)

        def shrink(values):
            *whole, e, g = values
            e = jnp.where(top, e, pltpu.roll(e, HALO // 2, 0))
            g = jnp.where(top, pltpu.roll(g, HALO // 2, 0), g)
            return whole + [jnp.where(upper, e, g)]

        def give(ref, at, values):
            for f, value in enumerate(values):
                ref[at + f * HALO : at + (f + 1) * HALO, :] = value

        for i in range(layers):
            give(strip_ref, i * sent * HALO, shrink([out_ref[f * planes + i, edge, :] for f in range(FIELDS)]))
        outer = []
        for f in range(FIELDS):
            left, right = (out_ref[f * planes + layers + side, edge, :] for side in range(2))
            outer.append(jnp.where(first, left, right))
        outer = shrink(outer)
        values = [jnp.where(low, outer[j], pltpu.roll(outer[j + 1], LANES // 2, 1)) for j in range(0, sent, 2)]
        give(strip_ref, layers * sent * HALO, values)
        whole, stride, later, shared = partner_rows(layers)
        pieces = [(f, i, m, f * stride + at) for f in range(sent - 1) for i, m, at in whole]
        pieces += [(sent - 1 + f, i, m, (sent - 1) * stride + at) for f, i, m, at in later]
        for f, i, m, at in pieces:
            start = edge_at(top, rows) + jnp.where(top, 0, HALO - m)
            partner_ref[at : at + m, :] = out_ref[f * planes + i, pl.ds(start, m), :]
        give(partner_ref, (sent - 1) * stride + shared, values)


def planes_of(count, total):
    return list(range(count)) + [total - 2, total - 1]


def lateral(buf, at, n, which):
    sums = []
    for i in which:
        centre = buf[i, pl.ds(at, n), :]
        beside = pltpu.roll(centre, 1, 1) + pltpu.roll(centre, LANES - 1, 1)
        sums.append(beside + (buf[i, pl.ds(at - 1, n), :] + buf[i, pl.ds(at + 1, n), :]))
    return sums


def vertical(planes, edges, count):
    sums = []
    for i in range(count):
        near = [planes[j] for j in (i - 1, i + 1) if 0 <= j < len(planes)]
        sums.append(functools.reduce(jnp.add, near))
    for edge in edges:
        lane = lane_of(edge.shape[0])
        up = jnp.where(lane >= GROUP, pltpu.roll(edge, GROUP, 1), 0.0)
        down = jnp.where(lane < LANES - GROUP, pltpu.roll(edge, LANES - GROUP, 1), 0.0)
        sums.append(up + down)
    return sums


def coefficients(s_ref, at, n, raw, dests, to, outside):
    a_ref, q_ref, r_ref, e_ref, g_ref, root_ref = dests
    total = s_ref.shape[0]
    sums = lateral(s_ref, at, n, range(total))
    t = [raw(1, i) for i in range(total)]
    above = vertical(t[:-2], t[-2:], total - 2)
    here = pl.ds(to, n)
    for i in range(total):
        s = s_ref[i, pl.ds(at, n), :]
        diag = raw(3, i) + s * sums[i] + t[i] * above[i]
        if outside or i >= total - 2:
            inverse = 1.0 / jnp.where(diag > 0.0, diag, 1.0)
            root = jnp.where(s > 0.0, 1.0 / jnp.where(s > 0.0, s, 1.0), 0.0)
        else:
            inverse, root = 1.0 / diag, 1.0 / s
        if i < root_ref.shape[0]:
            root_ref[i, here, :] = root
        scaled = s * inverse
        a_ref[i, here, :] = s * scaled
        r_ref[i, here, :] = raw(4, i) * scaled
        e_ref[i, here, :] = raw(5, i) * scaled
        g_ref[i, here, :] = raw(6, i) * inverse
        q_ref[i, here, :] = t[i] * root


def sweep(src_ref, dst_ref, at, n, count, coefs, base):
    a_ref, q_ref, r_ref = coefs[:3]
    total = src_ref.shape[0]
    here, there = pl.ds(base, n), pl.ds(at, n)
    which = planes_of(count, total)
    sums = lateral(src_ref, at, n, which)
    scaled = [q_ref[i, here, :] * src_ref[i, there, :] for i in planes_of(min(count + 1, total - 2), total)]
    above = vertical(scaled[:-2], scaled[-2:], count)
    for j, i in enumerate(which):
        dst_ref[i, there, :] = r_ref[i, here, :] + a_ref[i, here, :] * (sums[j] + q_ref[i, here, :] * above[j])


def next_rhs(coefs, v_ref, at, n, base):
    r_ref, e_ref, g_ref = coefs[2:5]
    here = pl.ds(base, n)
    for i in range(v_ref.shape[0]):
        r_ref[i, here, :] = e_ref[i, here, :] + g_ref[i, here, :] * v_ref[i, pl.ds(at, n), :]


def meet(v_ref, at, n, count, back):
    total = v_ref.shape[0]
    here = pl.ds(at, n)
    lane = lane_of(n)
    j, group = lane % GROUP, lane // GROUP
    outer = jnp.logical_or(lane < ITERS, lane >= LANES - ITERS)
    left, right = v_ref[total - 2, here, :], v_ref[total - 1, here, :]
    middle = jnp.where(j < HALO, right, left)
    for i in range(count):
        value = v_ref[i, here, :]
        if back:
            moved = pltpu.roll(value, (i * GROUP + HALO) % LANES, 1)
            left = jnp.where(jnp.logical_and(group == i, j >= GROUP - ITERS), moved, left)
            right = jnp.where(jnp.logical_and(group == i, j < ITERS), moved, right)
        v_ref[i, here, :] = jnp.where(outer, pltpu.roll(middle, LANES - (i * GROUP + HALO), 1), value)
    if back:
        v_ref[total - 2, here, :] = left
        v_ref[total - 1, here, :] = right


def needed(layers, n):
    return min(2 * layers, layers + STEPS * ITERS - 1 - n)


def two_steps(layers, sweep_all, between, after):
    for step in range(STEPS):
        whole = [n for n in range(step * ITERS, (step + 1) * ITERS) if needed(layers, n) == 2 * layers]
        pairs = len(whole) // 2

        def pair(k, carry):
            n = step * ITERS + 2 * k
            sweep_all(n, 0, 2 * layers)
            sweep_all(n + 1, 1, 2 * layers)
            return carry

        if pairs:
            lax.fori_loop(0, pairs, pair, 0)
        for n in range(step * ITERS + 2 * pairs, (step + 1) * ITERS):
            sweep_all(n, n % 2, needed(layers, n))
        after(step)
        if step < STEPS - 1:
            between()


PAD = 8


def tile_kernel(gx, gy, shape, *refs):
    layers, rows = shape
    own_ref, partner_ref, picks_ref, out_ref, below_ref, level_ref = refs[:6]
    s_ref, va_ref, vb_ref = refs[6:9]
    coefs = refs[9:]
    x, y, z = (lax.axis_index(a) for a in ("gx", "gy", "gz"))
    total = 2 * layers + 2
    zeros = jnp.zeros((PAD, LANES), jnp.float32)
    for ref in (s_ref, va_ref, vb_ref):
        for i in range(total):
            ref[i, 0:PAD, :] = zeros
            ref[i, PAD + rows : PAD + rows + PAD, :] = zeros

    def field(f, i, here):
        j = f * (layers + 2)
        if i >= 2 * layers:
            j = j + i - layers
            return own_ref[j, here, :] + partner_ref[j, here, :]
        return own_ref[j + i, here, :] if i < layers else partner_ref[j + i - layers, here, :]

    for i in range(total):
        s_ref[i, PAD : PAD + rows, :] = field(0, i, slice(None))
        va_ref[i, PAD : PAD + rows, :] = field(2, i, slice(None))
    n = 8
    for at in range(0, rows, n):
        coefficients(s_ref, PAD + at, n, lambda f, i: field(f, i, slice(at, at + n)), coefs, at, False)

    bufs = (va_ref, vb_ref)
    sides = sides_of(gy, y)

    def sweep_all(number, which, count):
        src_ref, dst_ref = bufs[which], bufs[1 - which]
        for side, (above, _) in enumerate(sides):
            inner = pl.ds(PAD + inner_at(above, rows), HALO)
            for i in range(total):
                level_ref[(side * STEPS * ITERS + number) * total + i] = src_ref[i, inner, :]
        for at in range(0, rows, n):
            sweep(src_ref, dst_ref, PAD + at, n, count, coefs, at)

    def after(step):
        last = step == STEPS - 1
        for at in range(0, rows, n):
            meet(va_ref, PAD + at, n, layers if last else 2 * layers, not last)
        heat = []
        for i in range(layers):
            here = pl.ds(PAD, rows)
            heat.append(va_ref[i, here, :] * coefs[5][i])
            if step == STEPS - 1:
                out_ref[flip(z, layers, i)] = heat[-1]
        below_ref[step] = exact_dot(picks_ref[...], jnp.concatenate(heat, axis=0))

    def between():
        for at in range(0, rows, n):
            next_rhs(coefs, va_ref, PAD + at, n, at)

    two_steps(layers, sweep_all, between, after)


def edge_kernel(gx, gy, shape, seg, *refs):
    layers, rows = shape
    own_ref, partner_ref, picks_ref, mine_ref, segments_ref, below_ref, level_ref = refs[:7]
    sides_n = 1 if gy == 2 else 2
    along, across = refs[7 : 7 + sides_n], refs[7 + sides_n : 7 + 2 * sides_n]
    refs = refs[7 + 2 * sides_n :]
    heat_ref, returns = refs[0], refs[1 : 1 + gx]
    ret_ref, s_ref, va_ref, vb_ref = refs[1 + gx : 5 + gx]
    coefs = refs[5 + gx :]
    x, y, z = (lax.axis_index(a) for a in ("gx", "gy", "gz"))
    total = 2 * layers + 2
    count = mine_ref.shape[0]
    below = [below_ref[step] for step in range(STEPS)]
    lane = lane_of(HALO)
    low, first = lane < LANES // 2, lane % GROUP < HALO
    columns = edge_columns(HALO, False)
    bufs = (va_ref, vb_ref)

    def tile(j):
        return pl.ds(j if isinstance(j, int) else pl.multiple_of(j, HALO), HALO)

    for side, (above, live) in enumerate(sides_of(gy, y)):
        def place(when_top, otherwise):
            if above is True or above is False:
                return when_top * HALO if above else otherwise * HALO
            return jnp.where(above, when_top * HALO, otherwise * HALO)

        outer, strip, edge, inner = place(0, 3), place(1, 2), place(2, 1), place(3, 0)
        edge_rows = tile(edge_at(above, rows))
        inner_rows = tile(inner_at(above, rows))

        def field(f, i, here):
            j = f * (layers + 2)
            if i >= 2 * layers:
                j = j + i - layers
                return own_ref[j, here, :] + partner_ref[j, here, :]
            return own_ref[j + i, here, :] if i < layers else partner_ref[j + i - layers, here, :]

        t_ref, d_ref, q_ref, e_ref, g_ref = coefs[1], coefs[0], coefs[2], coefs[3], coefs[4]
        keep = {0: s_ref, 1: t_ref, 2: va_ref, 3: d_ref, 4: q_ref, 5: e_ref, 6: g_ref}
        zeros = jnp.zeros((HALO, LANES), jnp.float32)
        src = lane % (LANES // 2)
        turned = (layers - 1 - src // GROUP) * GROUP + src % GROUP
        half_tile = lax.broadcasted_iota(jnp.int32, (HALO, LANES), 0) < HALO // 2

        def unpack(value, f):
            if f < FIELDS - 2:
                return value
            turned_value = pltpu.roll(value, HALO // 2, 0)
            if f == FIELDS - 2:
                at_top, at_bottom = jnp.where(half_tile, 0.0, turned_value), jnp.where(half_tile, value, 0.0)
            else:
                at_top, at_bottom = jnp.where(half_tile, 0.0, value), jnp.where(half_tile, turned_value, 0.0)
            return jnp.where(above, at_top, at_bottom)

        whole, stride, later, shared = partner_rows(layers)
        sublane = lax.broadcasted_iota(jnp.int32, (HALO, LANES), 0)

        def nearest(ref, m, at):
            at_top = jnp.where(sublane >= HALO - m, ref[at - HALO + m : at + m, :], 0.0)
            return jnp.where(above, at_top, jnp.where(sublane < m, ref[at : at + HALO, :], 0.0))

        for f in range(FIELDS):
            g = min(f, FIELDS - 2)
            if f < FIELDS - 2:
                rows_of = {i: (m, f * stride + at) for i, m, at in whole}
            else:
                rows_of = {i: (m, (FIELDS - 2) * stride + at) for which, i, m, at in later if which == f - FIELDS + 2}
            values, inside = [], zeros
            for i in range(2 * layers):
                if i < layers:
                    at = (i * (FIELDS - 1) + g) * HALO
                    value = unpack(along[side][at : at + HALO, :], f)
                else:
                    j = 2 * layers - 1 - i
                    value = nearest(across[side], *rows_of[j]) if j in rows_of else zeros
                values.append(value)
                inside = jnp.where(lane // GROUP == i, take(value, columns), inside)
            half = (LANES // 2) * (g % 2)
            at = (layers * (FIELDS - 1) + g // 2) * HALO
            a = take(along[side][at : at + HALO, :], src + half)
            at = (FIELDS - 2) * stride + shared + (g // 2) * HALO
            b = take(across[side][at : at + HALO, :], turned + half)
            outside = unpack(jnp.where(low, a, b), f)
            values += [jnp.where(first, outside, inside), jnp.where(first, inside, outside)]
            for i, value in enumerate(values):
                ref, shift = keep[f], 0 if f in (0, 2) else HALO
                ref[i, tile(strip - shift), :] = value
                ref[i, tile(edge - shift), :] = field(f, i, edge_rows)
        for i in range(total):
            s_ref[i, tile(outer), :] = zeros
            va_ref[i, tile(outer), :] = zeros
            vb_ref[i, tile(outer), :] = zeros
            s_ref[i, tile(inner), :] = field(0, i, inner_rows)
        n = 2 * HALO
        held = [[keep[f][i, pl.ds(0, n), :] for i in range(total)] if f in (1, 3, 4, 5, 6) else None for f in range(FIELDS)]
        coefficients(s_ref, HALO, n, lambda f, i: held[f][i], coefs, 0, True)

        def sweep_all(number, which, needed_layers):
            src_ref, dst_ref = bufs[which], bufs[1 - which]
            for i in range(total):
                src_ref[i, tile(inner), :] = level_ref[(side * STEPS * ITERS + number) * total + i]
            sweep(src_ref, dst_ref, HALO, n, needed_layers, coefs, 0)

        picks = picks_ref[side * count : (side + 1) * count, :]

        def after(step):
            last = step == STEPS - 1
            meet(va_ref, HALO, n, layers if last else 2 * layers, not last)
            heat = []
            for i in range(layers):
                heat.append(va_ref[i, tile(edge), :] * coefs[5][i, tile(edge - HALO), :])
                if step == STEPS - 1:
                    heat_ref[side * layers + flip(z, layers, i)] = heat[-1]
            heat.append(jnp.zeros((LANES - layers * HALO, LANES), jnp.float32))
            below[step] = below[step] + exact_dot(picks, jnp.concatenate(heat, axis=0))

        two_steps(layers, sweep_all, lambda: next_rhs(coefs, va_ref, HALO, n, 0), after)

    coef, warmth = segments_ref[:count, :], segments_ref[count:, :]
    for step in range(STEPS):
        warmth = warmth + coolant_gain * coef * (below[step] - warmth)
    ret_ref[...] = jnp.where(mine_ref[...] > 0.0, warmth, 0.0)
    for k, ref in enumerate(returns):
        ref[...] = ret_ref[pl.ds(pl.multiple_of(lax.rem(x + k, gx) * seg, seg), seg), :]


def merge_kernel(gy, whole_ref, heat_ref, out_ref):
    layers, rows, _ = whole_ref.shape
    out_ref[...] = whole_ref[...]
    for side, (above, live) in enumerate(sides_of(gy, lax.axis_index("gy"))):
        def put(side=side, above=above):
            out_ref[:, pl.ds(edge_at(above, rows), HALO), :] = heat_ref[side * layers : (side + 1) * layers]

        if live is True:
            put()
        else:
            pl.when(live)(put)


def local(gx, gy, gz, u, power, storage, conductance, warmth, coef, holder, stratum, transverse):
    layers, rows, columns = u.shape
    seg = warmth.shape[1]
    segments = stratum.shape[1]
    if gz != 2 or gx < 3 or columns != LANES or 2 * layers * GROUP != LANES or rows % 32:
        raise ValueError("unsupported shape")
    holder = holder[:, :, 0]
    shape = (layers, rows)
    f32 = jnp.float32
    chunk = rows // 4
    wide = RAW * chunk + 2 * seg

    def struct(*dims):
        return jax.ShapeDtypeStruct(dims, f32)

    def vmem(*dims):
        return pltpu.VMEM(dims, f32)

    indices = (holder, stratum, transverse)
    flat = [a.reshape(-1, LANES) for a in (u, power, storage, conductance, warmth, coef)]
    own, to_left, to_right, only, *indices = pl.pallas_call(
        functools.partial(pack_kernel, shape),
        out_shape=(
            struct(RAW * layers * rows + 2 * seg + 2 * RAW * chunk, LANES),
            struct(wide, LANES),
            struct(wide, LANES),
            struct(2 * seg, LANES),
            *(jax.ShapeDtypeStruct(a.shape, a.dtype) for a in indices),
        ),
        in_specs=[pl.BlockSpec(memory_space=pltpu.HBM)] * 9,
        out_specs=(VMEM,) * 7,
        scratch_shapes=[pltpu.SemaphoreType.DMA((9,))],
        compiler_params=PARAMS,
        name="pack",
    )(*(pltpu.with_memory_space_constraint(a, pltpu.HBM) for a in (*flat, *indices)))

    swap = [(0, 1), (1, 0)]
    partner = lax.ppermute(own, "gz", swap)
    def from_distance(value, k):
        return lax.ppermute(value, "gx", [(i, (i - k) % gx) for i in range(gx)])

    received = [from_distance(to_left, 1), from_distance(to_right, gx - 1)]
    received += [from_distance(only, k) for k in range(2, gx - 1)]

    sides = 1 if gy == 2 else 2
    fields = struct(FIELDS * (layers + 2), rows, LANES)
    strip_rows = (FIELDS - 1) * layers * HALO + (FIELDS - 1) // 2 * HALO
    _, stride, _, shared = partner_rows(layers)
    partner_strip = (FIELDS - 2) * stride + shared + (FIELDS - 1) // 2 * HALO
    sides = 1 if gy == 2 else 2
    bf16 = jnp.bfloat16
    one_group = (
        jax.ShapeDtypeStruct((layers * rows, segments), bf16),
        jax.ShapeDtypeStruct((rows, segments), bf16),
        struct(2 * segments, LANES),
    )
    maps = pl.pallas_call(
        functools.partial(maps_kernel, gx, gy, shape),
        out_shape=one_group
        + one_group
        + (
            jax.ShapeDtypeStruct((segments, layers * rows), bf16),
            jax.ShapeDtypeStruct((sides * segments, LANES), bf16),
            struct(segments, LANES),
        ),
        in_specs=[VMEM] * 3,
        out_specs=(VMEM,) * 9,
        compiler_params=PARAMS,
        cost_estimate=cost(1),
        name="maps",
    )(*indices)
    own_maps, partner_maps, (picks, picks_beside, mine) = maps[:3], maps[3:6], maps[6:]
    joined = pl.pallas_call(
        join_kernel,
        out_shape=struct(sum(a.shape[0] for a in received), LANES),
        in_specs=[pl.BlockSpec(memory_space=pl.ANY)] + [VMEM] * (gx - 1),
        out_specs=VMEM,
        compiler_params=PARAMS,
        name="join",
    )(mine, *received)
    late = lax.ppermute(joined, "gz", swap)
    filled = pl.pallas_call(
        functools.partial(fill_kernel, False, gx, gy, shape, seg),
        out_shape=(fields,) + (struct(strip_rows, LANES),) * sides
        + (struct(partner_strip, LANES),) * sides
        + (struct(2 * segments, LANES),),
        in_specs=[VMEM] * (4 + gx - 1),
        out_specs=(VMEM,) * (2 + 2 * sides),
        compiler_params=PARAMS,
        cost_estimate=cost(1.5),
        name="fill_own",
    )(own, *own_maps, *received)
    own_fields, held = filled[0], filled[-1]
    strips, partner_strips = filled[1 : 1 + sides], filled[1 + sides : 1 + 2 * sides]
    if gy == 2:
        routes = [(0, swap)]
    else:
        up = [(i, i + 1) for i in range(gy - 1)]
        routes = [(1, up), (0, [(j, i) for i, j in up])]
    along = [lax.ppermute(strips[side], "gy", pairs) for side, pairs in routes]
    across = []
    for side, pairs in routes:
        both = [(2 * i + z, 2 * j + 1 - z) for i, j in pairs for z in range(2)]
        across.append(lax.ppermute(partner_strips[side], ("gy", "gz"), both))

    partner_fields = pl.pallas_call(
        functools.partial(fill_kernel, True, gx, gy, shape, seg),
        out_shape=fields,
        in_specs=[VMEM] * 5,
        out_specs=VMEM,
        scratch_shapes=[vmem(segments, LANES)] * 2,
        compiler_params=PARAMS,
        cost_estimate=cost(1.5),
        name="fill_partner",
    )(partner, *partner_maps, late)

    total = 2 * layers + 2
    padded = vmem(total, rows + 2 * PAD, LANES)
    inside, below, levels = pl.pallas_call(
        functools.partial(tile_kernel, gx, gy, shape),
        out_shape=(
            struct(layers, rows, LANES),
            struct(STEPS, segments, LANES),
            struct(sides * STEPS * ITERS * total, HALO, LANES),
        ),
        in_specs=[VMEM] * 3,
        out_specs=(VMEM,) * 3,
        scratch_shapes=[padded] * 3 + [vmem(total, rows, LANES)] * 5 + [vmem(layers, rows, LANES)],
        compiler_params=PARAMS,
        cost_estimate=cost(7),
        name="tile_sweeps",
    )(own_fields, partner_fields, picks)

    results = pl.pallas_call(
        functools.partial(edge_kernel, gx, gy, shape, seg),
        out_shape=(struct(sides * layers, HALO, LANES),) + (struct(seg, LANES),) * gx,
        in_specs=[VMEM] * (7 + 2 * sides),
        out_specs=(VMEM,) * (1 + gx),
        scratch_shapes=[vmem(segments, LANES)]
        + [vmem(total, 4 * HALO, LANES)] * 3
        + [vmem(total, 2 * HALO, LANES)] * 5
        + [vmem(layers, 2 * HALO, LANES)],
        compiler_params=PARAMS,
        cost_estimate=cost(1.5),
        name="edge_sweeps",
    )(own_fields, partner_fields, picks_beside, mine, held, below, levels, *along, *across)
    heat, coolant = results[0], results[1]
    returned = [lax.ppermute(results[1 + k], "gx", [(i, (i + k) % gx) for i in range(gx)]) for k in range(1, gx)]
    temperature = pl.pallas_call(
        functools.partial(merge_kernel, gy),
        out_shape=struct(layers, rows, LANES),
        in_specs=[VMEM] * 2,
        out_specs=VMEM,
        compiler_params=PARAMS,
        cost_estimate=cost(1),
        name="merge",
    )(inside, heat)
    for value in returned:
        coolant = coolant + value
    return temperature, coolant[None]


def solution(mesh):
    gx, gy, gz = (mesh.shape[a] for a in ("gx", "gy", "gz"))
    cells = P(("stack", "gz"), "gy", "gx")
    segments = P(("stack", "gy", "gz"), "gx", None)
    return jax.shard_map(
        functools.partial(local, gx, gy, gz),
        mesh=mesh,
        in_specs=(cells, cells, cells, P(None, ("stack", "gz"), "gy", "gx"), segments, segments, P(), P(), P()),
        out_specs=(cells, segments),
        check_vma=False,
    )
```

profile of v0, /device:TPU:0, one launch (start us, length us, event | category | flops | bytes accessed | tf_op | source)
XLA Modules:
  0.0 31.5 jit_solution(12077684902035342097)
XLA Ops:
  0.6 1.9 %pack.1 = (f32[2944,128]{1,0:T(8,128)S(1)}, f32[224,128]{1,0:T(8,128)S(1)}, f32[224,128]{1,0:T(8,128)S(1)}, f32[64,128]{1,0:T(8,128)S(1)}, s32[4,128]{1,0:T(4,12...) custom-call(f32[512,128]{1,0:T(8,128)} %bitcast.10, f32[512,128]{1,0:T(8,128)} %bitcast.11, f32[512,128]{1,0:T(8,128)} %bitcast.12, ...), custom_call_target="tpu_custom_call" | custom-call | tf_op jit(solution)/shard_map/pack/pallas_call | solution.py:687
  2.6 0.5 %collective-permute-start.3 = (f32[2944,128]{1,0:T(8,128)S(1)}, f32[2944,128]{1,0:T(8,128)S(1)}, u32[]{:S(2)}, u32[]{:S(2)}) collective-permute-start(f32[2944,128]{1,0:T(8,128)S(1)} %get-tuple-element.30.refs_0_), channel_id=1, source_target_pairs={{0,1},{1,0},{2,3},{3,2},{4,5},{5,4},{6,7},{7,6},{8,9},{9,8},{10,11... | collective-permute-start | bytes 4521992 | tf_op jit(solution)/shard_map/ppermute | solution.py:704
  3.1 4.7 %collective-permute-start = (f32[224,128]{1,0:T(8,128)S(1)}, f32[224,128]{1,0:T(8,128)S(1)}, u32[]{:S(2)}, u32[]{:S(2)}) collective-permute-start(f32[224,128]{1,0:T(8,128)S(1)} %get-tuple-element.37), channel_id=1, source_target_pairs={{0,12},{4,0},{8,4},{12,8},{1,13},{5,1},{9,5},{13,9},{2,14},{6,2},{... | collective-permute-start | bytes 344072 | tf_op jit(solution)/shard_map/ppermute | solution.py:706
  7.7 1.0 %collective-permute-start.2 = (f32[64,128]{1,0:T(8,128)S(1)}, f32[64,128]{1,0:T(8,128)S(1)}, u32[]{:S(2)}, u32[]{:S(2)}) collective-permute-start(f32[64,128]{1,0:T(8,128)S(1)} %get-tuple-element.39), channel_id=1, source_target_pairs={{0,8},{4,12},{8,0},{12,4},{1,9},{5,13},{9,1},{13,5},{2,10},{6,14},... | collective-permute-start | bytes 98312 | tf_op jit(solution)/shard_map/ppermute | solution.py:706
  8.8 0.5 %maps.1 = (bf16[512,128]{1,0:T(8,128)(2,1)S(1)}, bf16[128,128]{1,0:T(8,128)(2,1)S(1)}, f32[256,128]{1,0:T(8,128)S(1)}, bf16[512,128]{1,0:T(8,128)(2,1)S(1)}, bf1...) custom-call(s32[4,128]{1,0:T(4,128)S(1)} %get-tuple-element.31.holde, ...), custom_call_target="tpu_custom_call" | custom-call | bytes 3000000 | tf_op jit(solution)/shard_map/maps/pallas_call | solution.py:723
  9.3 6.4 %collective-permute-done.2.refs_6_.refs_2_ = f32[64,128]{1,0:T(8,128)S(1)} collective-permute-done((f32[64,128]{1,0:T(8,128)S(1)}, f32[64,128]{1,0:T(8,128)S(1)}, u32[]{:S(2)}, u32[]{:S(2)}) %collective-permute-start.2) | collective-permute-done | bytes 32800 | tf_op jit(solution)/shard_map/ppermute | solution.py:706
  15.7 0.0 collective-permute-done.refs_4_.refs_0_
  15.7 0.0 collective-permute-done.1.refs_5_.refs_1_
  15.8 0.1 collective-permute-start.4
  15.8 0.6 %fill_own.1 = (f32[42,128,128]{2,1,0:T(8,128)S(1)}, f32[216,128]{1,0:T(8,128)S(1)}, f32[152,128]{1,0:T(8,128)S(1)}, f32[256,128]{1,0:T(8,128)S(1)}) custom-call(f32[2944,128]{1,0:T(8,128)S(1)} %get-tuple-element.30.refs_0_, bf16[512,128]{1,0:T(8,128)(2,1)S(1)} %get-tuple-element.34.refs_1_, bf16[128,128]{1,0:T(8,128)(2,1)S(1)} %get-tuple-element.35.refs_2_, ...), custom_call_target="tpu_custom_call" | custom-call | bytes 4500000 | tf_op jit(solution)/shard_map/fill_own/pallas_call | solution.py:748
  16.4 1.5 %collective-permute-start.5 = (f32[216,128]{1,0:T(8,128)S(1)}, f32[216,128]{1,0:T(8,128)S(1)}, u32[]{:S(2)}, u32[]{:S(2)}) collective-permute-start(f32[216,128]{1,0:T(8,128)S(1)} %get-tuple-element.51), channel_id=1, source_target_pairs={{0,2},{2,0},{1,3},{3,1},{4,6},{6,4},{5,7},{7,5},{8,10},{10,8},{9,1... | collective-permute-start | bytes 331784 | tf_op jit(solution)/shard_map/ppermute | solution.py:766
  18.0 0.4 %collective-permute-start.6 = (f32[152,128]{1,0:T(8,128)S(1)}, f32[152,128]{1,0:T(8,128)S(1)}, u32[]{:S(2)}, u32[]{:S(2)}) collective-permute-start(f32[152,128]{1,0:T(8,128)S(1)} %get-tuple-element.52), channel_id=1, source_target_pairs={{0,3},{1,2},{2,1},{3,0},{4,7},{5,6},{6,5},{7,4},{8,11},{9,10},{10,... | collective-permute-start | bytes 233480 | tf_op jit(solution)/shard_map/ppermute | solution.py:770
  18.3 0.5 %fill_partner.1.refs_1_ = f32[42,128,128]{2,1,0:T(8,128)S(1)} custom-call(f32[2944,128]{1,0:T(8,128)S(1)} %collective-permute-done.3.refs_0_, bf16[512,128]{1,0:T(8,128)(2,1)S(1)} %get-tuple-element.41.refs_1_, bf16[128,128]{1,0:T(8,128)(2,1)S(1)} %get-tuple-element.42.refs_2_, f32[256,128]{1,0:T(8,128)S(1)} %get-tuple-element.43.refs_3_, ...), custom_call_target="tpu_custom_call" | custom-call | bytes 4500000 | tf_op jit(solution)/shard_map/fill_partner/pallas_call | solution.py:772
  18.8 4.5 %tile_sweeps.1 = (f32[4,128,128]{2,1,0:T(8,128)S(1)}, f32[2,128,128]{2,1,0:T(8,128)S(1)}, f32[80,8,128]{2,1,0:T(8,128)S(1)}) custom-call(f32[42,128,128]{2,1,0:T(8,128)S(1)} %get-tuple-element.40.refs_0_, f32[42,128,128]{2,1,0:T(8,128)S(1)} %fill_partner.1.refs_1_, bf16[128,512]{1,0:T(8,128)(2,1)S(1)} %get-tuple-element.45.refs_2_), custom_call_target="tpu_custom_call" | custom-call | bytes 21000000 | tf_op jit(solution)/shard_map/tile_sweeps/pallas_call | solution.py:785
  23.3 0.0 collective-permute-done.6.refs_8_
  23.3 1.4 %edge_sweeps.1 = (f32[4,8,128]{2,1,0:T(8,128)S(1)}, f32[32,128]{1,0:T(8,128)S(1)}, f32[32,128]{1,0:T(8,128)S(1)}, f32[32,128]{1,0:T(8,128)S(1)}, f32[32,128]{1,0:T(8,128)S(1)}) custom-call(f32[42,128,128]{2,1,0:T(8,128)S(1)} %get-tuple-element.40.refs_0_, f32[42,128,128]{2,1,0:T(8,128)S(1)} %fill_partner.1.refs_1_, ...), custom_call_target="tpu_custom_call" | custom-call | bytes 4500000 | tf_op jit(solution)/shard_map/edge_sweeps/pallas_call | solution.py:800
  24.7 0.5 %collective-permute-start.7 = (f32[32,128]{1,0:T(8,128)S(1)}, f32[32,128]{1,0:T(8,128)S(1)}, u32[]{:S(2)}, u32[]{:S(2)}) collective-permute-start(f32[32,128]{1,0:T(8,128)S(1)} %get-tuple-element.55), channel_id=1, source_target_pairs={{0,4},{4,8},{8,12},{12,0},{1,5},{5,9},{9,13},{13,1},{2,6},{6,10},{... | collective-permute-start | bytes 49160 | tf_op jit(solution)/shard_map/ppermute | solution.py:814
  25.2 1.3 %collective-permute-start.8 = (f32[32,128]{1,0:T(8,128)S(1)}, f32[32,128]{1,0:T(8,128)S(1)}, u32[]{:S(2)}, u32[]{:S(2)}) collective-permute-start(f32[32,128]{1,0:T(8,128)S(1)} %get-tuple-element.56), channel_id=1, source_target_pairs={{0,8},{4,12},{8,0},{12,4},{1,9},{5,13},{9,1},{13,5},{2,10},{6,14},... | collective-permute-start | bytes 49160 | tf_op jit(solution)/shard_map/ppermute | solution.py:814
  26.5 2.8 %collective-permute-start.9 = (f32[32,128]{1,0:T(8,128)S(1)}, f32[32,128]{1,0:T(8,128)S(1)}, u32[]{:S(2)}, u32[]{:S(2)}) collective-permute-start(f32[32,128]{1,0:T(8,128)S(1)} %get-tuple-element.57), channel_id=1, source_target_pairs={{0,12},{4,0},{8,4},{12,8},{1,13},{5,1},{9,5},{13,9},{2,14},{6,2},{... | collective-permute-start | bytes 49160 | tf_op jit(solution)/shard_map/ppermute | solution.py:814
  29.3 0.7 %merge.1 = f32[4,128,128]{2,1,0:T(8,128)} custom-call(f32[4,128,128]{2,1,0:T(8,128)S(1)} %get-tuple-element.46.whole_ref, f32[4,8,128]{2,1,0:T(8,128)S(1)} %get-tuple-element.53.heat_ref), custom_call_target="tpu_custom_call" | custom-call | bytes 3000000 | tf_op jit(solution)/shard_map/merge/pallas_call | solution.py:815
  30.1 0.4 %collective-permute-done.7 = f32[32,128]{1,0:T(8,128)S(1)} collective-permute-done((f32[32,128]{1,0:T(8,128)S(1)}, f32[32,128]{1,0:T(8,128)S(1)}, u32[]{:S(2)}, u32[]{:S(2)}) %collective-permute-start.7) | collective-permute-done | bytes 16416 | tf_op jit(solution)/shard_map/ppermute | solution.py:814
  30.4 0.0 collective-permute-done.8
  30.5 0.4 %collective-permute-done.9 = f32[32,128]{1,0:T(8,128)S(1)} collective-permute-done((f32[32,128]{1,0:T(8,128)S(1)}, f32[32,128]{1,0:T(8,128)S(1)}, u32[]{:S(2)}, u32[]{:S(2)}) %collective-permute-start.9) | collective-permute-done | bytes 16416 | tf_op jit(solution)/shard_map/ppermute | solution.py:814
  30.9 0.6 %add_bitcast_fusion = f32[1,32,128]{2,1,0:T(8,128)} fusion(f32[32,128]{1,0:T(8,128)S(1)} %collective-permute-done.9, f32[32,128]{1,0:T(8,128)S(1)} %collective-permute-done.8, f32[32,128]{1,0:T(8,128)S(1)} %get-tuple-element.54, f32[32,128]{1,0:T(8,128)S(1)} %collective-permute-done.7), kind=kLoop, calls=%fused_computation | loop fusion | flops 12288 | bytes 81920 | tf_op jit(solution)/shard_map/broadcast_in_dim | solution.py:826
  (5 shorter events, 0.0 us)
Async XLA Ops:
  2.6 15.8 %collective-permute-start.3 = (f32[2944,128]{1,0:T(8,128)S(1)}, f32[2944,128]{1,0:T(8,128)S(1)}, u32[]{:S(2)}, u32[]{:S(2)}) collective-permute-start(f32[2944,128]{1,0:T(8,128)S(1)} %get-tuple-element.30.refs_0_), channel_id=1, source_target_pairs={{0,1},{1,0},{2,3},{3,2},{4,5},{5,4},{6,7},{7,6},{8,9},{9,8},{10,11... | collective-permute-start | bytes 4521992 | tf_op jit(solution)/shard_map/ppermute | solution.py:704
  3.1 12.6 %collective-permute-start = (f32[224,128]{1,0:T(8,128)S(1)}, f32[224,128]{1,0:T(8,128)S(1)}, u32[]{:S(2)}, u32[]{:S(2)}) collective-permute-start(f32[224,128]{1,0:T(8,128)S(1)} %get-tuple-element.37), channel_id=1, source_target_pairs={{0,12},{4,0},{8,4},{12,8},{1,13},{5,1},{9,5},{13,9},{2,14},{6,2},{... | collective-permute-start | bytes 344072 | tf_op jit(solution)/shard_map/ppermute | solution.py:706
  7.7 8.0 %collective-permute-start.1 = (f32[224,128]{1,0:T(8,128)S(1)}, f32[224,128]{1,0:T(8,128)S(1)}, u32[]{:S(2)}, u32[]{:S(2)}) collective-permute-start(f32[224,128]{1,0:T(8,128)S(1)} %get-tuple-element.38), channel_id=1, source_target_pairs={{0,4},{4,8},{8,12},{12,0},{1,5},{5,9},{9,13},{13,1},{2,6},{6,10},{... | collective-permute-start | bytes 344072 | tf_op jit(solution)/shard_map/ppermute | solution.py:706
  7.7 8.0 %collective-permute-start.2 = (f32[64,128]{1,0:T(8,128)S(1)}, f32[64,128]{1,0:T(8,128)S(1)}, u32[]{:S(2)}, u32[]{:S(2)}) collective-permute-start(f32[64,128]{1,0:T(8,128)S(1)} %get-tuple-element.39), channel_id=1, source_target_pairs={{0,8},{4,12},{8,0},{12,4},{1,9},{5,13},{9,1},{13,5},{2,10},{6,14},... | collective-permute-start | bytes 98312 | tf_op jit(solution)/shard_map/ppermute | solution.py:706
  15.8 2.6 %collective-permute-start.4 = (f32[512,128]{1,0:T(8,128)S(1)}, f32[512,128]{1,0:T(8,128)S(1)}, u32[]{:S(2)}, u32[]{:S(2)}) collective-permute-start(f32[512,128]{1,0:T(8,128)S(1)} %join.1), channel_id=1, source_target_pairs={{0,1},{1,0},{2,3},{3,2},{4,5},{5,4},{6,7},{7,6},{8,9},{9,8},{10,11... | collective-permute-start | bytes 786440 | tf_op jit(solution)/shard_map/ppermute | solution.py:747
  16.4 6.8 %collective-permute-start.5 = (f32[216,128]{1,0:T(8,128)S(1)}, f32[216,128]{1,0:T(8,128)S(1)}, u32[]{:S(2)}, u32[]{:S(2)}) collective-permute-start(f32[216,128]{1,0:T(8,128)S(1)} %get-tuple-element.51), channel_id=1, source_target_pairs={{0,2},{2,0},{1,3},{3,1},{4,6},{6,4},{5,7},{7,5},{8,10},{10,8},{9,1... | collective-permute-start | bytes 331784 | tf_op jit(solution)/shard_map/ppermute | solution.py:766
  18.0 5.3 %collective-permute-start.6 = (f32[152,128]{1,0:T(8,128)S(1)}, f32[152,128]{1,0:T(8,128)S(1)}, u32[]{:S(2)}, u32[]{:S(2)}) collective-permute-start(f32[152,128]{1,0:T(8,128)S(1)} %get-tuple-element.52), channel_id=1, source_target_pairs={{0,3},{1,2},{2,1},{3,0},{4,7},{5,6},{6,5},{7,4},{8,11},{9,10},{10,... | collective-permute-start | bytes 233480 | tf_op jit(solution)/shard_map/ppermute | solution.py:770
  24.7 5.7 %collective-permute-start.7 = (f32[32,128]{1,0:T(8,128)S(1)}, f32[32,128]{1,0:T(8,128)S(1)}, u32[]{:S(2)}, u32[]{:S(2)}) collective-permute-start(f32[32,128]{1,0:T(8,128)S(1)} %get-tuple-element.55), channel_id=1, source_target_pairs={{0,4},{4,8},{8,12},{12,0},{1,5},{5,9},{9,13},{13,1},{2,6},{6,10},{... | collective-permute-start | bytes 49160 | tf_op jit(solution)/shard_map/ppermute | solution.py:814
  25.2 5.3 %collective-permute-start.8 = (f32[32,128]{1,0:T(8,128)S(1)}, f32[32,128]{1,0:T(8,128)S(1)}, u32[]{:S(2)}, u32[]{:S(2)}) collective-permute-start(f32[32,128]{1,0:T(8,128)S(1)} %get-tuple-element.56), channel_id=1, source_target_pairs={{0,8},{4,12},{8,0},{12,4},{1,9},{5,13},{9,1},{13,5},{2,10},{6,14},... | collective-permute-start | bytes 49160 | tf_op jit(solution)/shard_map/ppermute | solution.py:814
  26.5 4.4 %collective-permute-start.9 = (f32[32,128]{1,0:T(8,128)S(1)}, f32[32,128]{1,0:T(8,128)S(1)}, u32[]{:S(2)}, u32[]{:S(2)}) collective-permute-start(f32[32,128]{1,0:T(8,128)S(1)} %get-tuple-element.57), channel_id=1, source_target_pairs={{0,12},{4,0},{8,4},{12,8},{1,13},{5,1},{9,5},{13,9},{2,14},{6,2},{... | collective-permute-start | bytes 49160 | tf_op jit(solution)/shard_map/ppermute | solution.py:814
where the time goes:
time: 31.6 us; the launch traced here: 31.5 us
  starting transfers between devices  12.7 us (40%)
  Pallas kernels  10.2 us (32%)
  waiting for transfers between devices  7.27 us (23%)
  between operations  0.71 us (2%)
  other arithmetic  0.61 us (2%)
    ppermute x3, waiting for transfers between devices, from_distance(): return lax.ppermute(value, 'gx', [(i, (i - k) % gx) for i in range(gx)])  6.44 us
    ppermute x3, starting transfers between devices, from_distance(): return lax.ppermute(value, 'gx', [(i, (i - k) % gx) for i in range(gx)])  5.67 us
    ppermute x3, starting transfers between devices, local(): lax.ppermute(results[1 + k], 'gx', [(i, (i + k) % gx) for i in range(gx)])  4.61 us
    pallas_call x1, Pallas kernels, local(): pl.pallas_call(functools.partial(tile_kernel, gx, gy, shape), out_shape=(...  4.48 us
    pallas_call x1, Pallas kernels, local(): pl.pallas_call(functools.partial(pack_kernel, shape), out_shape=(struct(R...  1.92 us
    ppermute x1, starting transfers between devices, local(): along = [lax.ppermute(strips[side], 'gy', pairs) for side, pairs in routes]  1.51 us
    pallas_call x1, Pallas kernels, local(): pl.pallas_call(functools.partial(edge_kernel, gx, gy, shape, seg), out_sh...  1.42 us
    ppermute x3, waiting for transfers between devices, local(): lax.ppermute(results[1 + k], 'gx', [(i, (i + k) % gx) for i in range(gx)])  0.82 us
  transfers between devices with their start and end apart: 10, of which 3 were waited for; matrix products, arithmetic and copies ran while one was open for 0% of the time, Pallas kernels for 22%

commit v1 on v0

--- a/solution.py
+++ b/solution.py
@@ -400,14 +400,37 @@
         q_ref[i, here, :] = t[i] * root
 
 
-def sweep(src_ref, dst_ref, at, n, count, coefs, base):
+def shifted_sums(distance):
+    to = lax.broadcasted_iota(jnp.int32, (2 * LANES, LANES), 1)
+    of = lax.broadcasted_iota(jnp.int32, (2 * LANES, LANES), 0) % LANES
+    return as_onehot(jnp.abs(of - to) == distance)
+
+
+def sweep_edges(src_ref, dst_ref, at, n, coefs, base, matrices):
     a_ref, q_ref, r_ref = coefs[:3]
     total = src_ref.shape[0]
     here, there = pl.ds(base, n), pl.ds(at, n)
-    which = planes_of(count, total)
+
+    def product(value, matrix):
+        return jnp.dot(jnp.concatenate(split(value), axis=1), matrix, preferred_element_type=jnp.float32)
+
+    for i in (total - 2, total - 1):
+        centre = src_ref[i, there, :]
+        beside = product(centre, matrices[0])
+        above = product(q_ref[i, here, :] * centre, matrices[1])
+        beside = beside + (src_ref[i, pl.ds(at - 1, n), :] + src_ref[i, pl.ds(at + 1, n), :])
+        dst_ref[i, there, :] = r_ref[i, here, :] + a_ref[i, here, :] * (beside + q_ref[i, here, :] * above)
+
+
+def sweep(src_ref, dst_ref, at, n, count, coefs, base, edges=True):
+    a_ref, q_ref, r_ref = coefs[:3]
+    total = src_ref.shape[0]
+    here, there = pl.ds(base, n), pl.ds(at, n)
+    which = planes_of(count, total) if edges else list(range(count))
     sums = lateral(src_ref, at, n, which)
-    scaled = [q_ref[i, here, :] * src_ref[i, there, :] for i in planes_of(min(count + 1, total - 2), total)]
-    above = vertical(scaled[:-2], scaled[-2:], count)
+    scaled = [q_ref[i, here, :] * src_ref[i, there, :] for i in range(min(count + 1, total - 2))]
+    outer = [q_ref[i, here, :] * src_ref[i, there, :] for i in which[count:]]
+    above = vertical(scaled, outer, count)
     for j, i in enumerate(which):
         dst_ref[i, there, :] = r_ref[i, here, :] + a_ref[i, here, :] * (sums[j] + q_ref[i, here, :] * above[j])
 
@@ -495,6 +518,7 @@
 
     bufs = (va_ref, vb_ref)
     sides = sides_of(gy, y)
+    matrices = shifted_sums(1), shifted_sums(GROUP)
 
     def sweep_all(number, which, count):
         src_ref, dst_ref = bufs[which], bufs[1 - which]
@@ -502,8 +526,9 @@
             inner = pl.ds(PAD + inner_at(above, rows), HALO)
             for i in range(total):
                 level_ref[(side * STEPS * ITERS + number) * total + i] = src_ref[i, inner, :]
+        sweep_edges(src_ref, dst_ref, PAD, rows, coefs, 0, matrices)
         for at in range(0, rows, n):
-            sweep(src_ref, dst_ref, PAD + at, n, count, coefs, at)
+            sweep(src_ref, dst_ref, PAD + at, n, count, coefs, at, edges=False)
 
     def after(step):
         last = step == STEPS - 1

time: 31.6 us -> 31.5 us (level)
  Pallas kernels: 10.2 us -> 9.52 us
  waiting for transfers between devices: 7.27 us -> 7.82 us
    pallas_call x1, Pallas kernels: 4.48 us -> 3.84 us  [local(): pl.pallas_call(functools.partial(tile_kernel, gx, gy, shape), out_shape=(...]
    ppermute x1, waiting for transfers between devices: 0.01 us -> 0.55 us  [local(): across.append(lax.ppermute(partner_strips[side], ('gy', 'gz'), both))]
  transfers between devices with their start and end apart: 10 -> 10, of which waited for: 3 -> 4; matrix products, arithmetic and copies ran while one was open for 0% -> 0% of each run, Pallas kernels for 22% -> 20%
where the time goes in v1:
time: 31.5 us; the launch traced here: 31.4 us
  starting transfers between devices  12.7 us (40%)
  Pallas kernels  9.52 us (30%)
  waiting for transfers between devices  7.82 us (25%)
  between operations  0.69 us (2%)
  other arithmetic  0.61 us (2%)
    ppermute x3, waiting for transfers between devices, from_distance(): return lax.ppermute(value, 'gx', [(i, (i - k) % gx) for i in range(gx)])  6.44 us
    ppermute x3, starting transfers between devices, from_distance(): return lax.ppermute(value, 'gx', [(i, (i - k) % gx) for i in range(gx)])  5.67 us
    ppermute x3, starting transfers between devices, local(): lax.ppermute(results[1 + k], 'gx', [(i, (i + k) % gx) for i in range(gx)])  4.61 us
    pallas_call x1, Pallas kernels, local(): pl.pallas_call(functools.partial(tile_kernel, gx, gy, shape), out_shape=(...  3.84 us
    pallas_call x1, Pallas kernels, local(): pl.pallas_call(functools.partial(pack_kernel, shape), out_shape=(struct(R...  1.92 us
    ppermute x1, starting transfers between devices, local(): along = [lax.ppermute(strips[side], 'gy', pairs) for side, pairs in routes]  1.51 us
    pallas_call x1, Pallas kernels, local(): pl.pallas_call(functools.partial(edge_kernel, gx, gy, shape, seg), out_sh...  1.42 us
    ppermute x3, waiting for transfers between devices, local(): lax.ppermute(results[1 + k], 'gx', [(i, (i + k) % gx) for i in range(gx)])  0.82 us
  transfers between devices with their start and end apart: 10, of which 4 were waited for; matrix products, arithmetic and copies ran while one was open for 0% of the time, Pallas kernels for 20%

profile of v1, /device:TPU:0, one launch (start us, length us, event | category | flops | bytes accessed | tf_op | source)
XLA Modules:
  0.0 31.4 jit_solution(3483207621372803527)
XLA Ops:
  0.6 1.9 %pack.1 = (f32[2944,128]{1,0:T(8,128)S(1)}, f32[224,128]{1,0:T(8,128)S(1)}, f32[224,128]{1,0:T(8,128)S(1)}, f32[64,128]{1,0:T(8,128)S(1)}, s32[4,128]{1,0:T(4,12...) custom-call(f32[512,128]{1,0:T(8,128)} %bitcast.10, f32[512,128]{1,0:T(8,128)} %bitcast.11, f32[512,128]{1,0:T(8,128)} %bitcast.12, ...), custom_call_target="tpu_custom_call" | custom-call | tf_op jit(solution)/shard_map/pack/pallas_call | solution.py:712
  2.6 0.5 %collective-permute-start.3 = (f32[2944,128]{1,0:T(8,128)S(1)}, f32[2944,128]{1,0:T(8,128)S(1)}, u32[]{:S(2)}, u32[]{:S(2)}) collective-permute-start(f32[2944,128]{1,0:T(8,128)S(1)} %get-tuple-element.30.refs_0_), channel_id=1, source_target_pairs={{0,1},{1,0},{2,3},{3,2},{4,5},{5,4},{6,7},{7,6},{8,9},{9,8},{10,11... | collective-permute-start | bytes 4521992 | tf_op jit(solution)/shard_map/ppermute | solution.py:729
  3.1 4.7 %collective-permute-start = (f32[224,128]{1,0:T(8,128)S(1)}, f32[224,128]{1,0:T(8,128)S(1)}, u32[]{:S(2)}, u32[]{:S(2)}) collective-permute-start(f32[224,128]{1,0:T(8,128)S(1)} %get-tuple-element.37), channel_id=1, source_target_pairs={{0,12},{4,0},{8,4},{12,8},{1,13},{5,1},{9,5},{13,9},{2,14},{6,2},{... | collective-permute-start | bytes 344072 | tf_op jit(solution)/shard_map/ppermute | solution.py:731
  7.7 1.0 %collective-permute-start.2 = (f32[64,128]{1,0:T(8,128)S(1)}, f32[64,128]{1,0:T(8,128)S(1)}, u32[]{:S(2)}, u32[]{:S(2)}) collective-permute-start(f32[64,128]{1,0:T(8,128)S(1)} %get-tuple-element.39), channel_id=1, source_target_pairs={{0,8},{4,12},{8,0},{12,4},{1,9},{5,13},{9,1},{13,5},{2,10},{6,14},... | collective-permute-start | bytes 98312 | tf_op jit(solution)/shard_map/ppermute | solution.py:731
  8.8 0.5 %maps.1 = (bf16[512,128]{1,0:T(8,128)(2,1)S(1)}, bf16[128,128]{1,0:T(8,128)(2,1)S(1)}, f32[256,128]{1,0:T(8,128)S(1)}, bf16[512,128]{1,0:T(8,128)(2,1)S(1)}, bf1...) custom-call(s32[4,128]{1,0:T(4,128)S(1)} %get-tuple-element.31.holde, ...), custom_call_target="tpu_custom_call" | custom-call | bytes 3000000 | tf_op jit(solution)/shard_map/maps/pallas_call | solution.py:748
  9.3 6.4 %collective-permute-done.2.refs_6_.refs_2_ = f32[64,128]{1,0:T(8,128)S(1)} collective-permute-done((f32[64,128]{1,0:T(8,128)S(1)}, f32[64,128]{1,0:T(8,128)S(1)}, u32[]{:S(2)}, u32[]{:S(2)}) %collective-permute-start.2) | collective-permute-done | bytes 32800 | tf_op jit(solution)/shard_map/ppermute | solution.py:731
  15.7 0.0 collective-permute-done.refs_4_.refs_0_
  15.8 0.1 collective-permute-start.4
  15.8 0.6 %fill_own.1 = (f32[42,128,128]{2,1,0:T(8,128)S(1)}, f32[216,128]{1,0:T(8,128)S(1)}, f32[152,128]{1,0:T(8,128)S(1)}, f32[256,128]{1,0:T(8,128)S(1)}) custom-call(f32[2944,128]{1,0:T(8,128)S(1)} %get-tuple-element.30.refs_0_, bf16[512,128]{1,0:T(8,128)(2,1)S(1)} %get-tuple-element.34.refs_1_, bf16[128,128]{1,0:T(8,128)(2,1)S(1)} %get-tuple-element.35.refs_2_, ...), custom_call_target="tpu_custom_call" | custom-call | bytes 4500000 | tf_op jit(solution)/shard_map/fill_own/pallas_call | solution.py:773
  16.4 1.5 %collective-permute-start.5 = (f32[216,128]{1,0:T(8,128)S(1)}, f32[216,128]{1,0:T(8,128)S(1)}, u32[]{:S(2)}, u32[]{:S(2)}) collective-permute-start(f32[216,128]{1,0:T(8,128)S(1)} %get-tuple-element.51), channel_id=1, source_target_pairs={{0,2},{2,0},{1,3},{3,1},{4,6},{6,4},{5,7},{7,5},{8,10},{10,8},{9,1... | collective-permute-start | bytes 331784 | tf_op jit(solution)/shard_map/ppermute | solution.py:791
  18.0 0.4 %collective-permute-start.6 = (f32[152,128]{1,0:T(8,128)S(1)}, f32[152,128]{1,0:T(8,128)S(1)}, u32[]{:S(2)}, u32[]{:S(2)}) collective-permute-start(f32[152,128]{1,0:T(8,128)S(1)} %get-tuple-element.52), channel_id=1, source_target_pairs={{0,3},{1,2},{2,1},{3,0},{4,7},{5,6},{6,5},{7,4},{8,11},{9,10},{10,... | collective-permute-start | bytes 233480 | tf_op jit(solution)/shard_map/ppermute | solution.py:795
  18.3 0.5 %fill_partner.1.refs_1_ = f32[42,128,128]{2,1,0:T(8,128)S(1)} custom-call(f32[2944,128]{1,0:T(8,128)S(1)} %collective-permute-done.3.refs_0_, bf16[512,128]{1,0:T(8,128)(2,1)S(1)} %get-tuple-element.41.refs_1_, bf16[128,128]{1,0:T(8,128)(2,1)S(1)} %get-tuple-element.42.refs_2_, f32[256,128]{1,0:T(8,128)S(1)} %get-tuple-element.43.refs_3_, ...), custom_call_target="tpu_custom_call" | custom-call | bytes 4500000 | tf_op jit(solution)/shard_map/fill_partner/pallas_call | solution.py:797
  18.8 3.8 %tile_sweeps.1 = (f32[4,128,128]{2,1,0:T(8,128)S(1)}, f32[2,128,128]{2,1,0:T(8,128)S(1)}, f32[80,8,128]{2,1,0:T(8,128)S(1)}) custom-call(f32[42,128,128]{2,1,0:T(8,128)S(1)} %get-tuple-element.40.refs_0_, f32[42,128,128]{2,1,0:T(8,128)S(1)} %fill_partner.1.refs_1_, bf16[128,512]{1,0:T(8,128)(2,1)S(1)} %get-tuple-element.45.refs_2_), custom_call_target="tpu_custom_call" | custom-call | bytes 21000000 | tf_op jit(solution)/shard_map/tile_sweeps/pallas_call | solution.py:810
  22.6 0.5 %collective-permute-done.6.refs_8_ = f32[152,128]{1,0:T(8,128)S(1)} collective-permute-done((f32[152,128]{1,0:T(8,128)S(1)}, f32[152,128]{1,0:T(8,128)S(1)}, u32[]{:S(2)}, u32[]{:S(2)}) %collective-permute-start.6) | collective-permute-done | bytes 77856 | tf_op jit(solution)/shard_map/ppermute | solution.py:795
  23.2 0.0 collective-permute-done.5.refs_7_
  23.2 1.4 %edge_sweeps.1 = (f32[4,8,128]{2,1,0:T(8,128)S(1)}, f32[32,128]{1,0:T(8,128)S(1)}, f32[32,128]{1,0:T(8,128)S(1)}, f32[32,128]{1,0:T(8,128)S(1)}, f32[32,128]{1,0:T(8,128)S(1)}) custom-call(f32[42,128,128]{2,1,0:T(8,128)S(1)} %get-tuple-element.40.refs_0_, f32[42,128,128]{2,1,0:T(8,128)S(1)} %fill_partner.1.refs_1_, ...), custom_call_target="tpu_custom_call" | custom-call | bytes 4500000 | tf_op jit(solution)/shard_map/edge_sweeps/pallas_call | solution.py:825
  24.6 0.5 %collective-permute-start.7 = (f32[32,128]{1,0:T(8,128)S(1)}, f32[32,128]{1,0:T(8,128)S(1)}, u32[]{:S(2)}, u32[]{:S(2)}) collective-permute-start(f32[32,128]{1,0:T(8,128)S(1)} %get-tuple-element.55), channel_id=1, source_target_pairs={{0,4},{4,8},{8,12},{12,0},{1,5},{5,9},{9,13},{13,1},{2,6},{6,10},{... | collective-permute-start | bytes 49160 | tf_op jit(solution)/shard_map/ppermute | solution.py:839
  25.1 1.3 %collective-permute-start.8 = (f32[32,128]{1,0:T(8,128)S(1)}, f32[32,128]{1,0:T(8,128)S(1)}, u32[]{:S(2)}, u32[]{:S(2)}) collective-permute-start(f32[32,128]{1,0:T(8,128)S(1)} %get-tuple-element.56), channel_id=1, source_target_pairs={{0,8},{4,12},{8,0},{12,4},{1,9},{5,13},{9,1},{13,5},{2,10},{6,14},... | collective-permute-start | bytes 49160 | tf_op jit(solution)/shard_map/ppermute | solution.py:839
  26.4 2.8 %collective-permute-start.9 = (f32[32,128]{1,0:T(8,128)S(1)}, f32[32,128]{1,0:T(8,128)S(1)}, u32[]{:S(2)}, u32[]{:S(2)}) collective-permute-start(f32[32,128]{1,0:T(8,128)S(1)} %get-tuple-element.57), channel_id=1, source_target_pairs={{0,12},{4,0},{8,4},{12,8},{1,13},{5,1},{9,5},{13,9},{2,14},{6,2},{... | collective-permute-start | bytes 49160 | tf_op jit(solution)/shard_map/ppermute | solution.py:839
  29.2 0.7 %merge.1 = f32[4,128,128]{2,1,0:T(8,128)} custom-call(f32[4,128,128]{2,1,0:T(8,128)S(1)} %get-tuple-element.46.whole_ref, f32[4,8,128]{2,1,0:T(8,128)S(1)} %get-tuple-element.53.heat_ref), custom_call_target="tpu_custom_call" | custom-call | bytes 3000000 | tf_op jit(solution)/shard_map/merge/pallas_call | solution.py:840
  29.9 0.3 %collective-permute-done.7 = f32[32,128]{1,0:T(8,128)S(1)} collective-permute-done((f32[32,128]{1,0:T(8,128)S(1)}, f32[32,128]{1,0:T(8,128)S(1)}, u32[]{:S(2)}, u32[]{:S(2)}) %collective-permute-start.7) | collective-permute-done | bytes 16416 | tf_op jit(solution)/shard_map/ppermute | solution.py:839
  30.3 0.0 collective-permute-done.8
  30.3 0.5 %collective-permute-done.9 = f32[32,128]{1,0:T(8,128)S(1)} collective-permute-done((f32[32,128]{1,0:T(8,128)S(1)}, f32[32,128]{1,0:T(8,128)S(1)}, u32[]{:S(2)}, u32[]{:S(2)}) %collective-permute-start.9) | collective-permute-done | bytes 16416 | tf_op jit(solution)/shard_map/ppermute | solution.py:839
  30.8 0.6 %add_bitcast_fusion = f32[1,32,128]{2,1,0:T(8,128)} fusion(f32[32,128]{1,0:T(8,128)S(1)} %collective-permute-done.9, f32[32,128]{1,0:T(8,128)S(1)} %collective-permute-done.8, f32[32,128]{1,0:T(8,128)S(1)} %get-tuple-element.54, f32[32,128]{1,0:T(8,128)S(1)} %collective-permute-done.7), kind=kLoop, calls=%fused_computation | loop fusion | flops 12288 | bytes 81920 | tf_op jit(solution)/shard_map/broadcast_in_dim | solution.py:851
  (5 shorter events, 0.0 us)
Async XLA Ops:
  2.6 15.8 %collective-permute-start.3 = (f32[2944,128]{1,0:T(8,128)S(1)}, f32[2944,128]{1,0:T(8,128)S(1)}, u32[]{:S(2)}, u32[]{:S(2)}) collective-permute-start(f32[2944,128]{1,0:T(8,128)S(1)} %get-tuple-element.30.refs_0_), channel_id=1, source_target_pairs={{0,1},{1,0},{2,3},{3,2},{4,5},{5,4},{6,7},{7,6},{8,9},{9,8},{10,11... | collective-permute-start | bytes 4521992 | tf_op jit(solution)/shard_map/ppermute | solution.py:729
  3.1 12.6 %collective-permute-start = (f32[224,128]{1,0:T(8,128)S(1)}, f32[224,128]{1,0:T(8,128)S(1)}, u32[]{:S(2)}, u32[]{:S(2)}) collective-permute-start(f32[224,128]{1,0:T(8,128)S(1)} %get-tuple-element.37), channel_id=1, source_target_pairs={{0,12},{4,0},{8,4},{12,8},{1,13},{5,1},{9,5},{13,9},{2,14},{6,2},{... | collective-permute-start | bytes 344072 | tf_op jit(solution)/shard_map/ppermute | solution.py:731
  7.7 8.0 %collective-permute-start.1 = (f32[224,128]{1,0:T(8,128)S(1)}, f32[224,128]{1,0:T(8,128)S(1)}, u32[]{:S(2)}, u32[]{:S(2)}) collective-permute-start(f32[224,128]{1,0:T(8,128)S(1)} %get-tuple-element.38), channel_id=1, source_target_pairs={{0,4},{4,8},{8,12},{12,0},{1,5},{5,9},{9,13},{13,1},{2,6},{6,10},{... | collective-permute-start | bytes 344072 | tf_op jit(solution)/shard_map/ppermute | solution.py:731
  7.7 8.0 %collective-permute-start.2 = (f32[64,128]{1,0:T(8,128)S(1)}, f32[64,128]{1,0:T(8,128)S(1)}, u32[]{:S(2)}, u32[]{:S(2)}) collective-permute-start(f32[64,128]{1,0:T(8,128)S(1)} %get-tuple-element.39), channel_id=1, source_target_pairs={{0,8},{4,12},{8,0},{12,4},{1,9},{5,13},{9,1},{13,5},{2,10},{6,14},... | collective-permute-start | bytes 98312 | tf_op jit(solution)/shard_map/ppermute | solution.py:731
  15.8 2.6 %collective-permute-start.4 = (f32[512,128]{1,0:T(8,128)S(1)}, f32[512,128]{1,0:T(8,128)S(1)}, u32[]{:S(2)}, u32[]{:S(2)}) collective-permute-start(f32[512,128]{1,0:T(8,128)S(1)} %join.1), channel_id=1, source_target_pairs={{0,1},{1,0},{2,3},{3,2},{4,5},{5,4},{6,7},{7,6},{8,9},{9,8},{10,11... | collective-permute-start | bytes 786440 | tf_op jit(solution)/shard_map/ppermute | solution.py:772
  16.4 6.7 %collective-permute-start.5 = (f32[216,128]{1,0:T(8,128)S(1)}, f32[216,128]{1,0:T(8,128)S(1)}, u32[]{:S(2)}, u32[]{:S(2)}) collective-permute-start(f32[216,128]{1,0:T(8,128)S(1)} %get-tuple-element.51), channel_id=1, source_target_pairs={{0,2},{2,0},{1,3},{3,1},{4,6},{6,4},{5,7},{7,5},{8,10},{10,8},{9,1... | collective-permute-start | bytes 331784 | tf_op jit(solution)/shard_map/ppermute | solution.py:791
  18.0 5.2 %collective-permute-start.6 = (f32[152,128]{1,0:T(8,128)S(1)}, f32[152,128]{1,0:T(8,128)S(1)}, u32[]{:S(2)}, u32[]{:S(2)}) collective-permute-start(f32[152,128]{1,0:T(8,128)S(1)} %get-tuple-element.52), channel_id=1, source_target_pairs={{0,3},{1,2},{2,1},{3,0},{4,7},{5,6},{6,5},{7,4},{8,11},{9,10},{10,... | collective-permute-start | bytes 233480 | tf_op jit(solution)/shard_map/ppermute | solution.py:795
  24.6 5.7 %collective-permute-start.7 = (f32[32,128]{1,0:T(8,128)S(1)}, f32[32,128]{1,0:T(8,128)S(1)}, u32[]{:S(2)}, u32[]{:S(2)}) collective-permute-start(f32[32,128]{1,0:T(8,128)S(1)} %get-tuple-element.55), channel_id=1, source_target_pairs={{0,4},{4,8},{8,12},{12,0},{1,5},{5,9},{9,13},{13,1},{2,6},{6,10},{... | collective-permute-start | bytes 49160 | tf_op jit(solution)/shard_map/ppermute | solution.py:839
  25.1 5.2 %collective-permute-start.8 = (f32[32,128]{1,0:T(8,128)S(1)}, f32[32,128]{1,0:T(8,128)S(1)}, u32[]{:S(2)}, u32[]{:S(2)}) collective-permute-start(f32[32,128]{1,0:T(8,128)S(1)} %get-tuple-element.56), channel_id=1, source_target_pairs={{0,8},{4,12},{8,0},{12,4},{1,9},{5,13},{9,1},{13,5},{2,10},{6,14},... | collective-permute-start | bytes 49160 | tf_op jit(solution)/shard_map/ppermute | solution.py:839
  26.4 4.4 %collective-permute-start.9 = (f32[32,128]{1,0:T(8,128)S(1)}, f32[32,128]{1,0:T(8,128)S(1)}, u32[]{:S(2)}, u32[]{:S(2)}) collective-permute-start(f32[32,128]{1,0:T(8,128)S(1)} %get-tuple-element.57), channel_id=1, source_target_pairs={{0,12},{4,0},{8,4},{12,8},{1,13},{5,1},{9,5},{13,9},{2,14},{6,2},{... | collective-permute-start | bytes 49160 | tf_op jit(solution)/shard_map/ppermute | solution.py:839

commit v2 on v1

--- a/solution.py
+++ b/solution.py
@@ -208,7 +208,7 @@
 def maps_kernel(gx, gy, shape, holder_ref, stratum_ref, transverse_ref, *refs):
     layers, rows = shape
     plane = layers * rows
-    picks_ref, beside_ref, mine_ref = refs[6:]
+    picks_ref, beside_ref, mine_ref, near_ref, line_ref = refs[6:]
     x, y, z = (lax.axis_index(a) for a in ("gx", "gy", "gz"))
     n = holder_ref.shape[1]
     for partner in range(2):
@@ -218,6 +218,17 @@
         cell = jnp.where(holder == x, layer * rows + row, -1)
         cells_ref[...] = as_onehot(lax.broadcasted_iota(jnp.int32, (plane, n), 0) == cell)
         rows_ref[...] = as_onehot(lax.broadcasted_iota(jnp.int32, (rows, n), 0) == row)
+        if not partner:
+            near, m = layers * HALO, 2 * HALO
+            for side, (above, _) in enumerate(sides_of(gy, y)):
+                start = edge_at(above, rows)
+                at_edge = row // HALO == start // HALO
+                cell = jnp.where(jnp.logical_and(holder == x, at_edge), layer * HALO + row - start, -1)
+                near_ref[side * near : (side + 1) * near, :] = as_onehot(
+                    lax.broadcasted_iota(jnp.int32, (near, n), 0) == cell
+                )
+                cell = jnp.where(at_edge, row - start, -1)
+                line_ref[side * m : (side + 1) * m, :] = as_onehot(lax.broadcasted_iota(jnp.int32, (m, n), 0) == cell)
         holder, layer, row = (columns[:, j : j + 1].astype(jnp.int32) for j in range(3))
         lane = lane_of(n)
         first = lane % GROUP < HALO
@@ -268,26 +279,17 @@
     cells_ref, where_ref, rows_ref, masks_ref = refs[:4]
     plane, chunk = layers * rows, rows // 4
     lengths = lengths_of(gx, chunk, seg)
+    x, z = lax.axis_index("gx"), lax.axis_index("gz")
     if partner:
-        sources = [(refs[4], sum(lengths[:k])) for k in range(gx - 1)]
-        refs = refs[5:]
+        late_ref, out_ref, coef_ref, warmth_ref = refs[4:]
+        sources = [(late_ref, sum(lengths[:k])) for k in range(gx - 1)]
+        lay_segments(x, gx, seg, chunk, cells_ref, RAW * plane, sources, coef_ref, warmth_ref)
+        coef, warmth = coef_ref[...], warmth_ref[...]
     else:
-        sources = [(ref, 0) for ref in refs[4 : 4 + gx - 1]]
-        refs = refs[4 + gx - 1 :]
-    sides = 1 if gy == 2 else 2
-    out_ref = refs[0]
-    if partner:
-        coef_ref, warmth_ref = refs[1:3]
-    else:
-        strip_refs, partner_refs, segments_ref = refs[1 : 1 + sides], refs[1 + sides : 1 + 2 * sides], refs[1 + 2 * sides]
+        right_ref, left_ref, segments_ref, out_ref = refs[4:]
+        sources = [(right_ref, 0), (left_ref, 0)]
         n = segments_ref.shape[0] // 2
-        coef_ref, warmth_ref = segments_ref.at[pl.ds(0, n), :], segments_ref.at[pl.ds(n, n), :]
-    x, y, z = (lax.axis_index(a) for a in ("gx", "gy", "gz"))
-    base = layers if partner else 0
-    distances = [1, gx - 1] + list(range(2, gx - 1))
-    held = [(k, ref, at + (RAW * chunk if j < 2 else 0)) for j, (k, (ref, at)) in enumerate(zip(distances, sources))]
-    place_segments(x, gx, seg, coef_ref, warmth_ref, [(0, cells_ref, RAW * plane)] + held)
-    coef, warmth = coef_ref[...], warmth_ref[...]
+        coef, warmth = segments_ref[:n, :], segments_ref[n:, :]
     n = coef.shape[0]
     added = exact_dot(where_ref[...], coupling(coef, warmth))
     near = edge_columns(n, False)
@@ -312,41 +314,82 @@
             cells = [jnp.where(half, value[side], 0.0) for value in raw]
             for f, value in enumerate(combine(cells, beside[side][here])):
                 out_ref[f * planes + layers + side, here, :] = value
-    if partner:
-        return
+
+
+def lay_segments(x, gx, seg, chunk, own_ref, at, sources, coef_ref, warmth_ref):
+    distances = [1, gx - 1] + list(range(2, gx - 1))
+    held = [(k, ref, at + (RAW * chunk if j < 2 else 0)) for j, (k, (ref, at)) in enumerate(zip(distances, sources))]
+    place_segments(x, gx, seg, coef_ref, warmth_ref, [(0, own_ref, at)] + held)
+
+
+def strip_kernel(gx, gy, shape, seg, *refs):
+    layers, rows = shape
+    cells_ref, near_ref, line_ref, masks_ref = refs[:4]
+    received, refs = refs[4 : 4 + gx - 1], refs[4 + gx - 1 :]
+    sides = 1 if gy == 2 else 2
+    strip_refs, partner_refs, segments_ref = refs[:sides], refs[sides : 2 * sides], refs[2 * sides]
+    plane, chunk = layers * rows, rows // 4
+    x, y, z = (lax.axis_index(a) for a in ("gx", "gy", "gz"))
+    n = segments_ref.shape[0] // 2
+    coef_ref, warmth_ref = segments_ref.at[pl.ds(0, n), :], segments_ref.at[pl.ds(n, n), :]
+    lay_segments(x, gx, seg, chunk, cells_ref, RAW * plane, [(ref, 0) for ref in received], coef_ref, warmth_ref)
+    coef, warmth = coef_ref[...], warmth_ref[...]
+    coupled = coupling(coef, warmth)
+    columns = edge_columns(n, False)
+    coef, warmth = take(coef, columns), take(warmth, columns)
+    outer = [coupling(coef * masks_ref[side * n : (side + 1) * n, :], warmth) for side in range(2)]
+    strips = Strips(received[:2], [0, 0], cells_ref, RAW * plane + 2 * seg, rows, layers)
     low = lane_of(HALO) < LANES // 2
+    first = lane_of(HALO) % GROUP < HALO
     upper = lax.broadcasted_iota(jnp.int32, (HALO, LANES), 0) < HALO // 2
-    first = lane_of(HALO) % GROUP < HALO
     sent = FIELDS - 1
-    for strip_ref, partner_ref, (top, _) in zip(strip_refs, partner_refs, sides_of(gy, y)):
-        edge = pl.ds(edge_at(top, rows), HALO)
+
+    def give(ref, at, values):
+        for f, value in enumerate(values):
+            ref[at + f * HALO : at + (f + 1) * HALO, :] = value
+
+    def make(side, top):
+        start = 0 if top else rows - HALO
+        strip_ref, partner_ref = strip_refs[side], partner_refs[side]
 
         def shrink(values):
             *whole, e, g = values
-            e = jnp.where(top, e, pltpu.roll(e, HALO // 2, 0))
-            g = jnp.where(top, pltpu.roll(g, HALO // 2, 0), g)
+            if top:
+                g = pltpu.roll(g, HALO // 2, 0)
+            else:
+                e = pltpu.roll(e, HALO // 2, 0)
             return whole + [jnp.where(upper, e, g)]
 
-        def give(ref, at, values):
-            for f, value in enumerate(values):
-                ref[at + f * HALO : at + (f + 1) * HALO, :] = value
-
+        near = layers * HALO
+        added = exact_dot(near_ref[side * near : (side + 1) * near, :], coupled)
+        line = line_ref[side * 2 * HALO : (side + 1) * 2 * HALO, :]
+        beside = [exact_dot(line, part)[:HALO] for part in outer]
+        whole, stride, later, shared = partner_rows(layers)
         for i in range(layers):
-            give(strip_ref, i * sent * HALO, shrink([out_ref[f * planes + i, edge, :] for f in range(FIELDS)]))
-        outer = []
-        for f in range(FIELDS):
-            left, right = (out_ref[f * planes + layers + side, edge, :] for side in range(2))
-            outer.append(jnp.where(first, left, right))
-        outer = shrink(outer)
-        values = [jnp.where(low, outer[j], pltpu.roll(outer[j + 1], LANES // 2, 1)) for j in range(0, sent, 2)]
+            src = flip(z, layers, i)
+            raw = [
+                cells_ref[pl.ds(pl.multiple_of((f * layers + src) * rows + start, HALO), HALO), :] for f in range(RAW)
+            ]
+            values = combine(raw, added[i * HALO : (i + 1) * HALO])
+            give(strip_ref, i * sent * HALO, shrink(values))
+            pieces = [(f, m, f * stride + at) for f in range(sent - 1) for j, m, at in whole if j == i]
+            pieces += [(sent - 1 + f, m, (sent - 1) * stride + at) for f, j, m, at in later if j == i]
+            for f, m, at in pieces:
+                skip = 0 if top else HALO - m
+                partner_ref[at : at + m, :] = values[f][skip : skip + m]
+        raw = [strips.both(f, start, HALO, x, gx, False) for f in range(RAW)]
+        left, right = (combine([value[j] for value in raw], beside[j]) for j in range(2))
+        values = shrink([jnp.where(first, a, b) for a, b in zip(left, right)])
+        values = [jnp.where(low, values[j], pltpu.roll(values[j + 1], LANES // 2, 1)) for j in range(0, sent, 2)]
         give(strip_ref, layers * sent * HALO, values)
-        whole, stride, later, shared = partner_rows(layers)
-        pieces = [(f, i, m, f * stride + at) for f in range(sent - 1) for i, m, at in whole]
-        pieces += [(sent - 1 + f, i, m, (sent - 1) * stride + at) for f, i, m, at in later]
-        for f, i, m, at in pieces:
-            start = edge_at(top, rows) + jnp.where(top, 0, HALO - m)
-            partner_ref[at : at + m, :] = out_ref[f * planes + i, pl.ds(start, m), :]
         give(partner_ref, (sent - 1) * stride + shared, values)
+
+    for side, (top, _) in enumerate(sides_of(gy, y)):
+        if top is True or top is False:
+            make(side, top)
+        else:
+            pl.when(top)(functools.partial(make, side, True))
+            pl.when(jnp.logical_not(top))(functools.partial(make, side, False))
 
 
 def planes_of(count, total):
@@ -753,14 +796,16 @@
             jax.ShapeDtypeStruct((segments, layers * rows), bf16),
             jax.ShapeDtypeStruct((sides * segments, LANES), bf16),
             struct(segments, LANES),
+            jax.ShapeDtypeStruct((sides * layers * HALO, segments), bf16),
+            jax.ShapeDtypeStruct((sides * 2 * HALO, segments), bf16),
         ),
         in_specs=[VMEM] * 3,
-        out_specs=(VMEM,) * 9,
+        out_specs=(VMEM,) * 11,
         compiler_params=PARAMS,
         cost_estimate=cost(1),
         name="maps",
     )(*indices)
-    own_maps, partner_maps, (picks, picks_beside, mine) = maps[:3], maps[3:6], maps[6:]
+    own_maps, partner_maps, (picks, picks_beside, mine, near, line) = maps[:3], maps[3:6], maps[6:]
     joined = pl.pallas_call(
         join_kernel,
         out_shape=struct(sum(a.shape[0] for a in received), LANES),
@@ -770,19 +815,27 @@
         name="join",
     )(mine, *received)
     late = lax.ppermute(joined, "gz", swap)
-    filled = pl.pallas_call(
-        functools.partial(fill_kernel, False, gx, gy, shape, seg),
-        out_shape=(fields,) + (struct(strip_rows, LANES),) * sides
+    made = pl.pallas_call(
+        functools.partial(strip_kernel, gx, gy, shape, seg),
+        out_shape=(struct(strip_rows, LANES),) * sides
         + (struct(partner_strip, LANES),) * sides
         + (struct(2 * segments, LANES),),
         in_specs=[VMEM] * (4 + gx - 1),
-        out_specs=(VMEM,) * (2 + 2 * sides),
+        out_specs=(VMEM,) * (1 + 2 * sides),
+        compiler_params=PARAMS,
+        cost_estimate=cost(0.5),
+        name="strips",
+    )(own, near, line, own_maps[2], *received)
+    strips, partner_strips, held = made[:sides], made[sides : 2 * sides], made[2 * sides]
+    own_fields = pl.pallas_call(
+        functools.partial(fill_kernel, False, gx, gy, shape, seg),
+        out_shape=fields,
+        in_specs=[VMEM] * 7,
+        out_specs=VMEM,
         compiler_params=PARAMS,
         cost_estimate=cost(1.5),
         name="fill_own",
-    )(own, *own_maps, *received)
-    own_fields, held = filled[0], filled[-1]
-    strips, partner_strips = filled[1 : 1 + sides], filled[1 + sides : 1 + 2 * sides]
+    )(own, *own_maps, *received[:2], held)
     if gy == 2:
         routes = [(0, swap)]
     else:

time: 31.5 us -> 31.3 us (level)
  waiting for transfers between devices: 7.82 us -> 7.37 us
    ppermute x1, waiting for transfers between devices: 0.55 us -> 0.06 us  [local(): across.append(lax.ppermute(partner_strips[side], ('gy', 'gz'), both))]
    pallas_call x0 -> x1, Pallas kernels: none -> 0.44 us  [local(): pl.pallas_call(functools.partial(strip_kernel, gx, gy, shape, seg), out_s...]
  transfers between devices with their start and end apart: 10 -> 10, of which waited for: 4 -> 4; matrix products, arithmetic and copies ran while one was open for 0% -> 0% of each run, Pallas kernels for 20% -> 21%
where the time goes in v2:
time: 31.3 us; the launch traced here: 31.2 us
  starting transfers between devices  12.7 us (41%)
  Pallas kernels  9.77 us (31%)
  waiting for transfers between devices  7.37 us (24%)
  between operations  0.71 us (2%)
  other arithmetic  0.61 us (2%)
    ppermute x3, waiting for transfers between devices, from_distance(): return lax.ppermute(value, 'gx', [(i, (i - k) % gx) for i in range(gx)])  6.47 us
    ppermute x3, starting transfers between devices, from_distance(): return lax.ppermute(value, 'gx', [(i, (i - k) % gx) for i in range(gx)])  5.67 us
    ppermute x3, starting transfers between devices, local(): lax.ppermute(results[1 + k], 'gx', [(i, (i + k) % gx) for i in range(gx)])  4.6 us
    pallas_call x1, Pallas kernels, local(): pl.pallas_call(functools.partial(tile_kernel, gx, gy, shape), out_shape=(...  3.82 us
    pallas_call x1, Pallas kernels, local(): pl.pallas_call(functools.partial(pack_kernel, shape), out_shape=(struct(R...  1.92 us
    ppermute x1, starting transfers between devices, local(): along = [lax.ppermute(strips[side], 'gy', pairs) for side, pairs in routes]  1.5 us
    pallas_call x1, Pallas kernels, local(): pl.pallas_call(functools.partial(edge_kernel, gx, gy, shape, seg), out_sh...  1.42 us
    ppermute x3, waiting for transfers between devices, local(): lax.ppermute(results[1 + k], 'gx', [(i, (i + k) % gx) for i in range(gx)])  0.83 us
  transfers between devices with their start and end apart: 10, of which 4 were waited for; matrix products, arithmetic and copies ran while one was open for 0% of the time, Pallas kernels for 21%

profile of v2, /device:TPU:0, one launch (start us, length us, event | category | flops | bytes accessed | tf_op | source)
XLA Modules:
  0.0 31.2 jit_solution(6049281147451172992)
XLA Ops:
  0.6 1.9 %pack.1 = (f32[2944,128]{1,0:T(8,128)S(1)}, f32[224,128]{1,0:T(8,128)S(1)}, f32[224,128]{1,0:T(8,128)S(1)}, f32[64,128]{1,0:T(8,128)S(1)}, s32[4,128]{1,0:T(4,12...) custom-call(f32[512,128]{1,0:T(8,128)} %bitcast.10, f32[512,128]{1,0:T(8,128)} %bitcast.11, f32[512,128]{1,0:T(8,128)} %bitcast.12, ...), custom_call_target="tpu_custom_call" | custom-call | tf_op jit(solution)/shard_map/pack/pallas_call | solution.py:755
  2.6 0.5 %collective-permute-start.3 = (f32[2944,128]{1,0:T(8,128)S(1)}, f32[2944,128]{1,0:T(8,128)S(1)}, u32[]{:S(2)}, u32[]{:S(2)}) collective-permute-start(f32[2944,128]{1,0:T(8,128)S(1)} %get-tuple-element.31.refs_0_), channel_id=1, source_target_pairs={{0,1},{1,0},{2,3},{3,2},{4,5},{5,4},{6,7},{7,6},{8,9},{9,8},{10,11... | collective-permute-start | bytes 4521992 | tf_op jit(solution)/shard_map/ppermute | solution.py:772
  3.1 4.7 %collective-permute-start = (f32[224,128]{1,0:T(8,128)S(1)}, f32[224,128]{1,0:T(8,128)S(1)}, u32[]{:S(2)}, u32[]{:S(2)}) collective-permute-start(f32[224,128]{1,0:T(8,128)S(1)} %get-tuple-element.38), channel_id=1, source_target_pairs={{0,12},{4,0},{8,4},{12,8},{1,13},{5,1},{9,5},{13,9},{2,14},{6,2},{... | collective-permute-start | bytes 344072 | tf_op jit(solution)/shard_map/ppermute | solution.py:774
  7.7 1.0 %collective-permute-start.2 = (f32[64,128]{1,0:T(8,128)S(1)}, f32[64,128]{1,0:T(8,128)S(1)}, u32[]{:S(2)}, u32[]{:S(2)}) collective-permute-start(f32[64,128]{1,0:T(8,128)S(1)} %get-tuple-element.42), channel_id=1, source_target_pairs={{0,8},{4,12},{8,0},{12,4},{1,9},{5,13},{9,1},{13,5},{2,10},{6,14},... | collective-permute-start | bytes 98312 | tf_op jit(solution)/shard_map/ppermute | solution.py:774
  8.8 0.5 %maps.1 = (bf16[512,128]{1,0:T(8,128)(2,1)S(1)}, bf16[128,128]{1,0:T(8,128)(2,1)S(1)}, f32[256,128]{1,0:T(8,128)S(1)}, bf16[512,128]{1,0:T(8,128)(2,1)S(1)}, bf1...) custom-call(s32[4,128]{1,0:T(4,128)S(1)} %get-tuple-element.32.holde, ...), custom_call_target="tpu_custom_call" | custom-call | bytes 3000000 | tf_op jit(solution)/shard_map/maps/pallas_call | solution.py:791
  9.3 6.5 %collective-permute-done.2.refs_6_.refs_2_ = f32[64,128]{1,0:T(8,128)S(1)} collective-permute-done((f32[64,128]{1,0:T(8,128)S(1)}, f32[64,128]{1,0:T(8,128)S(1)}, u32[]{:S(2)}, u32[]{:S(2)}) %collective-permute-start.2) | collective-permute-done | bytes 32800 | tf_op jit(solution)/shard_map/ppermute | solution.py:774
  15.7 0.0 collective-permute-done.refs_4_.refs_0_
  15.7 0.0 collective-permute-done.1.refs_5_.refs_1_
  15.8 0.1 collective-permute-start.4
  15.8 0.4 %strips.1 = (f32[216,128]{1,0:T(8,128)S(1)}, f32[152,128]{1,0:T(8,128)S(1)}, f32[256,128]{1,0:T(8,128)S(1)}) custom-call(f32[2944,128]{1,0:T(8,128)S(1)} %get-tuple-element.31.refs_0_, bf16[32,128]{1,0:T(8,128)(2,1)S(1)} %get-tuple-element.40.refs_1_, bf16[16,128]{1,0:T(8,128)(2,1)S(1)} %get-tuple-element.41.refs_2_, ...), custom_call_target="tpu_custom_call" | custom-call | bytes 1500000 | tf_op jit(solution)/shard_map/strips/pallas_call | solution.py:818
  16.3 1.5 %collective-permute-start.5 = (f32[216,128]{1,0:T(8,128)S(1)}, f32[216,128]{1,0:T(8,128)S(1)}, u32[]{:S(2)}, u32[]{:S(2)}) collective-permute-start(f32[216,128]{1,0:T(8,128)S(1)} %get-tuple-element.53), channel_id=1, source_target_pairs={{0,2},{2,0},{1,3},{3,1},{4,6},{6,4},{5,7},{7,5},{8,10},{10,8},{9,1... | collective-permute-start | bytes 331784 | tf_op jit(solution)/shard_map/ppermute | solution.py:844
  17.8 0.3 %collective-permute-start.6 = (f32[152,128]{1,0:T(8,128)S(1)}, f32[152,128]{1,0:T(8,128)S(1)}, u32[]{:S(2)}, u32[]{:S(2)}) collective-permute-start(f32[152,128]{1,0:T(8,128)S(1)} %get-tuple-element.54), channel_id=1, source_target_pairs={{0,3},{1,2},{2,1},{3,0},{4,7},{5,6},{6,5},{7,4},{8,11},{9,10},{10,... | collective-permute-start | bytes 233480 | tf_op jit(solution)/shard_map/ppermute | solution.py:848
  18.1 0.5 %fill_own.1.refs_0_ = f32[42,128,128]{2,1,0:T(8,128)S(1)} custom-call(f32[2944,128]{1,0:T(8,128)S(1)} %get-tuple-element.31.refs_0_, bf16[512,128]{1,0:T(8,128)(2,1)S(1)} %get-tuple-element.35.refs_1_, bf16[128,128]{1,0:T(8,128)(2,1)S(1)} %get-tuple-element.36.refs_2_, f32[256,128]{1,0:T(8,128)S(1)} %get-tuple-element.37.refs_3_, ...), custom_call_target="tpu_custom_call" | custom-call | bytes 4500000 | tf_op jit(solution)/shard_map/fill_own/pallas_call | solution.py:830
  18.6 0.5 %fill_partner.1.refs_1_ = f32[42,128,128]{2,1,0:T(8,128)S(1)} custom-call(f32[2944,128]{1,0:T(8,128)S(1)} %collective-permute-done.3.refs_0_, bf16[512,128]{1,0:T(8,128)(2,1)S(1)} %get-tuple-element.44.refs_1_, bf16[128,128]{1,0:T(8,128)(2,1)S(1)} %get-tuple-element.45.refs_2_, f32[256,128]{1,0:T(8,128)S(1)} %get-tuple-element.46.refs_3_, ...), custom_call_target="tpu_custom_call" | custom-call | bytes 4500000 | tf_op jit(solution)/shard_map/fill_partner/pallas_call | solution.py:850
  19.1 3.8 %tile_sweeps.1 = (f32[4,128,128]{2,1,0:T(8,128)S(1)}, f32[2,128,128]{2,1,0:T(8,128)S(1)}, f32[80,8,128]{2,1,0:T(8,128)S(1)}) custom-call(f32[42,128,128]{2,1,0:T(8,128)S(1)} %fill_own.1.refs_0_, f32[42,128,128]{2,1,0:T(8,128)S(1)} %fill_partner.1.refs_1_, bf16[128,512]{1,0:T(8,128)(2,1)S(1)} %get-tuple-element.48.refs_2_), custom_call_target="tpu_custom_call" | custom-call | bytes 21000000 | tf_op jit(solution)/shard_map/tile_sweeps/pallas_call | solution.py:863
  22.9 0.1 collective-permute-done.6.refs_8_
  23.0 1.4 %edge_sweeps.1 = (f32[4,8,128]{2,1,0:T(8,128)S(1)}, f32[32,128]{1,0:T(8,128)S(1)}, f32[32,128]{1,0:T(8,128)S(1)}, f32[32,128]{1,0:T(8,128)S(1)}, f32[32,128]{1,0:T(8,128)S(1)}) custom-call(f32[42,128,128]{2,1,0:T(8,128)S(1)} %fill_own.1.refs_0_, f32[42,128,128]{2,1,0:T(8,128)S(1)} %fill_partner.1.refs_1_, bf16[128,128]{1,0:T(8,128)(2,1)S(1)} %get-tuple-element.50.refs_2_, ...), custom_call_target="tpu_custom_call" | custom-call | bytes 4500000 | tf_op jit(solution)/shard_map/edge_sweeps/pallas_call | solution.py:878
  24.4 0.5 %collective-permute-start.7 = (f32[32,128]{1,0:T(8,128)S(1)}, f32[32,128]{1,0:T(8,128)S(1)}, u32[]{:S(2)}, u32[]{:S(2)}) collective-permute-start(f32[32,128]{1,0:T(8,128)S(1)} %get-tuple-element.57), channel_id=1, source_target_pairs={{0,4},{4,8},{8,12},{12,0},{1,5},{5,9},{9,13},{13,1},{2,6},{6,10},{... | collective-permute-start | bytes 49160 | tf_op jit(solution)/shard_map/ppermute | solution.py:892
  24.9 1.3 %collective-permute-start.8 = (f32[32,128]{1,0:T(8,128)S(1)}, f32[32,128]{1,0:T(8,128)S(1)}, u32[]{:S(2)}, u32[]{:S(2)}) collective-permute-start(f32[32,128]{1,0:T(8,128)S(1)} %get-tuple-element.58), channel_id=1, source_target_pairs={{0,8},{4,12},{8,0},{12,4},{1,9},{5,13},{9,1},{13,5},{2,10},{6,14},... | collective-permute-start | bytes 49160 | tf_op jit(solution)/shard_map/ppermute | solution.py:892
  26.2 2.8 %collective-permute-start.9 = (f32[32,128]{1,0:T(8,128)S(1)}, f32[32,128]{1,0:T(8,128)S(1)}, u32[]{:S(2)}, u32[]{:S(2)}) collective-permute-start(f32[32,128]{1,0:T(8,128)S(1)} %get-tuple-element.59), channel_id=1, source_target_pairs={{0,12},{4,0},{8,4},{12,8},{1,13},{5,1},{9,5},{13,9},{2,14},{6,2},{... | collective-permute-start | bytes 49160 | tf_op jit(solution)/shard_map/ppermute | solution.py:892
  29.0 0.7 %merge.1 = f32[4,128,128]{2,1,0:T(8,128)} custom-call(f32[4,128,128]{2,1,0:T(8,128)S(1)} %get-tuple-element.49.whole_ref, f32[4,8,128]{2,1,0:T(8,128)S(1)} %get-tuple-element.55.heat_ref), custom_call_target="tpu_custom_call" | custom-call | bytes 3000000 | tf_op jit(solution)/shard_map/merge/pallas_call | solution.py:893
  29.7 0.4 %collective-permute-done.7 = f32[32,128]{1,0:T(8,128)S(1)} collective-permute-done((f32[32,128]{1,0:T(8,128)S(1)}, f32[32,128]{1,0:T(8,128)S(1)}, u32[]{:S(2)}, u32[]{:S(2)}) %collective-permute-start.7) | collective-permute-done | bytes 16416 | tf_op jit(solution)/shard_map/ppermute | solution.py:892
  30.1 0.4 %collective-permute-done.9 = f32[32,128]{1,0:T(8,128)S(1)} collective-permute-done((f32[32,128]{1,0:T(8,128)S(1)}, f32[32,128]{1,0:T(8,128)S(1)}, u32[]{:S(2)}, u32[]{:S(2)}) %collective-permute-start.9) | collective-permute-done | bytes 16416 | tf_op jit(solution)/shard_map/ppermute | solution.py:892
  30.6 0.6 %add_bitcast_fusion = f32[1,32,128]{2,1,0:T(8,128)} fusion(f32[32,128]{1,0:T(8,128)S(1)} %collective-permute-done.9, f32[32,128]{1,0:T(8,128)S(1)} %collective-permute-done.8, f32[32,128]{1,0:T(8,128)S(1)} %get-tuple-element.56, f32[32,128]{1,0:T(8,128)S(1)} %collective-permute-done.7), kind=kLoop, calls=%fused_computation | loop fusion | flops 12288 | bytes 81920 | tf_op jit(solution)/shard_map/broadcast_in_dim | solution.py:904
  (6 shorter events, 0.0 us)
Async XLA Ops:
  2.6 16.0 %collective-permute-start.3 = (f32[2944,128]{1,0:T(8,128)S(1)}, f32[2944,128]{1,0:T(8,128)S(1)}, u32[]{:S(2)}, u32[]{:S(2)}) collective-permute-start(f32[2944,128]{1,0:T(8,128)S(1)} %get-tuple-element.31.refs_0_), channel_id=1, source_target_pairs={{0,1},{1,0},{2,3},{3,2},{4,5},{5,4},{6,7},{7,6},{8,9},{9,8},{10,11... | collective-permute-start | bytes 4521992 | tf_op jit(solution)/shard_map/ppermute | solution.py:772
  3.1 12.6 %collective-permute-start = (f32[224,128]{1,0:T(8,128)S(1)}, f32[224,128]{1,0:T(8,128)S(1)}, u32[]{:S(2)}, u32[]{:S(2)}) collective-permute-start(f32[224,128]{1,0:T(8,128)S(1)} %get-tuple-element.38), channel_id=1, source_target_pairs={{0,12},{4,0},{8,4},{12,8},{1,13},{5,1},{9,5},{13,9},{2,14},{6,2},{... | collective-permute-start | bytes 344072 | tf_op jit(solution)/shard_map/ppermute | solution.py:774
  7.7 8.0 %collective-permute-start.1 = (f32[224,128]{1,0:T(8,128)S(1)}, f32[224,128]{1,0:T(8,128)S(1)}, u32[]{:S(2)}, u32[]{:S(2)}) collective-permute-start(f32[224,128]{1,0:T(8,128)S(1)} %get-tuple-element.39), channel_id=1, source_target_pairs={{0,4},{4,8},{8,12},{12,0},{1,5},{5,9},{9,13},{13,1},{2,6},{6,10},{... | collective-permute-start | bytes 344072 | tf_op jit(solution)/shard_map/ppermute | solution.py:774
  7.7 8.0 %collective-permute-start.2 = (f32[64,128]{1,0:T(8,128)S(1)}, f32[64,128]{1,0:T(8,128)S(1)}, u32[]{:S(2)}, u32[]{:S(2)}) collective-permute-start(f32[64,128]{1,0:T(8,128)S(1)} %get-tuple-element.42), channel_id=1, source_target_pairs={{0,8},{4,12},{8,0},{12,4},{1,9},{5,13},{9,1},{13,5},{2,10},{6,14},... | collective-permute-start | bytes 98312 | tf_op jit(solution)/shard_map/ppermute | solution.py:774
  15.8 2.8 %collective-permute-start.4 = (f32[512,128]{1,0:T(8,128)S(1)}, f32[512,128]{1,0:T(8,128)S(1)}, u32[]{:S(2)}, u32[]{:S(2)}) collective-permute-start(f32[512,128]{1,0:T(8,128)S(1)} %join.1), channel_id=1, source_target_pairs={{0,1},{1,0},{2,3},{3,2},{4,5},{5,4},{6,7},{7,6},{8,9},{9,8},{10,11... | collective-permute-start | bytes 786440 | tf_op jit(solution)/shard_map/ppermute | solution.py:817
  16.3 6.7 %collective-permute-start.5 = (f32[216,128]{1,0:T(8,128)S(1)}, f32[216,128]{1,0:T(8,128)S(1)}, u32[]{:S(2)}, u32[]{:S(2)}) collective-permute-start(f32[216,128]{1,0:T(8,128)S(1)} %get-tuple-element.53), channel_id=1, source_target_pairs={{0,2},{2,0},{1,3},{3,1},{4,6},{6,4},{5,7},{7,5},{8,10},{10,8},{9,1... | collective-permute-start | bytes 331784 | tf_op jit(solution)/shard_map/ppermute | solution.py:844
  17.8 5.2 %collective-permute-start.6 = (f32[152,128]{1,0:T(8,128)S(1)}, f32[152,128]{1,0:T(8,128)S(1)}, u32[]{:S(2)}, u32[]{:S(2)}) collective-permute-start(f32[152,128]{1,0:T(8,128)S(1)} %get-tuple-element.54), channel_id=1, source_target_pairs={{0,3},{1,2},{2,1},{3,0},{4,7},{5,6},{6,5},{7,4},{8,11},{9,10},{10,... | collective-permute-start | bytes 233480 | tf_op jit(solution)/shard_map/ppermute | solution.py:848
  24.4 5.7 %collective-permute-start.7 = (f32[32,128]{1,0:T(8,128)S(1)}, f32[32,128]{1,0:T(8,128)S(1)}, u32[]{:S(2)}, u32[]{:S(2)}) collective-permute-start(f32[32,128]{1,0:T(8,128)S(1)} %get-tuple-element.57), channel_id=1, source_target_pairs={{0,4},{4,8},{8,12},{12,0},{1,5},{5,9},{9,13},{13,1},{2,6},{6,10},{... | collective-permute-start | bytes 49160 | tf_op jit(solution)/shard_map/ppermute | solution.py:892
  24.9 5.3 %collective-permute-start.8 = (f32[32,128]{1,0:T(8,128)S(1)}, f32[32,128]{1,0:T(8,128)S(1)}, u32[]{:S(2)}, u32[]{:S(2)}) collective-permute-start(f32[32,128]{1,0:T(8,128)S(1)} %get-tuple-element.58), channel_id=1, source_target_pairs={{0,8},{4,12},{8,0},{12,4},{1,9},{5,13},{9,1},{13,5},{2,10},{6,14},... | collective-permute-start | bytes 49160 | tf_op jit(solution)/shard_map/ppermute | solution.py:892
  26.2 4.4 %collective-permute-start.9 = (f32[32,128]{1,0:T(8,128)S(1)}, f32[32,128]{1,0:T(8,128)S(1)}, u32[]{:S(2)}, u32[]{:S(2)}) collective-permute-start(f32[32,128]{1,0:T(8,128)S(1)} %get-tuple-element.59), channel_id=1, source_target_pairs={{0,12},{4,0},{8,4},{12,8},{1,13},{5,1},{9,5},{13,9},{2,14},{6,2},{... | collective-permute-start | bytes 49160 | tf_op jit(solution)/shard_map/ppermute | solution.py:892

commit v3 on v2

--- a/solution.py
+++ b/solution.py
@@ -511,18 +511,7 @@
 
 def two_steps(layers, sweep_all, between, after):
     for step in range(STEPS):
-        whole = [n for n in range(step * ITERS, (step + 1) * ITERS) if needed(layers, n) == 2 * layers]
-        pairs = len(whole) // 2
-
-        def pair(k, carry):
-            n = step * ITERS + 2 * k
-            sweep_all(n, 0, 2 * layers)
-            sweep_all(n + 1, 1, 2 * layers)
-            return carry
-
-        if pairs:
-            lax.fori_loop(0, pairs, pair, 0)
-        for n in range(step * ITERS + 2 * pairs, (step + 1) * ITERS):
+        for n in range(step * ITERS, (step + 1) * ITERS):
             sweep_all(n, n % 2, needed(layers, n))
         after(step)
         if step < STEPS - 1:

time: 31.3 us -> 31.1 us (level)
  Pallas kernels: 9.77 us -> 9.44 us
  transfers between devices with their start and end apart: 10 -> 10, of which waited for: 4 -> 4; matrix products, arithmetic and copies ran while one was open for 0% -> 0% of each run, Pallas kernels for 21% -> 20%
where the time goes in v3:
time: 31.1 us; the launch traced here: 31 us
  starting transfers between devices  12.7 us (41%)
  Pallas kernels  9.44 us (30%)
  waiting for transfers between devices  7.51 us (24%)
  between operations  0.71 us (2%)
  other arithmetic  0.61 us (2%)
    ppermute x3, waiting for transfers between devices, from_distance(): return lax.ppermute(value, 'gx', [(i, (i - k) % gx) for i in range(gx)])  6.47 us
    ppermute x3, starting transfers between devices, from_distance(): return lax.ppermute(value, 'gx', [(i, (i - k) % gx) for i in range(gx)])  5.67 us
    ppermute x3, starting transfers between devices, local(): lax.ppermute(results[1 + k], 'gx', [(i, (i + k) % gx) for i in range(gx)])  4.6 us
    pallas_call x1, Pallas kernels, local(): pl.pallas_call(functools.partial(tile_kernel, gx, gy, shape), out_shape=(...  3.68 us
    pallas_call x1, Pallas kernels, local(): pl.pallas_call(functools.partial(pack_kernel, shape), out_shape=(struct(R...  1.92 us
    ppermute x1, starting transfers between devices, local(): along = [lax.ppermute(strips[side], 'gy', pairs) for side, pairs in routes]  1.5 us
    pallas_call x1, Pallas kernels, local(): pl.pallas_call(functools.partial(edge_kernel, gx, gy, shape, seg), out_sh...  1.23 us
    ppermute x3, waiting for transfers between devices, local(): lax.ppermute(results[1 + k], 'gx', [(i, (i + k) % gx) for i in range(gx)])  0.83 us
  transfers between devices with their start and end apart: 10, of which 4 were waited for; matrix products, arithmetic and copies ran while one was open for 0% of the time, Pallas kernels for 20%

profile of v3, /device:TPU:0, one launch (start us, length us, event | category | flops | bytes accessed | tf_op | source)
XLA Modules:
  0.0 31.0 jit_solution(11452687553959485868)
XLA Ops:
  0.6 1.9 %pack.1 = (f32[2944,128]{1,0:T(8,128)S(1)}, f32[224,128]{1,0:T(8,128)S(1)}, f32[224,128]{1,0:T(8,128)S(1)}, f32[64,128]{1,0:T(8,128)S(1)}, s32[4,128]{1,0:T(4,12...) custom-call(f32[512,128]{1,0:T(8,128)} %bitcast.10, f32[512,128]{1,0:T(8,128)} %bitcast.11, f32[512,128]{1,0:T(8,128)} %bitcast.12, ...), custom_call_target="tpu_custom_call" | custom-call | tf_op jit(solution)/shard_map/pack/pallas_call | solution.py:744
  2.6 0.5 %collective-permute-start.3 = (f32[2944,128]{1,0:T(8,128)S(1)}, f32[2944,128]{1,0:T(8,128)S(1)}, u32[]{:S(2)}, u32[]{:S(2)}) collective-permute-start(f32[2944,128]{1,0:T(8,128)S(1)} %get-tuple-element.31.refs_0_), channel_id=1, source_target_pairs={{0,1},{1,0},{2,3},{3,2},{4,5},{5,4},{6,7},{7,6},{8,9},{9,8},{10,11... | collective-permute-start | bytes 4521992 | tf_op jit(solution)/shard_map/ppermute | solution.py:761
  3.1 4.7 %collective-permute-start = (f32[224,128]{1,0:T(8,128)S(1)}, f32[224,128]{1,0:T(8,128)S(1)}, u32[]{:S(2)}, u32[]{:S(2)}) collective-permute-start(f32[224,128]{1,0:T(8,128)S(1)} %get-tuple-element.38), channel_id=1, source_target_pairs={{0,12},{4,0},{8,4},{12,8},{1,13},{5,1},{9,5},{13,9},{2,14},{6,2},{... | collective-permute-start | bytes 344072 | tf_op jit(solution)/shard_map/ppermute | solution.py:763
  7.7 0.0 collective-permute-start.1
  7.7 1.0 %collective-permute-start.2 = (f32[64,128]{1,0:T(8,128)S(1)}, f32[64,128]{1,0:T(8,128)S(1)}, u32[]{:S(2)}, u32[]{:S(2)}) collective-permute-start(f32[64,128]{1,0:T(8,128)S(1)} %get-tuple-element.42), channel_id=1, source_target_pairs={{0,8},{4,12},{8,0},{12,4},{1,9},{5,13},{9,1},{13,5},{2,10},{6,14},... | collective-permute-start | bytes 98312 | tf_op jit(solution)/shard_map/ppermute | solution.py:763
  8.8 0.5 %maps.1 = (bf16[512,128]{1,0:T(8,128)(2,1)S(1)}, bf16[128,128]{1,0:T(8,128)(2,1)S(1)}, f32[256,128]{1,0:T(8,128)S(1)}, bf16[512,128]{1,0:T(8,128)(2,1)S(1)}, bf1...) custom-call(s32[4,128]{1,0:T(4,128)S(1)} %get-tuple-element.32.holde, ...), custom_call_target="tpu_custom_call" | custom-call | bytes 3000000 | tf_op jit(solution)/shard_map/maps/pallas_call | solution.py:780
  9.3 6.5 %collective-permute-done.2.refs_6_.refs_2_ = f32[64,128]{1,0:T(8,128)S(1)} collective-permute-done((f32[64,128]{1,0:T(8,128)S(1)}, f32[64,128]{1,0:T(8,128)S(1)}, u32[]{:S(2)}, u32[]{:S(2)}) %collective-permute-start.2) | collective-permute-done | bytes 32800 | tf_op jit(solution)/shard_map/ppermute | solution.py:763
  15.8 0.1 collective-permute-start.4
  15.8 0.4 %strips.1 = (f32[216,128]{1,0:T(8,128)S(1)}, f32[152,128]{1,0:T(8,128)S(1)}, f32[256,128]{1,0:T(8,128)S(1)}) custom-call(f32[2944,128]{1,0:T(8,128)S(1)} %get-tuple-element.31.refs_0_, bf16[32,128]{1,0:T(8,128)(2,1)S(1)} %get-tuple-element.40.refs_1_, bf16[16,128]{1,0:T(8,128)(2,1)S(1)} %get-tuple-element.41.refs_2_, ...), custom_call_target="tpu_custom_call" | custom-call | bytes 1500000 | tf_op jit(solution)/shard_map/strips/pallas_call | solution.py:807
  16.3 1.5 %collective-permute-start.5 = (f32[216,128]{1,0:T(8,128)S(1)}, f32[216,128]{1,0:T(8,128)S(1)}, u32[]{:S(2)}, u32[]{:S(2)}) collective-permute-start(f32[216,128]{1,0:T(8,128)S(1)} %get-tuple-element.53), channel_id=1, source_target_pairs={{0,2},{2,0},{1,3},{3,1},{4,6},{6,4},{5,7},{7,5},{8,10},{10,8},{9,1... | collective-permute-start | bytes 331784 | tf_op jit(solution)/shard_map/ppermute | solution.py:833
  17.8 0.3 %collective-permute-start.6 = (f32[152,128]{1,0:T(8,128)S(1)}, f32[152,128]{1,0:T(8,128)S(1)}, u32[]{:S(2)}, u32[]{:S(2)}) collective-permute-start(f32[152,128]{1,0:T(8,128)S(1)} %get-tuple-element.54), channel_id=1, source_target_pairs={{0,3},{1,2},{2,1},{3,0},{4,7},{5,6},{6,5},{7,4},{8,11},{9,10},{10,... | collective-permute-start | bytes 233480 | tf_op jit(solution)/shard_map/ppermute | solution.py:837
  18.1 0.5 %fill_own.1.refs_0_ = f32[42,128,128]{2,1,0:T(8,128)S(1)} custom-call(f32[2944,128]{1,0:T(8,128)S(1)} %get-tuple-element.31.refs_0_, bf16[512,128]{1,0:T(8,128)(2,1)S(1)} %get-tuple-element.35.refs_1_, bf16[128,128]{1,0:T(8,128)(2,1)S(1)} %get-tuple-element.36.refs_2_, f32[256,128]{1,0:T(8,128)S(1)} %get-tuple-element.37.refs_3_, ...), custom_call_target="tpu_custom_call" | custom-call | bytes 4500000 | tf_op jit(solution)/shard_map/fill_own/pallas_call | solution.py:819
  18.6 0.0 collective-permute-done.3.refs_0_
  18.6 0.5 %fill_partner.1.refs_1_ = f32[42,128,128]{2,1,0:T(8,128)S(1)} custom-call(f32[2944,128]{1,0:T(8,128)S(1)} %collective-permute-done.3.refs_0_, bf16[512,128]{1,0:T(8,128)(2,1)S(1)} %get-tuple-element.44.refs_1_, bf16[128,128]{1,0:T(8,128)(2,1)S(1)} %get-tuple-element.45.refs_2_, f32[256,128]{1,0:T(8,128)S(1)} %get-tuple-element.46.refs_3_, ...), custom_call_target="tpu_custom_call" | custom-call | bytes 4500000 | tf_op jit(solution)/shard_map/fill_partner/pallas_call | solution.py:839
  19.1 3.7 %tile_sweeps.1 = (f32[4,128,128]{2,1,0:T(8,128)S(1)}, f32[2,128,128]{2,1,0:T(8,128)S(1)}, f32[80,8,128]{2,1,0:T(8,128)S(1)}) custom-call(f32[42,128,128]{2,1,0:T(8,128)S(1)} %fill_own.1.refs_0_, f32[42,128,128]{2,1,0:T(8,128)S(1)} %fill_partner.1.refs_1_, bf16[128,512]{1,0:T(8,128)(2,1)S(1)} %get-tuple-element.48.refs_2_), custom_call_target="tpu_custom_call" | custom-call | bytes 21000000 | tf_op jit(solution)/shard_map/tile_sweeps/pallas_call | solution.py:852
  22.8 0.2 collective-permute-done.6.refs_8_
  23.0 1.2 %edge_sweeps.1 = (f32[4,8,128]{2,1,0:T(8,128)S(1)}, f32[32,128]{1,0:T(8,128)S(1)}, f32[32,128]{1,0:T(8,128)S(1)}, f32[32,128]{1,0:T(8,128)S(1)}, f32[32,128]{1,0:T(8,128)S(1)}) custom-call(f32[42,128,128]{2,1,0:T(8,128)S(1)} %fill_own.1.refs_0_, f32[42,128,128]{2,1,0:T(8,128)S(1)} %fill_partner.1.refs_1_, bf16[128,128]{1,0:T(8,128)(2,1)S(1)} %get-tuple-element.50.refs_2_, ...), custom_call_target="tpu_custom_call" | custom-call | bytes 4500000 | tf_op jit(solution)/shard_map/edge_sweeps/pallas_call | solution.py:867
  24.2 0.5 %collective-permute-start.7 = (f32[32,128]{1,0:T(8,128)S(1)}, f32[32,128]{1,0:T(8,128)S(1)}, u32[]{:S(2)}, u32[]{:S(2)}) collective-permute-start(f32[32,128]{1,0:T(8,128)S(1)} %get-tuple-element.57), channel_id=1, source_target_pairs={{0,4},{4,8},{8,12},{12,0},{1,5},{5,9},{9,13},{13,1},{2,6},{6,10},{... | collective-permute-start | bytes 49160 | tf_op jit(solution)/shard_map/ppermute | solution.py:881
  24.7 1.3 %collective-permute-start.8 = (f32[32,128]{1,0:T(8,128)S(1)}, f32[32,128]{1,0:T(8,128)S(1)}, u32[]{:S(2)}, u32[]{:S(2)}) collective-permute-start(f32[32,128]{1,0:T(8,128)S(1)} %get-tuple-element.58), channel_id=1, source_target_pairs={{0,8},{4,12},{8,0},{12,4},{1,9},{5,13},{9,1},{13,5},{2,10},{6,14},... | collective-permute-start | bytes 49160 | tf_op jit(solution)/shard_map/ppermute | solution.py:881
  26.0 2.8 %collective-permute-start.9 = (f32[32,128]{1,0:T(8,128)S(1)}, f32[32,128]{1,0:T(8,128)S(1)}, u32[]{:S(2)}, u32[]{:S(2)}) collective-permute-start(f32[32,128]{1,0:T(8,128)S(1)} %get-tuple-element.59), channel_id=1, source_target_pairs={{0,12},{4,0},{8,4},{12,8},{1,13},{5,1},{9,5},{13,9},{2,14},{6,2},{... | collective-permute-start | bytes 49160 | tf_op jit(solution)/shard_map/ppermute | solution.py:881
  28.8 0.7 %merge.1 = f32[4,128,128]{2,1,0:T(8,128)} custom-call(f32[4,128,128]{2,1,0:T(8,128)S(1)} %get-tuple-element.49.whole_ref, f32[4,8,128]{2,1,0:T(8,128)S(1)} %get-tuple-element.55.heat_ref), custom_call_target="tpu_custom_call" | custom-call | bytes 3000000 | tf_op jit(solution)/shard_map/merge/pallas_call | solution.py:882
  29.5 0.3 %collective-permute-done.7 = f32[32,128]{1,0:T(8,128)S(1)} collective-permute-done((f32[32,128]{1,0:T(8,128)S(1)}, f32[32,128]{1,0:T(8,128)S(1)}, u32[]{:S(2)}, u32[]{:S(2)}) %collective-permute-start.7) | collective-permute-done | bytes 16416 | tf_op jit(solution)/shard_map/ppermute | solution.py:881
  29.9 0.5 %collective-permute-done.9 = f32[32,128]{1,0:T(8,128)S(1)} collective-permute-done((f32[32,128]{1,0:T(8,128)S(1)}, f32[32,128]{1,0:T(8,128)S(1)}, u32[]{:S(2)}, u32[]{:S(2)}) %collective-permute-start.9) | collective-permute-done | bytes 16416 | tf_op jit(solution)/shard_map/ppermute | solution.py:881
  30.4 0.6 %add_bitcast_fusion = f32[1,32,128]{2,1,0:T(8,128)} fusion(f32[32,128]{1,0:T(8,128)S(1)} %collective-permute-done.9, f32[32,128]{1,0:T(8,128)S(1)} %collective-permute-done.8, f32[32,128]{1,0:T(8,128)S(1)} %get-tuple-element.56, f32[32,128]{1,0:T(8,128)S(1)} %collective-permute-done.7), kind=kLoop, calls=%fused_computation | loop fusion | flops 12288 | bytes 81920 | tf_op jit(solution)/shard_map/broadcast_in_dim | solution.py:893
  (6 shorter events, 0.0 us)
Async XLA Ops:
  2.6 16.0 %collective-permute-start.3 = (f32[2944,128]{1,0:T(8,128)S(1)}, f32[2944,128]{1,0:T(8,128)S(1)}, u32[]{:S(2)}, u32[]{:S(2)}) collective-permute-start(f32[2944,128]{1,0:T(8,128)S(1)} %get-tuple-element.31.refs_0_), channel_id=1, source_target_pairs={{0,1},{1,0},{2,3},{3,2},{4,5},{5,4},{6,7},{7,6},{8,9},{9,8},{10,11... | collective-permute-start | bytes 4521992 | tf_op jit(solution)/shard_map/ppermute | solution.py:761
  3.1 12.6 %collective-permute-start = (f32[224,128]{1,0:T(8,128)S(1)}, f32[224,128]{1,0:T(8,128)S(1)}, u32[]{:S(2)}, u32[]{:S(2)}) collective-permute-start(f32[224,128]{1,0:T(8,128)S(1)} %get-tuple-element.38), channel_id=1, source_target_pairs={{0,12},{4,0},{8,4},{12,8},{1,13},{5,1},{9,5},{13,9},{2,14},{6,2},{... | collective-permute-start | bytes 344072 | tf_op jit(solution)/shard_map/ppermute | solution.py:763
  7.7 8.0 %collective-permute-start.1 = (f32[224,128]{1,0:T(8,128)S(1)}, f32[224,128]{1,0:T(8,128)S(1)}, u32[]{:S(2)}, u32[]{:S(2)}) collective-permute-start(f32[224,128]{1,0:T(8,128)S(1)} %get-tuple-element.39), channel_id=1, source_target_pairs={{0,4},{4,8},{8,12},{12,0},{1,5},{5,9},{9,13},{13,1},{2,6},{6,10},{... | collective-permute-start | bytes 344072 | tf_op jit(solution)/shard_map/ppermute | solution.py:763
  7.7 8.0 %collective-permute-start.2 = (f32[64,128]{1,0:T(8,128)S(1)}, f32[64,128]{1,0:T(8,128)S(1)}, u32[]{:S(2)}, u32[]{:S(2)}) collective-permute-start(f32[64,128]{1,0:T(8,128)S(1)} %get-tuple-element.42), channel_id=1, source_target_pairs={{0,8},{4,12},{8,0},{12,4},{1,9},{5,13},{9,1},{13,5},{2,10},{6,14},... | collective-permute-start | bytes 98312 | tf_op jit(solution)/shard_map/ppermute | solution.py:763
  15.8 2.8 %collective-permute-start.4 = (f32[512,128]{1,0:T(8,128)S(1)}, f32[512,128]{1,0:T(8,128)S(1)}, u32[]{:S(2)}, u32[]{:S(2)}) collective-permute-start(f32[512,128]{1,0:T(8,128)S(1)} %join.1), channel_id=1, source_target_pairs={{0,1},{1,0},{2,3},{3,2},{4,5},{5,4},{6,7},{7,6},{8,9},{9,8},{10,11... | collective-permute-start | bytes 786440 | tf_op jit(solution)/shard_map/ppermute | solution.py:806
  16.3 6.7 %collective-permute-start.5 = (f32[216,128]{1,0:T(8,128)S(1)}, f32[216,128]{1,0:T(8,128)S(1)}, u32[]{:S(2)}, u32[]{:S(2)}) collective-permute-start(f32[216,128]{1,0:T(8,128)S(1)} %get-tuple-element.53), channel_id=1, source_target_pairs={{0,2},{2,0},{1,3},{3,1},{4,6},{6,4},{5,7},{7,5},{8,10},{10,8},{9,1... | collective-permute-start | bytes 331784 | tf_op jit(solution)/shard_map/ppermute | solution.py:833
  17.8 5.2 %collective-permute-start.6 = (f32[152,128]{1,0:T(8,128)S(1)}, f32[152,128]{1,0:T(8,128)S(1)}, u32[]{:S(2)}, u32[]{:S(2)}) collective-permute-start(f32[152,128]{1,0:T(8,128)S(1)} %get-tuple-element.54), channel_id=1, source_target_pairs={{0,3},{1,2},{2,1},{3,0},{4,7},{5,6},{6,5},{7,4},{8,11},{9,10},{10,... | collective-permute-start | bytes 233480 | tf_op jit(solution)/shard_map/ppermute | solution.py:837
  24.2 5.6 %collective-permute-start.7 = (f32[32,128]{1,0:T(8,128)S(1)}, f32[32,128]{1,0:T(8,128)S(1)}, u32[]{:S(2)}, u32[]{:S(2)}) collective-permute-start(f32[32,128]{1,0:T(8,128)S(1)} %get-tuple-element.57), channel_id=1, source_target_pairs={{0,4},{4,8},{8,12},{12,0},{1,5},{5,9},{9,13},{13,1},{2,6},{6,10},{... | collective-permute-start | bytes 49160 | tf_op jit(solution)/shard_map/ppermute | solution.py:881
  24.7 5.2 %collective-permute-start.8 = (f32[32,128]{1,0:T(8,128)S(1)}, f32[32,128]{1,0:T(8,128)S(1)}, u32[]{:S(2)}, u32[]{:S(2)}) collective-permute-start(f32[32,128]{1,0:T(8,128)S(1)} %get-tuple-element.58), channel_id=1, source_target_pairs={{0,8},{4,12},{8,0},{12,4},{1,9},{5,13},{9,1},{13,5},{2,10},{6,14},... | collective-permute-start | bytes 49160 | tf_op jit(solution)/shard_map/ppermute | solution.py:881
  26.0 4.4 %collective-permute-start.9 = (f32[32,128]{1,0:T(8,128)S(1)}, f32[32,128]{1,0:T(8,128)S(1)}, u32[]{:S(2)}, u32[]{:S(2)}) collective-permute-start(f32[32,128]{1,0:T(8,128)S(1)} %get-tuple-element.59), channel_id=1, source_target_pairs={{0,12},{4,0},{8,4},{12,8},{1,13},{5,1},{9,5},{13,9},{2,14},{6,2},{... | collective-permute-start | bytes 49160 | tf_op jit(solution)/shard_map/ppermute | solution.py:881

commit v4 on v3

--- a/solution.py
+++ b/solution.py
@@ -337,7 +337,8 @@
     coupled = coupling(coef, warmth)
     columns = edge_columns(n, False)
     coef, warmth = take(coef, columns), take(warmth, columns)
-    outer = [coupling(coef * masks_ref[side * n : (side + 1) * n, :], warmth) for side in range(2)]
+    mask = jnp.where(lane_of(n) % GROUP < HALO, masks_ref[:n, :], masks_ref[n:, :])
+    outer = coupling(coef * mask, warmth)
     strips = Strips(received[:2], [0, 0], cells_ref, RAW * plane + 2 * seg, rows, layers)
     low = lane_of(HALO) < LANES // 2
     first = lane_of(HALO) % GROUP < HALO
@@ -363,7 +364,7 @@
         near = layers * HALO
         added = exact_dot(near_ref[side * near : (side + 1) * near, :], coupled)
         line = line_ref[side * 2 * HALO : (side + 1) * 2 * HALO, :]
-        beside = [exact_dot(line, part)[:HALO] for part in outer]
+        beside = exact_dot(line, outer)[:HALO]
         whole, stride, later, shared = partner_rows(layers)
         for i in range(layers):
             src = flip(z, layers, i)
@@ -377,9 +378,8 @@
             for f, m, at in pieces:
                 skip = 0 if top else HALO - m
                 partner_ref[at : at + m, :] = values[f][skip : skip + m]
-        raw = [strips.both(f, start, HALO, x, gx, False) for f in range(RAW)]
-        left, right = (combine([value[j] for value in raw], beside[j]) for j in range(2))
-        values = shrink([jnp.where(first, a, b) for a, b in zip(left, right)])
+        raw = [jnp.where(first, *strips.both(f, start, HALO, x, gx, False)) for f in range(RAW)]
+        values = shrink(combine(raw, beside))
         values = [jnp.where(low, values[j], pltpu.roll(values[j + 1], LANES // 2, 1)) for j in range(0, sent, 2)]
         give(strip_ref, layers * sent * HALO, values)
         give(partner_ref, (sent - 1) * stride + shared, values)

time: 31.1 us -> 31.1 us (level)
  no operation moved by 1% of the time
where the time goes in v4:
time: 31.1 us; the launch traced here: 30.9 us
  starting transfers between devices  12.7 us (41%)
  Pallas kernels  9.41 us (30%)
  waiting for transfers between devices  7.5 us (24%)
  between operations  0.71 us (2%)
  other arithmetic  0.61 us (2%)
    ppermute x3, waiting for transfers between devices, from_distance(): return lax.ppermute(value, 'gx', [(i, (i - k) % gx) for i in range(gx)])  6.47 us
    ppermute x3, starting transfers between devices, from_distance(): return lax.ppermute(value, 'gx', [(i, (i - k) % gx) for i in range(gx)])  5.67 us
    ppermute x3, starting transfers between devices, local(): lax.ppermute(results[1 + k], 'gx', [(i, (i + k) % gx) for i in range(gx)])  4.6 us
    pallas_call x1, Pallas kernels, local(): pl.pallas_call(functools.partial(tile_kernel, gx, gy, shape), out_shape=(...  3.67 us
    pallas_call x1, Pallas kernels, local(): pl.pallas_call(functools.partial(pack_kernel, shape), out_shape=(struct(R...  1.92 us
    ppermute x1, starting transfers between devices, local(): along = [lax.ppermute(strips[side], 'gy', pairs) for side, pairs in routes]  1.49 us
    pallas_call x1, Pallas kernels, local(): pl.pallas_call(functools.partial(edge_kernel, gx, gy, shape, seg), out_sh...  1.23 us
    ppermute x3, waiting for transfers between devices, local(): lax.ppermute(results[1 + k], 'gx', [(i, (i + k) % gx) for i in range(gx)])  0.83 us
  transfers between devices with their start and end apart: 10, of which 4 were waited for; matrix products, arithmetic and copies ran while one was open for 0% of the time, Pallas kernels for 20%

profile of v4, /device:TPU:0, one launch (start us, length us, event | category | flops | bytes accessed | tf_op | source)
XLA Modules:
  0.0 30.9 jit_solution(4496373329137265917)
XLA Ops:
  0.6 1.9 %pack.1 = (f32[2944,128]{1,0:T(8,128)S(1)}, f32[224,128]{1,0:T(8,128)S(1)}, f32[224,128]{1,0:T(8,128)S(1)}, f32[64,128]{1,0:T(8,128)S(1)}, s32[4,128]{1,0:T(4,12...) custom-call(f32[512,128]{1,0:T(8,128)} %bitcast.10, f32[512,128]{1,0:T(8,128)} %bitcast.11, f32[512,128]{1,0:T(8,128)} %bitcast.12, ...), custom_call_target="tpu_custom_call" | custom-call | tf_op jit(solution)/shard_map/pack/pallas_call | solution.py:744
  2.6 0.5 %collective-permute-start.3 = (f32[2944,128]{1,0:T(8,128)S(1)}, f32[2944,128]{1,0:T(8,128)S(1)}, u32[]{:S(2)}, u32[]{:S(2)}) collective-permute-start(f32[2944,128]{1,0:T(8,128)S(1)} %get-tuple-element.31.refs_0_), channel_id=1, source_target_pairs={{0,1},{1,0},{2,3},{3,2},{4,5},{5,4},{6,7},{7,6},{8,9},{9,8},{10,11... | collective-permute-start | bytes 4521992 | tf_op jit(solution)/shard_map/ppermute | solution.py:761
  3.1 4.7 %collective-permute-start = (f32[224,128]{1,0:T(8,128)S(1)}, f32[224,128]{1,0:T(8,128)S(1)}, u32[]{:S(2)}, u32[]{:S(2)}) collective-permute-start(f32[224,128]{1,0:T(8,128)S(1)} %get-tuple-element.38), channel_id=1, source_target_pairs={{0,12},{4,0},{8,4},{12,8},{1,13},{5,1},{9,5},{13,9},{2,14},{6,2},{... | collective-permute-start | bytes 344072 | tf_op jit(solution)/shard_map/ppermute | solution.py:763
  7.7 0.0 collective-permute-start.1
  7.7 1.0 %collective-permute-start.2 = (f32[64,128]{1,0:T(8,128)S(1)}, f32[64,128]{1,0:T(8,128)S(1)}, u32[]{:S(2)}, u32[]{:S(2)}) collective-permute-start(f32[64,128]{1,0:T(8,128)S(1)} %get-tuple-element.42), channel_id=1, source_target_pairs={{0,8},{4,12},{8,0},{12,4},{1,9},{5,13},{9,1},{13,5},{2,10},{6,14},... | collective-permute-start | bytes 98312 | tf_op jit(solution)/shard_map/ppermute | solution.py:763
  8.8 0.5 %maps.1 = (bf16[512,128]{1,0:T(8,128)(2,1)S(1)}, bf16[128,128]{1,0:T(8,128)(2,1)S(1)}, f32[256,128]{1,0:T(8,128)S(1)}, bf16[512,128]{1,0:T(8,128)(2,1)S(1)}, bf1...) custom-call(s32[4,128]{1,0:T(4,128)S(1)} %get-tuple-element.32.holde, ...), custom_call_target="tpu_custom_call" | custom-call | bytes 3000000 | tf_op jit(solution)/shard_map/maps/pallas_call | solution.py:780
  9.3 6.5 %collective-permute-done.2.refs_6_.refs_2_ = f32[64,128]{1,0:T(8,128)S(1)} collective-permute-done((f32[64,128]{1,0:T(8,128)S(1)}, f32[64,128]{1,0:T(8,128)S(1)}, u32[]{:S(2)}, u32[]{:S(2)}) %collective-permute-start.2) | collective-permute-done | bytes 32800 | tf_op jit(solution)/shard_map/ppermute | solution.py:763
  15.7 0.0 collective-permute-done.refs_4_.refs_0_
  15.8 0.1 collective-permute-start.4
  15.8 0.4 %strips.1 = (f32[216,128]{1,0:T(8,128)S(1)}, f32[152,128]{1,0:T(8,128)S(1)}, f32[256,128]{1,0:T(8,128)S(1)}) custom-call(f32[2944,128]{1,0:T(8,128)S(1)} %get-tuple-element.31.refs_0_, bf16[32,128]{1,0:T(8,128)(2,1)S(1)} %get-tuple-element.40.refs_1_, bf16[16,128]{1,0:T(8,128)(2,1)S(1)} %get-tuple-element.41.refs_2_, ...), custom_call_target="tpu_custom_call" | custom-call | bytes 1500000 | tf_op jit(solution)/shard_map/strips/pallas_call | solution.py:807
  16.2 1.5 %collective-permute-start.5 = (f32[216,128]{1,0:T(8,128)S(1)}, f32[216,128]{1,0:T(8,128)S(1)}, u32[]{:S(2)}, u32[]{:S(2)}) collective-permute-start(f32[216,128]{1,0:T(8,128)S(1)} %get-tuple-element.53), channel_id=1, source_target_pairs={{0,2},{2,0},{1,3},{3,1},{4,6},{6,4},{5,7},{7,5},{8,10},{10,8},{9,1... | collective-permute-start | bytes 331784 | tf_op jit(solution)/shard_map/ppermute | solution.py:833
  17.7 0.3 %collective-permute-start.6 = (f32[152,128]{1,0:T(8,128)S(1)}, f32[152,128]{1,0:T(8,128)S(1)}, u32[]{:S(2)}, u32[]{:S(2)}) collective-permute-start(f32[152,128]{1,0:T(8,128)S(1)} %get-tuple-element.54), channel_id=1, source_target_pairs={{0,3},{1,2},{2,1},{3,0},{4,7},{5,6},{6,5},{7,4},{8,11},{9,10},{10,... | collective-permute-start | bytes 233480 | tf_op jit(solution)/shard_map/ppermute | solution.py:837
  18.1 0.5 %fill_own.1.refs_0_ = f32[42,128,128]{2,1,0:T(8,128)S(1)} custom-call(f32[2944,128]{1,0:T(8,128)S(1)} %get-tuple-element.31.refs_0_, bf16[512,128]{1,0:T(8,128)(2,1)S(1)} %get-tuple-element.35.refs_1_, bf16[128,128]{1,0:T(8,128)(2,1)S(1)} %get-tuple-element.36.refs_2_, f32[256,128]{1,0:T(8,128)S(1)} %get-tuple-element.37.refs_3_, ...), custom_call_target="tpu_custom_call" | custom-call | bytes 4500000 | tf_op jit(solution)/shard_map/fill_own/pallas_call | solution.py:819
  18.6 0.5 %fill_partner.1.refs_1_ = f32[42,128,128]{2,1,0:T(8,128)S(1)} custom-call(f32[2944,128]{1,0:T(8,128)S(1)} %collective-permute-done.3.refs_0_, bf16[512,128]{1,0:T(8,128)(2,1)S(1)} %get-tuple-element.44.refs_1_, bf16[128,128]{1,0:T(8,128)(2,1)S(1)} %get-tuple-element.45.refs_2_, f32[256,128]{1,0:T(8,128)S(1)} %get-tuple-element.46.refs_3_, ...), custom_call_target="tpu_custom_call" | custom-call | bytes 4500000 | tf_op jit(solution)/shard_map/fill_partner/pallas_call | solution.py:839
  19.1 3.7 %tile_sweeps.1 = (f32[4,128,128]{2,1,0:T(8,128)S(1)}, f32[2,128,128]{2,1,0:T(8,128)S(1)}, f32[80,8,128]{2,1,0:T(8,128)S(1)}) custom-call(f32[42,128,128]{2,1,0:T(8,128)S(1)} %fill_own.1.refs_0_, f32[42,128,128]{2,1,0:T(8,128)S(1)} %fill_partner.1.refs_1_, bf16[128,512]{1,0:T(8,128)(2,1)S(1)} %get-tuple-element.48.refs_2_), custom_call_target="tpu_custom_call" | custom-call | bytes 21000000 | tf_op jit(solution)/shard_map/tile_sweeps/pallas_call | solution.py:852
  22.7 0.2 collective-permute-done.6.refs_8_
  22.9 1.2 %edge_sweeps.1 = (f32[4,8,128]{2,1,0:T(8,128)S(1)}, f32[32,128]{1,0:T(8,128)S(1)}, f32[32,128]{1,0:T(8,128)S(1)}, f32[32,128]{1,0:T(8,128)S(1)}, f32[32,128]{1,0:T(8,128)S(1)}) custom-call(f32[42,128,128]{2,1,0:T(8,128)S(1)} %fill_own.1.refs_0_, f32[42,128,128]{2,1,0:T(8,128)S(1)} %fill_partner.1.refs_1_, bf16[128,128]{1,0:T(8,128)(2,1)S(1)} %get-tuple-element.50.refs_2_, ...), custom_call_target="tpu_custom_call" | custom-call | bytes 4500000 | tf_op jit(solution)/shard_map/edge_sweeps/pallas_call | solution.py:867
  24.2 0.5 %collective-permute-start.7 = (f32[32,128]{1,0:T(8,128)S(1)}, f32[32,128]{1,0:T(8,128)S(1)}, u32[]{:S(2)}, u32[]{:S(2)}) collective-permute-start(f32[32,128]{1,0:T(8,128)S(1)} %get-tuple-element.57), channel_id=1, source_target_pairs={{0,4},{4,8},{8,12},{12,0},{1,5},{5,9},{9,13},{13,1},{2,6},{6,10},{... | collective-permute-start | bytes 49160 | tf_op jit(solution)/shard_map/ppermute | solution.py:881
  24.6 1.3 %collective-permute-start.8 = (f32[32,128]{1,0:T(8,128)S(1)}, f32[32,128]{1,0:T(8,128)S(1)}, u32[]{:S(2)}, u32[]{:S(2)}) collective-permute-start(f32[32,128]{1,0:T(8,128)S(1)} %get-tuple-element.58), channel_id=1, source_target_pairs={{0,8},{4,12},{8,0},{12,4},{1,9},{5,13},{9,1},{13,5},{2,10},{6,14},... | collective-permute-start | bytes 49160 | tf_op jit(solution)/shard_map/ppermute | solution.py:881
  25.9 2.8 %collective-permute-start.9 = (f32[32,128]{1,0:T(8,128)S(1)}, f32[32,128]{1,0:T(8,128)S(1)}, u32[]{:S(2)}, u32[]{:S(2)}) collective-permute-start(f32[32,128]{1,0:T(8,128)S(1)} %get-tuple-element.59), channel_id=1, source_target_pairs={{0,12},{4,0},{8,4},{12,8},{1,13},{5,1},{9,5},{13,9},{2,14},{6,2},{... | collective-permute-start | bytes 49160 | tf_op jit(solution)/shard_map/ppermute | solution.py:881
  28.8 0.7 %merge.1 = f32[4,128,128]{2,1,0:T(8,128)} custom-call(f32[4,128,128]{2,1,0:T(8,128)S(1)} %get-tuple-element.49.whole_ref, f32[4,8,128]{2,1,0:T(8,128)S(1)} %get-tuple-element.55.heat_ref), custom_call_target="tpu_custom_call" | custom-call | bytes 3000000 | tf_op jit(solution)/shard_map/merge/pallas_call | solution.py:882
  29.5 0.3 %collective-permute-done.7 = f32[32,128]{1,0:T(8,128)S(1)} collective-permute-done((f32[32,128]{1,0:T(8,128)S(1)}, f32[32,128]{1,0:T(8,128)S(1)}, u32[]{:S(2)}, u32[]{:S(2)}) %collective-permute-start.7) | collective-permute-done | bytes 16416 | tf_op jit(solution)/shard_map/ppermute | solution.py:881
  29.8 0.5 %collective-permute-done.9 = f32[32,128]{1,0:T(8,128)S(1)} collective-permute-done((f32[32,128]{1,0:T(8,128)S(1)}, f32[32,128]{1,0:T(8,128)S(1)}, u32[]{:S(2)}, u32[]{:S(2)}) %collective-permute-start.9) | collective-permute-done | bytes 16416 | tf_op jit(solution)/shard_map/ppermute | solution.py:881
  30.3 0.6 %add_bitcast_fusion = f32[1,32,128]{2,1,0:T(8,128)} fusion(f32[32,128]{1,0:T(8,128)S(1)} %collective-permute-done.9, f32[32,128]{1,0:T(8,128)S(1)} %collective-permute-done.8, f32[32,128]{1,0:T(8,128)S(1)} %get-tuple-element.56, f32[32,128]{1,0:T(8,128)S(1)} %collective-permute-done.7), kind=kLoop, calls=%fused_computation | loop fusion | flops 12288 | bytes 81920 | tf_op jit(solution)/shard_map/broadcast_in_dim | solution.py:893
  (6 shorter events, 0.0 us)
Async XLA Ops:
  2.6 16.0 %collective-permute-start.3 = (f32[2944,128]{1,0:T(8,128)S(1)}, f32[2944,128]{1,0:T(8,128)S(1)}, u32[]{:S(2)}, u32[]{:S(2)}) collective-permute-start(f32[2944,128]{1,0:T(8,128)S(1)} %get-tuple-element.31.refs_0_), channel_id=1, source_target_pairs={{0,1},{1,0},{2,3},{3,2},{4,5},{5,4},{6,7},{7,6},{8,9},{9,8},{10,11... | collective-permute-start | bytes 4521992 | tf_op jit(solution)/shard_map/ppermute | solution.py:761
  3.1 12.6 %collective-permute-start = (f32[224,128]{1,0:T(8,128)S(1)}, f32[224,128]{1,0:T(8,128)S(1)}, u32[]{:S(2)}, u32[]{:S(2)}) collective-permute-start(f32[224,128]{1,0:T(8,128)S(1)} %get-tuple-element.38), channel_id=1, source_target_pairs={{0,12},{4,0},{8,4},{12,8},{1,13},{5,1},{9,5},{13,9},{2,14},{6,2},{... | collective-permute-start | bytes 344072 | tf_op jit(solution)/shard_map/ppermute | solution.py:763
  7.7 8.0 %collective-permute-start.1 = (f32[224,128]{1,0:T(8,128)S(1)}, f32[224,128]{1,0:T(8,128)S(1)}, u32[]{:S(2)}, u32[]{:S(2)}) collective-permute-start(f32[224,128]{1,0:T(8,128)S(1)} %get-tuple-element.39), channel_id=1, source_target_pairs={{0,4},{4,8},{8,12},{12,0},{1,5},{5,9},{9,13},{13,1},{2,6},{6,10},{... | collective-permute-start | bytes 344072 | tf_op jit(solution)/shard_map/ppermute | solution.py:763
  7.7 8.0 %collective-permute-start.2 = (f32[64,128]{1,0:T(8,128)S(1)}, f32[64,128]{1,0:T(8,128)S(1)}, u32[]{:S(2)}, u32[]{:S(2)}) collective-permute-start(f32[64,128]{1,0:T(8,128)S(1)} %get-tuple-element.42), channel_id=1, source_target_pairs={{0,8},{4,12},{8,0},{12,4},{1,9},{5,13},{9,1},{13,5},{2,10},{6,14},... | collective-permute-start | bytes 98312 | tf_op jit(solution)/shard_map/ppermute | solution.py:763
  15.8 2.8 %collective-permute-start.4 = (f32[512,128]{1,0:T(8,128)S(1)}, f32[512,128]{1,0:T(8,128)S(1)}, u32[]{:S(2)}, u32[]{:S(2)}) collective-permute-start(f32[512,128]{1,0:T(8,128)S(1)} %join.1), channel_id=1, source_target_pairs={{0,1},{1,0},{2,3},{3,2},{4,5},{5,4},{6,7},{7,6},{8,9},{9,8},{10,11... | collective-permute-start | bytes 786440 | tf_op jit(solution)/shard_map/ppermute | solution.py:806
  16.2 6.7 %collective-permute-start.5 = (f32[216,128]{1,0:T(8,128)S(1)}, f32[216,128]{1,0:T(8,128)S(1)}, u32[]{:S(2)}, u32[]{:S(2)}) collective-permute-start(f32[216,128]{1,0:T(8,128)S(1)} %get-tuple-element.53), channel_id=1, source_target_pairs={{0,2},{2,0},{1,3},{3,1},{4,6},{6,4},{5,7},{7,5},{8,10},{10,8},{9,1... | collective-permute-start | bytes 331784 | tf_op jit(solution)/shard_map/ppermute | solution.py:833
  17.7 5.2 %collective-permute-start.6 = (f32[152,128]{1,0:T(8,128)S(1)}, f32[152,128]{1,0:T(8,128)S(1)}, u32[]{:S(2)}, u32[]{:S(2)}) collective-permute-start(f32[152,128]{1,0:T(8,128)S(1)} %get-tuple-element.54), channel_id=1, source_target_pairs={{0,3},{1,2},{2,1},{3,0},{4,7},{5,6},{6,5},{7,4},{8,11},{9,10},{10,... | collective-permute-start | bytes 233480 | tf_op jit(solution)/shard_map/ppermute | solution.py:837
  24.2 5.7 %collective-permute-start.7 = (f32[32,128]{1,0:T(8,128)S(1)}, f32[32,128]{1,0:T(8,128)S(1)}, u32[]{:S(2)}, u32[]{:S(2)}) collective-permute-start(f32[32,128]{1,0:T(8,128)S(1)} %get-tuple-element.57), channel_id=1, source_target_pairs={{0,4},{4,8},{8,12},{12,0},{1,5},{5,9},{9,13},{13,1},{2,6},{6,10},{... | collective-permute-start | bytes 49160 | tf_op jit(solution)/shard_map/ppermute | solution.py:881
  24.6 5.2 %collective-permute-start.8 = (f32[32,128]{1,0:T(8,128)S(1)}, f32[32,128]{1,0:T(8,128)S(1)}, u32[]{:S(2)}, u32[]{:S(2)}) collective-permute-start(f32[32,128]{1,0:T(8,128)S(1)} %get-tuple-element.58), channel_id=1, source_target_pairs={{0,8},{4,12},{8,0},{12,4},{1,9},{5,13},{9,1},{13,5},{2,10},{6,14},... | collective-permute-start | bytes 49160 | tf_op jit(solution)/shard_map/ppermute | solution.py:881
  25.9 4.4 %collective-permute-start.9 = (f32[32,128]{1,0:T(8,128)S(1)}, f32[32,128]{1,0:T(8,128)S(1)}, u32[]{:S(2)}, u32[]{:S(2)}) collective-permute-start(f32[32,128]{1,0:T(8,128)S(1)} %get-tuple-element.59), channel_id=1, source_target_pairs={{0,12},{4,0},{8,4},{12,8},{1,13},{5,1},{9,5},{13,9},{2,14},{6,2},{... | collective-permute-start | bytes 49160 | tf_op jit(solution)/shard_map/ppermute | solution.py:881

commit v5 on v4

--- a/solution.py
+++ b/solution.py
@@ -762,7 +762,8 @@
     def from_distance(value, k):
         return lax.ppermute(value, "gx", [(i, (i - k) % gx) for i in range(gx)])
 
-    received = [from_distance(to_left, 1), from_distance(to_right, gx - 1)]
+    from_left = from_distance(to_right, gx - 1)
+    received = [from_distance(to_left, 1), from_left]
     received += [from_distance(only, k) for k in range(2, gx - 1)]
 
     sides = 1 if gy == 2 else 2

time: 31.1 us -> 31.1 us (level)
  no operation moved by 1% of the time
where the time goes in v5:
time: 31.1 us; the launch traced here: 30.9 us
  starting transfers between devices  12.7 us (41%)
  Pallas kernels  9.41 us (30%)
  waiting for transfers between devices  7.5 us (24%)
  between operations  0.71 us (2%)
  other arithmetic  0.61 us (2%)
    ppermute x3, waiting for transfers between devices, from_distance(): return lax.ppermute(value, 'gx', [(i, (i - k) % gx) for i in range(gx)])  6.47 us
    ppermute x3, starting transfers between devices, from_distance(): return lax.ppermute(value, 'gx', [(i, (i - k) % gx) for i in range(gx)])  5.67 us
    ppermute x3, starting transfers between devices, local(): lax.ppermute(results[1 + k], 'gx', [(i, (i + k) % gx) for i in range(gx)])  4.6 us
    pallas_call x1, Pallas kernels, local(): pl.pallas_call(functools.partial(tile_kernel, gx, gy, shape), out_shape=(...  3.67 us
    pallas_call x1, Pallas kernels, local(): pl.pallas_call(functools.partial(pack_kernel, shape), out_shape=(struct(R...  1.92 us
    ppermute x1, starting transfers between devices, local(): along = [lax.ppermute(strips[side], 'gy', pairs) for side, pairs in routes]  1.49 us
    pallas_call x1, Pallas kernels, local(): pl.pallas_call(functools.partial(edge_kernel, gx, gy, shape, seg), out_sh...  1.23 us
    ppermute x3, waiting for transfers between devices, local(): lax.ppermute(results[1 + k], 'gx', [(i, (i + k) % gx) for i in range(gx)])  0.83 us
  transfers between devices with their start and end apart: 10, of which 4 were waited for; matrix products, arithmetic and copies ran while one was open for 0% of the time, Pallas kernels for 20%

profile of v5, /device:TPU:0, one launch (start us, length us, event | category | flops | bytes accessed | tf_op | source)
XLA Modules:
  0.0 30.9 jit_solution(4496373329137265917)
XLA Ops:
  0.6 1.9 %pack.1 = (f32[2944,128]{1,0:T(8,128)S(1)}, f32[224,128]{1,0:T(8,128)S(1)}, f32[224,128]{1,0:T(8,128)S(1)}, f32[64,128]{1,0:T(8,128)S(1)}, s32[4,128]{1,0:T(4,12...) custom-call(f32[512,128]{1,0:T(8,128)} %bitcast.10, f32[512,128]{1,0:T(8,128)} %bitcast.11, f32[512,128]{1,0:T(8,128)} %bitcast.12, ...), custom_call_target="tpu_custom_call" | custom-call | tf_op jit(solution)/shard_map/pack/pallas_call | solution.py:744
  2.6 0.5 %collective-permute-start.3 = (f32[2944,128]{1,0:T(8,128)S(1)}, f32[2944,128]{1,0:T(8,128)S(1)}, u32[]{:S(2)}, u32[]{:S(2)}) collective-permute-start(f32[2944,128]{1,0:T(8,128)S(1)} %get-tuple-element.31.refs_0_), channel_id=1, source_target_pairs={{0,1},{1,0},{2,3},{3,2},{4,5},{5,4},{6,7},{7,6},{8,9},{9,8},{10,11... | collective-permute-start | bytes 4521992 | tf_op jit(solution)/shard_map/ppermute | solution.py:761
  3.1 4.7 %collective-permute-start = (f32[224,128]{1,0:T(8,128)S(1)}, f32[224,128]{1,0:T(8,128)S(1)}, u32[]{:S(2)}, u32[]{:S(2)}) collective-permute-start(f32[224,128]{1,0:T(8,128)S(1)} %get-tuple-element.38), channel_id=1, source_target_pairs={{0,12},{4,0},{8,4},{12,8},{1,13},{5,1},{9,5},{13,9},{2,14},{6,2},{... | collective-permute-start | bytes 344072 | tf_op jit(solution)/shard_map/ppermute | solution.py:763
  7.7 0.0 collective-permute-start.1
  7.7 1.0 %collective-permute-start.2 = (f32[64,128]{1,0:T(8,128)S(1)}, f32[64,128]{1,0:T(8,128)S(1)}, u32[]{:S(2)}, u32[]{:S(2)}) collective-permute-start(f32[64,128]{1,0:T(8,128)S(1)} %get-tuple-element.42), channel_id=1, source_target_pairs={{0,8},{4,12},{8,0},{12,4},{1,9},{5,13},{9,1},{13,5},{2,10},{6,14},... | collective-permute-start | bytes 98312 | tf_op jit(solution)/shard_map/ppermute | solution.py:763
  8.8 0.5 %maps.1 = (bf16[512,128]{1,0:T(8,128)(2,1)S(1)}, bf16[128,128]{1,0:T(8,128)(2,1)S(1)}, f32[256,128]{1,0:T(8,128)S(1)}, bf16[512,128]{1,0:T(8,128)(2,1)S(1)}, bf1...) custom-call(s32[4,128]{1,0:T(4,128)S(1)} %get-tuple-element.32.holde, ...), custom_call_target="tpu_custom_call" | custom-call | bytes 3000000 | tf_op jit(solution)/shard_map/maps/pallas_call | solution.py:781
  9.3 6.5 %collective-permute-done.2.refs_6_.refs_2_ = f32[64,128]{1,0:T(8,128)S(1)} collective-permute-done((f32[64,128]{1,0:T(8,128)S(1)}, f32[64,128]{1,0:T(8,128)S(1)}, u32[]{:S(2)}, u32[]{:S(2)}) %collective-permute-start.2) | collective-permute-done | bytes 32800 | tf_op jit(solution)/shard_map/ppermute | solution.py:763
  15.7 0.0 collective-permute-done.refs_4_.refs_0_
  15.8 0.1 collective-permute-start.4
  15.8 0.4 %strips.1 = (f32[216,128]{1,0:T(8,128)S(1)}, f32[152,128]{1,0:T(8,128)S(1)}, f32[256,128]{1,0:T(8,128)S(1)}) custom-call(f32[2944,128]{1,0:T(8,128)S(1)} %get-tuple-element.31.refs_0_, bf16[32,128]{1,0:T(8,128)(2,1)S(1)} %get-tuple-element.40.refs_1_, bf16[16,128]{1,0:T(8,128)(2,1)S(1)} %get-tuple-element.41.refs_2_, ...), custom_call_target="tpu_custom_call" | custom-call | bytes 1500000 | tf_op jit(solution)/shard_map/strips/pallas_call | solution.py:808
  16.2 1.5 %collective-permute-start.5 = (f32[216,128]{1,0:T(8,128)S(1)}, f32[216,128]{1,0:T(8,128)S(1)}, u32[]{:S(2)}, u32[]{:S(2)}) collective-permute-start(f32[216,128]{1,0:T(8,128)S(1)} %get-tuple-element.53), channel_id=1, source_target_pairs={{0,2},{2,0},{1,3},{3,1},{4,6},{6,4},{5,7},{7,5},{8,10},{10,8},{9,1... | collective-permute-start | bytes 331784 | tf_op jit(solution)/shard_map/ppermute | solution.py:834
  17.7 0.3 %collective-permute-start.6 = (f32[152,128]{1,0:T(8,128)S(1)}, f32[152,128]{1,0:T(8,128)S(1)}, u32[]{:S(2)}, u32[]{:S(2)}) collective-permute-start(f32[152,128]{1,0:T(8,128)S(1)} %get-tuple-element.54), channel_id=1, source_target_pairs={{0,3},{1,2},{2,1},{3,0},{4,7},{5,6},{6,5},{7,4},{8,11},{9,10},{10,... | collective-permute-start | bytes 233480 | tf_op jit(solution)/shard_map/ppermute | solution.py:838
  18.1 0.5 %fill_own.1.refs_0_ = f32[42,128,128]{2,1,0:T(8,128)S(1)} custom-call(f32[2944,128]{1,0:T(8,128)S(1)} %get-tuple-element.31.refs_0_, bf16[512,128]{1,0:T(8,128)(2,1)S(1)} %get-tuple-element.35.refs_1_, bf16[128,128]{1,0:T(8,128)(2,1)S(1)} %get-tuple-element.36.refs_2_, f32[256,128]{1,0:T(8,128)S(1)} %get-tuple-element.37.refs_3_, ...), custom_call_target="tpu_custom_call" | custom-call | bytes 4500000 | tf_op jit(solution)/shard_map/fill_own/pallas_call | solution.py:820
  18.6 0.5 %fill_partner.1.refs_1_ = f32[42,128,128]{2,1,0:T(8,128)S(1)} custom-call(f32[2944,128]{1,0:T(8,128)S(1)} %collective-permute-done.3.refs_0_, bf16[512,128]{1,0:T(8,128)(2,1)S(1)} %get-tuple-element.44.refs_1_, bf16[128,128]{1,0:T(8,128)(2,1)S(1)} %get-tuple-element.45.refs_2_, f32[256,128]{1,0:T(8,128)S(1)} %get-tuple-element.46.refs_3_, ...), custom_call_target="tpu_custom_call" | custom-call | bytes 4500000 | tf_op jit(solution)/shard_map/fill_partner/pallas_call | solution.py:840
  19.1 3.7 %tile_sweeps.1 = (f32[4,128,128]{2,1,0:T(8,128)S(1)}, f32[2,128,128]{2,1,0:T(8,128)S(1)}, f32[80,8,128]{2,1,0:T(8,128)S(1)}) custom-call(f32[42,128,128]{2,1,0:T(8,128)S(1)} %fill_own.1.refs_0_, f32[42,128,128]{2,1,0:T(8,128)S(1)} %fill_partner.1.refs_1_, bf16[128,512]{1,0:T(8,128)(2,1)S(1)} %get-tuple-element.48.refs_2_), custom_call_target="tpu_custom_call" | custom-call | bytes 21000000 | tf_op jit(solution)/shard_map/tile_sweeps/pallas_call | solution.py:853
  22.7 0.2 collective-permute-done.6.refs_8_
  22.9 1.2 %edge_sweeps.1 = (f32[4,8,128]{2,1,0:T(8,128)S(1)}, f32[32,128]{1,0:T(8,128)S(1)}, f32[32,128]{1,0:T(8,128)S(1)}, f32[32,128]{1,0:T(8,128)S(1)}, f32[32,128]{1,0:T(8,128)S(1)}) custom-call(f32[42,128,128]{2,1,0:T(8,128)S(1)} %fill_own.1.refs_0_, f32[42,128,128]{2,1,0:T(8,128)S(1)} %fill_partner.1.refs_1_, bf16[128,128]{1,0:T(8,128)(2,1)S(1)} %get-tuple-element.50.refs_2_, ...), custom_call_target="tpu_custom_call" | custom-call | bytes 4500000 | tf_op jit(solution)/shard_map/edge_sweeps/pallas_call | solution.py:868
  24.2 0.5 %collective-permute-start.7 = (f32[32,128]{1,0:T(8,128)S(1)}, f32[32,128]{1,0:T(8,128)S(1)}, u32[]{:S(2)}, u32[]{:S(2)}) collective-permute-start(f32[32,128]{1,0:T(8,128)S(1)} %get-tuple-element.57), channel_id=1, source_target_pairs={{0,4},{4,8},{8,12},{12,0},{1,5},{5,9},{9,13},{13,1},{2,6},{6,10},{... | collective-permute-start | bytes 49160 | tf_op jit(solution)/shard_map/ppermute | solution.py:882
  24.6 1.3 %collective-permute-start.8 = (f32[32,128]{1,0:T(8,128)S(1)}, f32[32,128]{1,0:T(8,128)S(1)}, u32[]{:S(2)}, u32[]{:S(2)}) collective-permute-start(f32[32,128]{1,0:T(8,128)S(1)} %get-tuple-element.58), channel_id=1, source_target_pairs={{0,8},{4,12},{8,0},{12,4},{1,9},{5,13},{9,1},{13,5},{2,10},{6,14},... | collective-permute-start | bytes 49160 | tf_op jit(solution)/shard_map/ppermute | solution.py:882
  25.9 2.8 %collective-permute-start.9 = (f32[32,128]{1,0:T(8,128)S(1)}, f32[32,128]{1,0:T(8,128)S(1)}, u32[]{:S(2)}, u32[]{:S(2)}) collective-permute-start(f32[32,128]{1,0:T(8,128)S(1)} %get-tuple-element.59), channel_id=1, source_target_pairs={{0,12},{4,0},{8,4},{12,8},{1,13},{5,1},{9,5},{13,9},{2,14},{6,2},{... | collective-permute-start | bytes 49160 | tf_op jit(solution)/shard_map/ppermute | solution.py:882
  28.8 0.7 %merge.1 = f32[4,128,128]{2,1,0:T(8,128)} custom-call(f32[4,128,128]{2,1,0:T(8,128)S(1)} %get-tuple-element.49.whole_ref, f32[4,8,128]{2,1,0:T(8,128)S(1)} %get-tuple-element.55.heat_ref), custom_call_target="tpu_custom_call" | custom-call | bytes 3000000 | tf_op jit(solution)/shard_map/merge/pallas_call | solution.py:883
  29.5 0.3 %collective-permute-done.7 = f32[32,128]{1,0:T(8,128)S(1)} collective-permute-done((f32[32,128]{1,0:T(8,128)S(1)}, f32[32,128]{1,0:T(8,128)S(1)}, u32[]{:S(2)}, u32[]{:S(2)}) %collective-permute-start.7) | collective-permute-done | bytes 16416 | tf_op jit(solution)/shard_map/ppermute | solution.py:882
  29.8 0.5 %collective-permute-done.9 = f32[32,128]{1,0:T(8,128)S(1)} collective-permute-done((f32[32,128]{1,0:T(8,128)S(1)}, f32[32,128]{1,0:T(8,128)S(1)}, u32[]{:S(2)}, u32[]{:S(2)}) %collective-permute-start.9) | collective-permute-done | bytes 16416 | tf_op jit(solution)/shard_map/ppermute | solution.py:882
  30.3 0.6 %add_bitcast_fusion = f32[1,32,128]{2,1,0:T(8,128)} fusion(f32[32,128]{1,0:T(8,128)S(1)} %collective-permute-done.9, f32[32,128]{1,0:T(8,128)S(1)} %collective-permute-done.8, f32[32,128]{1,0:T(8,128)S(1)} %get-tuple-element.56, f32[32,128]{1,0:T(8,128)S(1)} %collective-permute-done.7), kind=kLoop, calls=%fused_computation | loop fusion | flops 12288 | bytes 81920 | tf_op jit(solution)/shard_map/broadcast_in_dim | solution.py:894
  (6 shorter events, 0.0 us)
Async XLA Ops:
  2.6 16.0 %collective-permute-start.3 = (f32[2944,128]{1,0:T(8,128)S(1)}, f32[2944,128]{1,0:T(8,128)S(1)}, u32[]{:S(2)}, u32[]{:S(2)}) collective-permute-start(f32[2944,128]{1,0:T(8,128)S(1)} %get-tuple-element.31.refs_0_), channel_id=1, source_target_pairs={{0,1},{1,0},{2,3},{3,2},{4,5},{5,4},{6,7},{7,6},{8,9},{9,8},{10,11... | collective-permute-start | bytes 4521992 | tf_op jit(solution)/shard_map/ppermute | solution.py:761
  3.1 12.6 %collective-permute-start = (f32[224,128]{1,0:T(8,128)S(1)}, f32[224,128]{1,0:T(8,128)S(1)}, u32[]{:S(2)}, u32[]{:S(2)}) collective-permute-start(f32[224,128]{1,0:T(8,128)S(1)} %get-tuple-element.38), channel_id=1, source_target_pairs={{0,12},{4,0},{8,4},{12,8},{1,13},{5,1},{9,5},{13,9},{2,14},{6,2},{... | collective-permute-start | bytes 344072 | tf_op jit(solution)/shard_map/ppermute | solution.py:763
  7.7 8.0 %collective-permute-start.1 = (f32[224,128]{1,0:T(8,128)S(1)}, f32[224,128]{1,0:T(8,128)S(1)}, u32[]{:S(2)}, u32[]{:S(2)}) collective-permute-start(f32[224,128]{1,0:T(8,128)S(1)} %get-tuple-element.39), channel_id=1, source_target_pairs={{0,4},{4,8},{8,12},{12,0},{1,5},{5,9},{9,13},{13,1},{2,6},{6,10},{... | collective-permute-start | bytes 344072 | tf_op jit(solution)/shard_map/ppermute | solution.py:763
  7.7 8.0 %collective-permute-start.2 = (f32[64,128]{1,0:T(8,128)S(1)}, f32[64,128]{1,0:T(8,128)S(1)}, u32[]{:S(2)}, u32[]{:S(2)}) collective-permute-start(f32[64,128]{1,0:T(8,128)S(1)} %get-tuple-element.42), channel_id=1, source_target_pairs={{0,8},{4,12},{8,0},{12,4},{1,9},{5,13},{9,1},{13,5},{2,10},{6,14},... | collective-permute-start | bytes 98312 | tf_op jit(solution)/shard_map/ppermute | solution.py:763
  15.8 2.8 %collective-permute-start.4 = (f32[512,128]{1,0:T(8,128)S(1)}, f32[512,128]{1,0:T(8,128)S(1)}, u32[]{:S(2)}, u32[]{:S(2)}) collective-permute-start(f32[512,128]{1,0:T(8,128)S(1)} %join.1), channel_id=1, source_target_pairs={{0,1},{1,0},{2,3},{3,2},{4,5},{5,4},{6,7},{7,6},{8,9},{9,8},{10,11... | collective-permute-start | bytes 786440 | tf_op jit(solution)/shard_map/ppermute | solution.py:807
  16.2 6.7 %collective-permute-start.5 = (f32[216,128]{1,0:T(8,128)S(1)}, f32[216,128]{1,0:T(8,128)S(1)}, u32[]{:S(2)}, u32[]{:S(2)}) collective-permute-start(f32[216,128]{1,0:T(8,128)S(1)} %get-tuple-element.53), channel_id=1, source_target_pairs={{0,2},{2,0},{1,3},{3,1},{4,6},{6,4},{5,7},{7,5},{8,10},{10,8},{9,1... | collective-permute-start | bytes 331784 | tf_op jit(solution)/shard_map/ppermute | solution.py:834
  17.7 5.2 %collective-permute-start.6 = (f32[152,128]{1,0:T(8,128)S(1)}, f32[152,128]{1,0:T(8,128)S(1)}, u32[]{:S(2)}, u32[]{:S(2)}) collective-permute-start(f32[152,128]{1,0:T(8,128)S(1)} %get-tuple-element.54), channel_id=1, source_target_pairs={{0,3},{1,2},{2,1},{3,0},{4,7},{5,6},{6,5},{7,4},{8,11},{9,10},{10,... | collective-permute-start | bytes 233480 | tf_op jit(solution)/shard_map/ppermute | solution.py:838
  24.2 5.7 %collective-permute-start.7 = (f32[32,128]{1,0:T(8,128)S(1)}, f32[32,128]{1,0:T(8,128)S(1)}, u32[]{:S(2)}, u32[]{:S(2)}) collective-permute-start(f32[32,128]{1,0:T(8,128)S(1)} %get-tuple-element.57), channel_id=1, source_target_pairs={{0,4},{4,8},{8,12},{12,0},{1,5},{5,9},{9,13},{13,1},{2,6},{6,10},{... | collective-permute-start | bytes 49160 | tf_op jit(solution)/shard_map/ppermute | solution.py:882
  24.6 5.2 %collective-permute-start.8 = (f32[32,128]{1,0:T(8,128)S(1)}, f32[32,128]{1,0:T(8,128)S(1)}, u32[]{:S(2)}, u32[]{:S(2)}) collective-permute-start(f32[32,128]{1,0:T(8,128)S(1)} %get-tuple-element.58), channel_id=1, source_target_pairs={{0,8},{4,12},{8,0},{12,4},{1,9},{5,13},{9,1},{13,5},{2,10},{6,14},... | collective-permute-start | bytes 49160 | tf_op jit(solution)/shard_map/ppermute | solution.py:882
  25.9 4.4 %collective-permute-start.9 = (f32[32,128]{1,0:T(8,128)S(1)}, f32[32,128]{1,0:T(8,128)S(1)}, u32[]{:S(2)}, u32[]{:S(2)}) collective-permute-start(f32[32,128]{1,0:T(8,128)S(1)} %get-tuple-element.59), channel_id=1, source_target_pairs={{0,12},{4,0},{8,4},{12,8},{1,13},{5,1},{9,5},{13,9},{2,14},{6,2},{... | collective-permute-start | bytes 49160 | tf_op jit(solution)/shard_map/ppermute | solution.py:882

commit v6 on v4

--- a/solution.py
+++ b/solution.py
@@ -683,7 +683,8 @@
             src_ref, dst_ref = bufs[which], bufs[1 - which]
             for i in range(total):
                 src_ref[i, tile(inner), :] = level_ref[(side * STEPS * ITERS + number) * total + i]
-            sweep(src_ref, dst_ref, HALO, n, needed_layers, coefs, 0)
+            for at in range(0, n, HALO):
+                sweep(src_ref, dst_ref, HALO + at, HALO, needed_layers, coefs, at)
 
         picks = picks_ref[side * count : (side + 1) * count, :]
 

time: 31.1 us -> 31.1 us (level)
  no operation moved by 1% of the time
where the time goes in v6:
time: 31.1 us; the launch traced here: 30.9 us
  starting transfers between devices  12.7 us (41%)
  Pallas kernels  9.4 us (30%)
  waiting for transfers between devices  7.5 us (24%)
  between operations  0.71 us (2%)
  other arithmetic  0.61 us (2%)
    ppermute x3, waiting for transfers between devices, from_distance(): return lax.ppermute(value, 'gx', [(i, (i - k) % gx) for i in range(gx)])  6.47 us
    ppermute x3, starting transfers between devices, from_distance(): return lax.ppermute(value, 'gx', [(i, (i - k) % gx) for i in range(gx)])  5.67 us
    ppermute x3, starting transfers between devices, local(): lax.ppermute(results[1 + k], 'gx', [(i, (i + k) % gx) for i in range(gx)])  4.6 us
    pallas_call x1, Pallas kernels, local(): pl.pallas_call(functools.partial(tile_kernel, gx, gy, shape), out_shape=(...  3.67 us
    pallas_call x1, Pallas kernels, local(): pl.pallas_call(functools.partial(pack_kernel, shape), out_shape=(struct(R...  1.92 us
    ppermute x1, starting transfers between devices, local(): along = [lax.ppermute(strips[side], 'gy', pairs) for side, pairs in routes]  1.49 us
    pallas_call x1, Pallas kernels, local(): pl.pallas_call(functools.partial(edge_kernel, gx, gy, shape, seg), out_sh...  1.23 us
    ppermute x3, waiting for transfers between devices, local(): lax.ppermute(results[1 + k], 'gx', [(i, (i + k) % gx) for i in range(gx)])  0.83 us
  transfers between devices with their start and end apart: 10, of which 4 were waited for; matrix products, arithmetic and copies ran while one was open for 0% of the time, Pallas kernels for 20%

profile of v6, /device:TPU:0, one launch (start us, length us, event | category | flops | bytes accessed | tf_op | source)
XLA Modules:
  0.0 30.9 jit_solution(2417633850489909385)
XLA Ops:
  0.6 1.9 %pack.1 = (f32[2944,128]{1,0:T(8,128)S(1)}, f32[224,128]{1,0:T(8,128)S(1)}, f32[224,128]{1,0:T(8,128)S(1)}, f32[64,128]{1,0:T(8,128)S(1)}, s32[4,128]{1,0:T(4,12...) custom-call(f32[512,128]{1,0:T(8,128)} %bitcast.10, f32[512,128]{1,0:T(8,128)} %bitcast.11, f32[512,128]{1,0:T(8,128)} %bitcast.12, ...), custom_call_target="tpu_custom_call" | custom-call | tf_op jit(solution)/shard_map/pack/pallas_call | solution.py:745
  2.6 0.5 %collective-permute-start.3 = (f32[2944,128]{1,0:T(8,128)S(1)}, f32[2944,128]{1,0:T(8,128)S(1)}, u32[]{:S(2)}, u32[]{:S(2)}) collective-permute-start(f32[2944,128]{1,0:T(8,128)S(1)} %get-tuple-element.31.refs_0_), channel_id=1, source_target_pairs={{0,1},{1,0},{2,3},{3,2},{4,5},{5,4},{6,7},{7,6},{8,9},{9,8},{10,11... | collective-permute-start | bytes 4521992 | tf_op jit(solution)/shard_map/ppermute | solution.py:762
  3.1 4.7 %collective-permute-start = (f32[224,128]{1,0:T(8,128)S(1)}, f32[224,128]{1,0:T(8,128)S(1)}, u32[]{:S(2)}, u32[]{:S(2)}) collective-permute-start(f32[224,128]{1,0:T(8,128)S(1)} %get-tuple-element.38), channel_id=1, source_target_pairs={{0,12},{4,0},{8,4},{12,8},{1,13},{5,1},{9,5},{13,9},{2,14},{6,2},{... | collective-permute-start | bytes 344072 | tf_op jit(solution)/shard_map/ppermute | solution.py:764
  7.7 0.0 collective-permute-start.1
  7.7 1.0 %collective-permute-start.2 = (f32[64,128]{1,0:T(8,128)S(1)}, f32[64,128]{1,0:T(8,128)S(1)}, u32[]{:S(2)}, u32[]{:S(2)}) collective-permute-start(f32[64,128]{1,0:T(8,128)S(1)} %get-tuple-element.42), channel_id=1, source_target_pairs={{0,8},{4,12},{8,0},{12,4},{1,9},{5,13},{9,1},{13,5},{2,10},{6,14},... | collective-permute-start | bytes 98312 | tf_op jit(solution)/shard_map/ppermute | solution.py:764
  8.8 0.5 %maps.1 = (bf16[512,128]{1,0:T(8,128)(2,1)S(1)}, bf16[128,128]{1,0:T(8,128)(2,1)S(1)}, f32[256,128]{1,0:T(8,128)S(1)}, bf16[512,128]{1,0:T(8,128)(2,1)S(1)}, bf1...) custom-call(s32[4,128]{1,0:T(4,128)S(1)} %get-tuple-element.32.holde, ...), custom_call_target="tpu_custom_call" | custom-call | bytes 3000000 | tf_op jit(solution)/shard_map/maps/pallas_call | solution.py:781
  9.3 6.5 %collective-permute-done.2.refs_6_.refs_2_ = f32[64,128]{1,0:T(8,128)S(1)} collective-permute-done((f32[64,128]{1,0:T(8,128)S(1)}, f32[64,128]{1,0:T(8,128)S(1)}, u32[]{:S(2)}, u32[]{:S(2)}) %collective-permute-start.2) | collective-permute-done | bytes 32800 | tf_op jit(solution)/shard_map/ppermute | solution.py:764
  15.7 0.0 collective-permute-done.refs_4_.refs_0_
  15.8 0.1 collective-permute-start.4
  15.8 0.4 %strips.1 = (f32[216,128]{1,0:T(8,128)S(1)}, f32[152,128]{1,0:T(8,128)S(1)}, f32[256,128]{1,0:T(8,128)S(1)}) custom-call(f32[2944,128]{1,0:T(8,128)S(1)} %get-tuple-element.31.refs_0_, bf16[32,128]{1,0:T(8,128)(2,1)S(1)} %get-tuple-element.40.refs_1_, bf16[16,128]{1,0:T(8,128)(2,1)S(1)} %get-tuple-element.41.refs_2_, ...), custom_call_target="tpu_custom_call" | custom-call | bytes 1500000 | tf_op jit(solution)/shard_map/strips/pallas_call | solution.py:808
  16.2 1.5 %collective-permute-start.5 = (f32[216,128]{1,0:T(8,128)S(1)}, f32[216,128]{1,0:T(8,128)S(1)}, u32[]{:S(2)}, u32[]{:S(2)}) collective-permute-start(f32[216,128]{1,0:T(8,128)S(1)} %get-tuple-element.53), channel_id=1, source_target_pairs={{0,2},{2,0},{1,3},{3,1},{4,6},{6,4},{5,7},{7,5},{8,10},{10,8},{9,1... | collective-permute-start | bytes 331784 | tf_op jit(solution)/shard_map/ppermute | solution.py:834
  17.7 0.3 %collective-permute-start.6 = (f32[152,128]{1,0:T(8,128)S(1)}, f32[152,128]{1,0:T(8,128)S(1)}, u32[]{:S(2)}, u32[]{:S(2)}) collective-permute-start(f32[152,128]{1,0:T(8,128)S(1)} %get-tuple-element.54), channel_id=1, source_target_pairs={{0,3},{1,2},{2,1},{3,0},{4,7},{5,6},{6,5},{7,4},{8,11},{9,10},{10,... | collective-permute-start | bytes 233480 | tf_op jit(solution)/shard_map/ppermute | solution.py:838
  18.1 0.5 %fill_own.1.refs_0_ = f32[42,128,128]{2,1,0:T(8,128)S(1)} custom-call(f32[2944,128]{1,0:T(8,128)S(1)} %get-tuple-element.31.refs_0_, bf16[512,128]{1,0:T(8,128)(2,1)S(1)} %get-tuple-element.35.refs_1_, bf16[128,128]{1,0:T(8,128)(2,1)S(1)} %get-tuple-element.36.refs_2_, f32[256,128]{1,0:T(8,128)S(1)} %get-tuple-element.37.refs_3_, ...), custom_call_target="tpu_custom_call" | custom-call | bytes 4500000 | tf_op jit(solution)/shard_map/fill_own/pallas_call | solution.py:820
  18.6 0.5 %fill_partner.1.refs_1_ = f32[42,128,128]{2,1,0:T(8,128)S(1)} custom-call(f32[2944,128]{1,0:T(8,128)S(1)} %collective-permute-done.3.refs_0_, bf16[512,128]{1,0:T(8,128)(2,1)S(1)} %get-tuple-element.44.refs_1_, bf16[128,128]{1,0:T(8,128)(2,1)S(1)} %get-tuple-element.45.refs_2_, f32[256,128]{1,0:T(8,128)S(1)} %get-tuple-element.46.refs_3_, ...), custom_call_target="tpu_custom_call" | custom-call | bytes 4500000 | tf_op jit(solution)/shard_map/fill_partner/pallas_call | solution.py:840
  19.1 3.7 %tile_sweeps.1 = (f32[4,128,128]{2,1,0:T(8,128)S(1)}, f32[2,128,128]{2,1,0:T(8,128)S(1)}, f32[80,8,128]{2,1,0:T(8,128)S(1)}) custom-call(f32[42,128,128]{2,1,0:T(8,128)S(1)} %fill_own.1.refs_0_, f32[42,128,128]{2,1,0:T(8,128)S(1)} %fill_partner.1.refs_1_, bf16[128,512]{1,0:T(8,128)(2,1)S(1)} %get-tuple-element.48.refs_2_), custom_call_target="tpu_custom_call" | custom-call | bytes 21000000 | tf_op jit(solution)/shard_map/tile_sweeps/pallas_call | solution.py:853
  22.7 0.2 collective-permute-done.6.refs_8_
  22.9 1.2 %edge_sweeps.1 = (f32[4,8,128]{2,1,0:T(8,128)S(1)}, f32[32,128]{1,0:T(8,128)S(1)}, f32[32,128]{1,0:T(8,128)S(1)}, f32[32,128]{1,0:T(8,128)S(1)}, f32[32,128]{1,0:T(8,128)S(1)}) custom-call(f32[42,128,128]{2,1,0:T(8,128)S(1)} %fill_own.1.refs_0_, f32[42,128,128]{2,1,0:T(8,128)S(1)} %fill_partner.1.refs_1_, bf16[128,128]{1,0:T(8,128)(2,1)S(1)} %get-tuple-element.50.refs_2_, ...), custom_call_target="tpu_custom_call" | custom-call | bytes 4500000 | tf_op jit(solution)/shard_map/edge_sweeps/pallas_call | solution.py:868
  24.2 0.5 %collective-permute-start.7 = (f32[32,128]{1,0:T(8,128)S(1)}, f32[32,128]{1,0:T(8,128)S(1)}, u32[]{:S(2)}, u32[]{:S(2)}) collective-permute-start(f32[32,128]{1,0:T(8,128)S(1)} %get-tuple-element.57), channel_id=1, source_target_pairs={{0,4},{4,8},{8,12},{12,0},{1,5},{5,9},{9,13},{13,1},{2,6},{6,10},{... | collective-permute-start | bytes 49160 | tf_op jit(solution)/shard_map/ppermute | solution.py:882
  24.6 1.3 %collective-permute-start.8 = (f32[32,128]{1,0:T(8,128)S(1)}, f32[32,128]{1,0:T(8,128)S(1)}, u32[]{:S(2)}, u32[]{:S(2)}) collective-permute-start(f32[32,128]{1,0:T(8,128)S(1)} %get-tuple-element.58), channel_id=1, source_target_pairs={{0,8},{4,12},{8,0},{12,4},{1,9},{5,13},{9,1},{13,5},{2,10},{6,14},... | collective-permute-start | bytes 49160 | tf_op jit(solution)/shard_map/ppermute | solution.py:882
  25.9 2.8 %collective-permute-start.9 = (f32[32,128]{1,0:T(8,128)S(1)}, f32[32,128]{1,0:T(8,128)S(1)}, u32[]{:S(2)}, u32[]{:S(2)}) collective-permute-start(f32[32,128]{1,0:T(8,128)S(1)} %get-tuple-element.59), channel_id=1, source_target_pairs={{0,12},{4,0},{8,4},{12,8},{1,13},{5,1},{9,5},{13,9},{2,14},{6,2},{... | collective-permute-start | bytes 49160 | tf_op jit(solution)/shard_map/ppermute | solution.py:882
  28.8 0.7 %merge.1 = f32[4,128,128]{2,1,0:T(8,128)} custom-call(f32[4,128,128]{2,1,0:T(8,128)S(1)} %get-tuple-element.49.whole_ref, f32[4,8,128]{2,1,0:T(8,128)S(1)} %get-tuple-element.55.heat_ref), custom_call_target="tpu_custom_call" | custom-call | bytes 3000000 | tf_op jit(solution)/shard_map/merge/pallas_call | solution.py:883
  29.5 0.3 %collective-permute-done.7 = f32[32,128]{1,0:T(8,128)S(1)} collective-permute-done((f32[32,128]{1,0:T(8,128)S(1)}, f32[32,128]{1,0:T(8,128)S(1)}, u32[]{:S(2)}, u32[]{:S(2)}) %collective-permute-start.7) | collective-permute-done | bytes 16416 | tf_op jit(solution)/shard_map/ppermute | solution.py:882
  29.8 0.5 %collective-permute-done.9 = f32[32,128]{1,0:T(8,128)S(1)} collective-permute-done((f32[32,128]{1,0:T(8,128)S(1)}, f32[32,128]{1,0:T(8,128)S(1)}, u32[]{:S(2)}, u32[]{:S(2)}) %collective-permute-start.9) | collective-permute-done | bytes 16416 | tf_op jit(solution)/shard_map/ppermute | solution.py:882
  30.3 0.6 %add_bitcast_fusion = f32[1,32,128]{2,1,0:T(8,128)} fusion(f32[32,128]{1,0:T(8,128)S(1)} %collective-permute-done.9, f32[32,128]{1,0:T(8,128)S(1)} %collective-permute-done.8, f32[32,128]{1,0:T(8,128)S(1)} %get-tuple-element.56, f32[32,128]{1,0:T(8,128)S(1)} %collective-permute-done.7), kind=kLoop, calls=%fused_computation | loop fusion | flops 12288 | bytes 81920 | tf_op jit(solution)/shard_map/broadcast_in_dim | solution.py:894
  (6 shorter events, 0.0 us)
Async XLA Ops:
  2.6 16.0 %collective-permute-start.3 = (f32[2944,128]{1,0:T(8,128)S(1)}, f32[2944,128]{1,0:T(8,128)S(1)}, u32[]{:S(2)}, u32[]{:S(2)}) collective-permute-start(f32[2944,128]{1,0:T(8,128)S(1)} %get-tuple-element.31.refs_0_), channel_id=1, source_target_pairs={{0,1},{1,0},{2,3},{3,2},{4,5},{5,4},{6,7},{7,6},{8,9},{9,8},{10,11... | collective-permute-start | bytes 4521992 | tf_op jit(solution)/shard_map/ppermute | solution.py:762
  3.1 12.6 %collective-permute-start = (f32[224,128]{1,0:T(8,128)S(1)}, f32[224,128]{1,0:T(8,128)S(1)}, u32[]{:S(2)}, u32[]{:S(2)}) collective-permute-start(f32[224,128]{1,0:T(8,128)S(1)} %get-tuple-element.38), channel_id=1, source_target_pairs={{0,12},{4,0},{8,4},{12,8},{1,13},{5,1},{9,5},{13,9},{2,14},{6,2},{... | collective-permute-start | bytes 344072 | tf_op jit(solution)/shard_map/ppermute | solution.py:764
  7.7 8.0 %collective-permute-start.1 = (f32[224,128]{1,0:T(8,128)S(1)}, f32[224,128]{1,0:T(8,128)S(1)}, u32[]{:S(2)}, u32[]{:S(2)}) collective-permute-start(f32[224,128]{1,0:T(8,128)S(1)} %get-tuple-element.39), channel_id=1, source_target_pairs={{0,4},{4,8},{8,12},{12,0},{1,5},{5,9},{9,13},{13,1},{2,6},{6,10},{... | collective-permute-start | bytes 344072 | tf_op jit(solution)/shard_map/ppermute | solution.py:764
  7.7 8.0 %collective-permute-start.2 = (f32[64,128]{1,0:T(8,128)S(1)}, f32[64,128]{1,0:T(8,128)S(1)}, u32[]{:S(2)}, u32[]{:S(2)}) collective-permute-start(f32[64,128]{1,0:T(8,128)S(1)} %get-tuple-element.42), channel_id=1, source_target_pairs={{0,8},{4,12},{8,0},{12,4},{1,9},{5,13},{9,1},{13,5},{2,10},{6,14},... | collective-permute-start | bytes 98312 | tf_op jit(solution)/shard_map/ppermute | solution.py:764
  15.8 2.8 %collective-permute-start.4 = (f32[512,128]{1,0:T(8,128)S(1)}, f32[512,128]{1,0:T(8,128)S(1)}, u32[]{:S(2)}, u32[]{:S(2)}) collective-permute-start(f32[512,128]{1,0:T(8,128)S(1)} %join.1), channel_id=1, source_target_pairs={{0,1},{1,0},{2,3},{3,2},{4,5},{5,4},{6,7},{7,6},{8,9},{9,8},{10,11... | collective-permute-start | bytes 786440 | tf_op jit(solution)/shard_map/ppermute | solution.py:807
  16.2 6.7 %collective-permute-start.5 = (f32[216,128]{1,0:T(8,128)S(1)}, f32[216,128]{1,0:T(8,128)S(1)}, u32[]{:S(2)}, u32[]{:S(2)}) collective-permute-start(f32[216,128]{1,0:T(8,128)S(1)} %get-tuple-element.53), channel_id=1, source_target_pairs={{0,2},{2,0},{1,3},{3,1},{4,6},{6,4},{5,7},{7,5},{8,10},{10,8},{9,1... | collective-permute-start | bytes 331784 | tf_op jit(solution)/shard_map/ppermute | solution.py:834
  17.7 5.2 %collective-permute-start.6 = (f32[152,128]{1,0:T(8,128)S(1)}, f32[152,128]{1,0:T(8,128)S(1)}, u32[]{:S(2)}, u32[]{:S(2)}) collective-permute-start(f32[152,128]{1,0:T(8,128)S(1)} %get-tuple-element.54), channel_id=1, source_target_pairs={{0,3},{1,2},{2,1},{3,0},{4,7},{5,6},{6,5},{7,4},{8,11},{9,10},{10,... | collective-permute-start | bytes 233480 | tf_op jit(solution)/shard_map/ppermute | solution.py:838
  24.2 5.7 %collective-permute-start.7 = (f32[32,128]{1,0:T(8,128)S(1)}, f32[32,128]{1,0:T(8,128)S(1)}, u32[]{:S(2)}, u32[]{:S(2)}) collective-permute-start(f32[32,128]{1,0:T(8,128)S(1)} %get-tuple-element.57), channel_id=1, source_target_pairs={{0,4},{4,8},{8,12},{12,0},{1,5},{5,9},{9,13},{13,1},{2,6},{6,10},{... | collective-permute-start | bytes 49160 | tf_op jit(solution)/shard_map/ppermute | solution.py:882
  24.6 5.2 %collective-permute-start.8 = (f32[32,128]{1,0:T(8,128)S(1)}, f32[32,128]{1,0:T(8,128)S(1)}, u32[]{:S(2)}, u32[]{:S(2)}) collective-permute-start(f32[32,128]{1,0:T(8,128)S(1)} %get-tuple-element.58), channel_id=1, source_target_pairs={{0,8},{4,12},{8,0},{12,4},{1,9},{5,13},{9,1},{13,5},{2,10},{6,14},... | collective-permute-start | bytes 49160 | tf_op jit(solution)/shard_map/ppermute | solution.py:882
  25.9 4.4 %collective-permute-start.9 = (f32[32,128]{1,0:T(8,128)S(1)}, f32[32,128]{1,0:T(8,128)S(1)}, u32[]{:S(2)}, u32[]{:S(2)}) collective-permute-start(f32[32,128]{1,0:T(8,128)S(1)} %get-tuple-element.59), channel_id=1, source_target_pairs={{0,12},{4,0},{8,4},{12,8},{1,13},{5,1},{9,5},{13,9},{2,14},{6,2},{... | collective-permute-start | bytes 49160 | tf_op jit(solution)/shard_map/ppermute | solution.py:882
